TPU v7x, 256 devices: a whole 4x4x8 slice. The times are simulated.
256 devices in a mesh: seg: 16 (over z, core), tok: 16 (over x, y).
Axes of the slice: x: 4, y: 4, z: 8, core: 2. Of those that a mesh axis runs over, the one named last changes fastest.
Arguments:
- queries: bfloat16 [2, 16, 2, 20480, 256], P(None, 'seg', None, 'tok'), may hold values from -6 to 6
- key_vectors: bfloat16 [2, 16, 2, 20480, 256], P(None, 'seg', None, 'tok'), may hold values from -6 to 6
- values: bfloat16 [2, 16, 2, 20480, 256], P(None, 'seg', None, 'tok'), may hold values from -6 to 6
- token_rates: float32 [2, 16, 2, 20480], P(None, 'seg', None, 'tok'), may hold values from 0.05 to 3
- fast_weights: float32 [16, 3, 256, 256], P('seg', None, None, 'tok'), may hold values from -0.375 to 0.375
- momenta: float32 [16, 3, 256, 256], P('seg', None, None, 'tok'), may hold values from -3 to 3
- fresh_weights: float32 [3, 256, 256], P(None, None, 'tok'), may hold values from -0.375 to 0.375
- fresh_momenta: float32 [3, 256, 256], P(None, None, 'tok'), may hold values from -3 to 3
Outputs:
- outputs: bfloat16 [2, 16, 2, 20480, 256], P(None, 'seg', None, 'tok')
- final_weights: float32 [16, 3, 256, 256], P('seg', None, None, 'tok')
- final_momenta: float32 [16, 3, 256, 256], P('seg', None, None, 'tok')
All inputs are finite; a program needn't handle non-finite values.
Results may differ from a plain program's by a relative error of at most 0.033.
Values may be sent and summed in bfloat16 or wider, within the bound.
No kernel may reach another device: no remote copies, remote signals or barrier semaphores. Data moves between devices by JAX's collectives and lax.ppermute only.
A program may use at most 64 MiB of HBM per device.

v0:
```python
import jax
import jax.numpy as jnp
from jax import lax
from jax.sharding import Mesh
from jax.sharding import PartitionSpec as P

TOK = ("tok_0", "tok_1")


momentum_decay = 0.9
learn_rate = 0.05
epsilon = 1e-06


def from_everyone(array, axis):
    length = lax.axis_size(axis)
    return lax.all_to_all(
        jnp.broadcast_to(array[None], (length, *array.shape)), axis, 0, 0, tiled=True
    )


def laid_out(tiles, dim):
    dims = list(tiles.shape[1:])
    dims[dim] *= tiles.shape[0]
    return jnp.moveaxis(tiles, 0, dim).reshape(dims)


def gather_directly(array, axis, dim):
    tiles = from_everyone(array, axis)
    return laid_out(tiles, dim)


def split_up(array, dim, length):
    dims = array.shape
    tiles = array.reshape(*dims[:dim], length, dims[dim] // length, *dims[dim + 1 :])
    return jnp.moveaxis(tiles, dim, 0)


def sent_and_summed(array, axis, dim):
    tiles = split_up(array, dim, lax.axis_size(axis))
    arrived = lax.all_to_all(tiles, axis, split_axis=0, concat_axis=0, tiled=True)
    return arrived.astype(jnp.float32).sum(axis=0)


def over_copies(array, axis):
    everything = from_everyone(array, axis)
    return jnp.sum(everything, axis=0)


def shifted(array, axis, by):
    length = lax.axis_size(axis)
    pairs = [(i, i + by) for i in range(length) if 0 <= i + by < length]
    return lax.ppermute(array, axis, pairs)


def silu_parts(pre_gate):
    sigmoid_gate = jax.nn.sigmoid(pre_gate)
    return (pre_gate * sigmoid_gate, sigmoid_gate * (1.0 + pre_gate * (1.0 - sigmoid_gate)))


def local_grads(usable_weights, key_rows, value_rows, rate_rows):
    pre_gate = jnp.dot(key_rows, usable_weights[0], preferred_element_type=jnp.float32)
    pre_up = jnp.dot(key_rows, usable_weights[2], preferred_element_type=jnp.float32)
    active, slope_gate = silu_parts(pre_gate)
    hidden = (active * pre_up).astype(jnp.bfloat16)
    scaled = (rate_rows[:, None] * value_rows.astype(jnp.float32)).astype(jnp.bfloat16)
    back_hidden = -lax.dot_general(
        scaled, usable_weights[1], (((1,), (1,)), ((), ())), preferred_element_type=jnp.float32
    )
    back_gate = (back_hidden * pre_up * slope_gate).astype(jnp.bfloat16)
    back_up = (back_hidden * active).astype(jnp.bfloat16)
    contract_rows = (((0,), (0,)), ((), ()))
    grad_gate = lax.dot_general(
        key_rows, back_gate, contract_rows, preferred_element_type=jnp.float32
    )
    grad_down = -lax.dot_general(hidden, scaled, contract_rows, preferred_element_type=jnp.float32)
    grad_up = lax.dot_general(key_rows, back_up, contract_rows, preferred_element_type=jnp.float32)
    return (jnp.stack([grad_gate, grad_down, grad_up]), jnp.sum(rate_rows * rate_rows))


def update(weights, moment, gradients, rate_total):
    moment = momentum_decay * moment + gradients * lax.rsqrt(rate_total)
    stepped = weights - learn_rate * moment
    rescale = jnp.sqrt(
        jnp.sum(weights * weights, axis=1, keepdims=True)
        / (jnp.sum(stepped * stepped, axis=1, keepdims=True) + epsilon)
    )
    return (stepped * rescale, moment)


def apply_fast(usable_weights, query_rows):
    pre_gate = jnp.dot(query_rows, usable_weights[0], preferred_element_type=jnp.float32)
    pre_up = jnp.dot(query_rows, usable_weights[2], preferred_element_type=jnp.float32)
    hidden = (jax.nn.silu(pre_gate) * pre_up).astype(jnp.bfloat16)
    return jnp.dot(hidden, usable_weights[1], preferred_element_type=jnp.float32).astype(
        jnp.bfloat16
    )


def usable(weights):
    rounded = weights.astype(jnp.bfloat16)
    return gather_directly(rounded, TOK, 2)


def advance(
    weights, moment, usable_weights, query_rows, key_rows, value_rows, rate_rows, rate_total
):
    gradients, square = local_grads(usable_weights, key_rows, value_rows, rate_rows)
    gradients = sent_and_summed(gradients.astype(jnp.bfloat16), TOK, 2)
    weights, moment = update(weights, moment, gradients, rate_total)
    usable_weights = usable(weights)
    return (weights, moment, usable_weights, apply_fast(usable_weights, query_rows))


def body(
    queries, key_vectors, values, token_rates, fast_weights, momenta, fresh_weights, fresh_momenta
):
    sections = queries.shape[0]
    blocks = queries.shape[2]
    totals = over_copies(jnp.sum(token_rates[:, 0] * token_rates[:, 0], axis=-1), TOK)
    weights, moment, fresh_start, fresh_moment = (
        fast_weights[0],
        momenta[0],
        fresh_weights,
        fresh_momenta,
    )
    is_first = lax.axis_index("seg") == 0
    results = []
    for wave_step in range(sections):
        if wave_step > 0:
            passed = (
                shifted(weights.astype(jnp.bfloat16), "seg", 1).astype(weights.dtype),
                shifted(moment.astype(jnp.bfloat16), "seg", 1).astype(moment.dtype),
            )
            weights = jnp.where(is_first, fresh_start, passed[0])
            moment = jnp.where(is_first, fresh_moment, passed[1])
        usable_weights = usable(weights)
        for block_index in range(blocks):
            rate_total = totals[wave_step, block_index]
            weights, moment, usable_weights, result = advance(
                weights,
                moment,
                usable_weights,
                queries[wave_step, 0, block_index],
                key_vectors[wave_step, 0, block_index],
                values[wave_step, 0, block_index],
                token_rates[wave_step, 0, block_index],
                rate_total,
            )
            results.append(result)
    row_count = queries.shape[3]
    head_width = queries.shape[4]
    outputs = jnp.stack(results).reshape(sections, blocks, row_count, head_width)[:, None]
    return (outputs, weights[None], moment[None])


def solution(mesh):
    finer = Mesh(mesh.devices.reshape(mesh.shape["seg"], 4, 4), ("seg", "tok_0", "tok_1"))
    placed = (
        P(None, "seg", None, TOK, None),
        P(None, "seg", None, TOK, None),
        P(None, "seg", None, TOK, None),
        P(None, "seg", None, TOK),
        P("seg", None, None, TOK),
        P("seg", None, None, TOK),
        P(None, None, TOK),
        P(None, None, TOK),
    )
    return jax.shard_map(
        body,
        mesh=finer,
        in_specs=placed,
        out_specs=(
            P(None, "seg", None, TOK, None),
            P("seg", None, None, TOK),
            P("seg", None, None, TOK),
        ),
        check_vma=False,
    )
```

profile of v0, /device:TPU:96, one launch (start us, length us, event | category | flops | bytes accessed | tf_op | source)
XLA Modules:
  0.0 187.2 jit_solution(806003610483074748)
XLA Ops:
  2.2 7.2 %all-to-all-start = ((bf16[16,3,256,16]{2,3,1,0:T(8,128)(2,1)}), bf16[16,3,256,16]{2,3,1,0:T(8,128)(2,1)S(1)}, u32[]{:S(2)}, u32[]{:S(2)}) async-start(bf16[16,3,256,16]{2,3,1,0:T(8,128)(2,1)} %broadcast_in_dim.25), calls=%async_computation | async-start | bytes 786432 | tf_op jit(solution)/shard_map/all_to_all | solution.py:17
  10.9 8.4 %all-to-all-done = bf16[16,3,256,16]{2,3,1,0:T(8,128)(2,1)S(1)} async-done(((bf16[16,3,256,16]{2,3,1,0:T(8,128)(2,1)}), bf16[16,3,256,16]{2,3,1,0:T(8,128)(2,1)S(1)}, u32[]{:S(2)}, u32[]{:S(2)}) %all-to-all-start) | async-done | bytes 393248 | tf_op jit(solution)/shard_map/all_to_all | solution.py:17
  19.8 3.7 %all-to-all-start.2 = ((f32[16,2,2]{2,1,0:T(2,128)}), f32[16,2,2]{2,1,0:T(2,128)S(1)}, u32[]{:S(2)}, u32[]{:S(2)}) async-start(f32[16,2,2]{2,1,0:T(2,128)} %broadcast_in_dim.26), calls=%async_computation.2 | async-start | bytes 32768 | tf_op jit(solution)/shard_map/all_to_all | solution.py:17
  31.1 4.8 %all-to-all-start.1 = ((bf16[16,3,256,16]{2,3,1,0:T(8,128)(2,1)}), bf16[16,3,256,16]{2,3,1,0:T(8,128)(2,1)S(1)}, u32[]{:S(2)}, u32[]{:S(2)}) async-start(bf16[16,3,256,16]{2,3,1,0:T(8,128)(2,1)} %maximum_bitcast_fusion), calls=%async_computation.1 | async-start | bytes 786432 | tf_op jit(solution)/shard_map/all_to_all | solution.py:41
  37.4 7.8 %all-to-all-done.1 = bf16[16,3,256,16]{2,3,1,0:T(8,128)(2,1)S(1)} async-done(((bf16[16,3,256,16]{2,3,1,0:T(8,128)(2,1)}), bf16[16,3,256,16]{2,3,1,0:T(8,128)(2,1)S(1)}, u32[]{:S(2)}, u32[]{:S(2)}) %all-to-all-start.1) | async-done | bytes 393248 | tf_op jit(solution)/shard_map/all_to_all | solution.py:41
  45.4 12.6 %all_to_all.55 = bf16[16,3,256,16]{2,3,1,0:T(8,128)(2,1)S(1)} all-to-all(bf16[16,3,256,16]{2,3,1,0:T(8,128)(2,1)S(1)} %broadcast_in_dim.28), channel_id=1, replica_groups=mesh['seg'=16,'tok_0'=4,'tok_1'=4] {'tok_0','tok_1'}, dimensions={0} | all-to-all | bytes 786432 | tf_op jit(solution)/shard_map/all_to_all | solution.py:17
  63.4 3.7 %all-to-all-start.4 = ((bf16[16,3,256,16]{2,3,1,0:T(8,128)(2,1)}), bf16[16,3,256,16]{2,3,1,0:T(8,128)(2,1)S(1)}, u32[]{:S(2)}, u32[]{:S(2)}) async-start(bf16[16,3,256,16]{2,3,1,0:T(8,128)(2,1)} %maximum_bitcast_fusion.1), calls=%async_computation.4 | async-start | bytes 786432 | tf_op jit(solution)/shard_map/all_to_all | solution.py:41
  67.8 8.4 %all-to-all-done.4 = bf16[16,3,256,16]{2,3,1,0:T(8,128)(2,1)S(1)} async-done(((bf16[16,3,256,16]{2,3,1,0:T(8,128)(2,1)}), bf16[16,3,256,16]{2,3,1,0:T(8,128)(2,1)S(1)}, u32[]{:S(2)}, u32[]{:S(2)}) %all-to-all-start.4) | async-done | bytes 393248 | tf_op jit(solution)/shard_map/all_to_all | solution.py:41
  79.1 3.2 %collective-permute-done = bf16[3,256,16]{1,2,0:T(8,128)(2,1)S(1)} collective-permute-done((bf16[3,256,16]{1,2,0:T(8,128)(2,1)S(1)}, bf16[3,256,16]{1,2,0:T(8,128)(2,1)S(1)}, u32[]{:S(2)}, u32[]{:S(2)}) %collective-permute-start) | collective-permute-done | bytes 24608 | tf_op jit(solution)/shard_map/ppermute | solution.py:53
  83.1 3.7 %all-to-all-start.6 = ((bf16[16,3,256,16]{2,3,1,0:T(8,128)(2,1)}), bf16[16,3,256,16]{2,3,1,0:T(8,128)(2,1)S(1)}, u32[]{:S(2)}, u32[]{:S(2)}) async-start(bf16[16,3,256,16]{2,3,1,0:T(8,128)(2,1)} %broadcast_in_dim.31), calls=%async_computation.6 | async-start | bytes 786432 | tf_op jit(solution)/shard_map/all_to_all | solution.py:17
  88.0 10.0 %all-to-all-done.6 = bf16[16,3,256,16]{2,3,1,0:T(8,128)(2,1)S(1)} async-done(((bf16[16,3,256,16]{2,3,1,0:T(8,128)(2,1)}), bf16[16,3,256,16]{2,3,1,0:T(8,128)(2,1)S(1)}, u32[]{:S(2)}, u32[]{:S(2)}) %all-to-all-start.6) | async-done | bytes 393248 | tf_op jit(solution)/shard_map/all_to_all | solution.py:17
  103.3 3.7 %all-to-all-start.7 = ((bf16[16,3,256,16]{2,3,1,0:T(8,128)(2,1)}), bf16[16,3,256,16]{2,3,1,0:T(8,128)(2,1)S(1)}, u32[]{:S(2)}, u32[]{:S(2)}) async-start(bf16[16,3,256,16]{2,3,1,0:T(8,128)(2,1)} %maximum_bitcast_fusion.2), calls=%async_computation.7 | async-start | bytes 786432 | tf_op jit(solution)/shard_map/all_to_all | solution.py:41
  111.5 5.3 %all-to-all-done.7 = bf16[16,3,256,16]{2,3,1,0:T(8,128)(2,1)S(1)} async-done(((bf16[16,3,256,16]{2,3,1,0:T(8,128)(2,1)}), bf16[16,3,256,16]{2,3,1,0:T(8,128)(2,1)S(1)}, u32[]{:S(2)}, u32[]{:S(2)}) %all-to-all-start.7) | async-done | bytes 393248 | tf_op jit(solution)/shard_map/all_to_all | solution.py:41
  117.6 3.9 %all-to-all-start.5 = ((bf16[16,3,256,16]{2,3,1,0:T(8,128)(2,1)}), bf16[16,3,256,16]{2,3,1,0:T(8,128)(2,1)S(1)}, u32[]{:S(2)}, u32[]{:S(2)}) async-start(bf16[16,3,256,16]{2,3,1,0:T(8,128)(2,1)} %broadcast_in_dim.30), calls=%async_computation.5 | async-start | bytes 786432 | tf_op jit(solution)/shard_map/all_to_all | solution.py:17
  123.0 9.0 %all-to-all-done.5 = bf16[16,3,256,16]{2,3,1,0:T(8,128)(2,1)S(1)} async-done(((bf16[16,3,256,16]{2,3,1,0:T(8,128)(2,1)}), bf16[16,3,256,16]{2,3,1,0:T(8,128)(2,1)S(1)}, u32[]{:S(2)}, u32[]{:S(2)}) %all-to-all-start.5) | async-done | bytes 393248 | tf_op jit(solution)/shard_map/all_to_all | solution.py:17
  132.8 3.8 %all-to-all-start.8 = ((bf16[16,3,256,16]{2,3,1,0:T(8,128)(2,1)}), bf16[16,3,256,16]{2,3,1,0:T(8,128)(2,1)S(1)}, u32[]{:S(2)}, u32[]{:S(2)}) async-start(bf16[16,3,256,16]{2,3,1,0:T(8,128)(2,1)} %broadcast_in_dim.32), calls=%async_computation.8 | async-start | bytes 786432 | tf_op jit(solution)/shard_map/all_to_all | solution.py:17
  136.6 3.0 %fusion.8 = bf16[1,1280,256]{2,1,0:T(8,128)(2,1)} fusion(bf16[256,256]{0,1:T(8,128)(2,1)} %bitcast.344, bf16[256,256]{0,1:T(8,128)(2,1)S(1)} %bitcast.342, f32[1280,256]{1,0:T(8,128)} %convolution_bitcast_fusion.13, bf16[2,1,2,1280,256]{4,3,2,1,0:T(8,128)(2,1)} %param.8), kind=kOutput, calls=%fused_computation.31 | convolution fusion | flops 337838080 | bytes 2883584 | tf_op jit(solution)/shard_map/dot_general | solution.py:95
  140.4 5.7 %all-to-all-done.8 = bf16[16,3,256,16]{2,3,1,0:T(8,128)(2,1)S(1)} async-done(((bf16[16,3,256,16]{2,3,1,0:T(8,128)(2,1)}), bf16[16,3,256,16]{2,3,1,0:T(8,128)(2,1)S(1)}, u32[]{:S(2)}, u32[]{:S(2)}) %all-to-all-start.8) | async-done | bytes 393248 | tf_op jit(solution)/shard_map/all_to_all | solution.py:17
  151.3 4.0 %all-to-all-start.9 = ((bf16[16,3,256,16]{2,3,1,0:T(8,128)(2,1)}), bf16[16,3,256,16]{2,3,1,0:T(8,128)(2,1)S(1)}, u32[]{:S(2)}, u32[]{:S(2)}) async-start(bf16[16,3,256,16]{2,3,1,0:T(8,128)(2,1)} %maximum_bitcast_fusion.3), calls=%async_computation.9 | async-start | bytes 786432 | tf_op jit(solution)/shard_map/all_to_all | solution.py:41
  160.6 3.8 %all-to-all-done.9 = bf16[16,3,256,16]{2,3,1,0:T(8,128)(2,1)S(1)} async-done(((bf16[16,3,256,16]{2,3,1,0:T(8,128)(2,1)}), bf16[16,3,256,16]{2,3,1,0:T(8,128)(2,1)S(1)}, u32[]{:S(2)}, u32[]{:S(2)}) %all-to-all-start.9) | async-done | bytes 393248 | tf_op jit(solution)/shard_map/all_to_all | solution.py:41
  166.7 3.7 %all-to-all-start.10 = ((bf16[16,3,256,16]{2,3,1,0:T(8,128)(2,1)}), bf16[16,3,256,16]{2,3,1,0:T(8,128)(2,1)S(1)}, u32[]{:S(2)}, u32[]{:S(2)}) async-start(bf16[16,3,256,16]{2,3,1,0:T(8,128)(2,1)} %broadcast_in_dim.33), calls=%async_computation.10 | async-start | bytes 786432 | tf_op jit(solution)/shard_map/all_to_all | solution.py:17
  174.7 4.9 %all-to-all-done.10 = bf16[16,3,256,16]{2,3,1,0:T(8,128)(2,1)S(1)} async-done(((bf16[16,3,256,16]{2,3,1,0:T(8,128)(2,1)}), bf16[16,3,256,16]{2,3,1,0:T(8,128)(2,1)S(1)}, u32[]{:S(2)}, u32[]{:S(2)}) %all-to-all-start.10) | async-done | bytes 393248 | tf_op jit(solution)/shard_map/all_to_all | solution.py:17
  181.0 2.9 %fusion.11 = bf16[1,1280,256]{2,1,0:T(8,128)(2,1)} fusion(bf16[256,256]{0,1:T(8,128)(2,1)S(1)} %bitcast.371, bf16[256,256]{0,1:T(8,128)(2,1)S(1)} %bitcast.372, f32[1280,256]{1,0:T(8,128)} %convolution_bitcast_fusion.1, bf16[2,1,2,1280,256]{4,3,2,1,0:T(8,128)(2,1)S(1)} %copy-done.5), kind=kOutput, calls=%fused_computation.34 | convolution fusion | flops 337838080 | bytes 2883584 | tf_op jit(solution)/shard_map/dot_general | solution.py:95
  183.9 3.3 %pad_maximum_fusion = bf16[4,1280,256]{2,1,0:T(8,128)(2,1)} fusion(bf16[1,1280,256]{2,1,0:T(8,128)(2,1)} %fusion.11, bf16[1,1280,256]{2,1,0:T(8,128)(2,1)} %fusion.10, bf16[1,1280,256]{2,1,0:T(8,128)(2,1)} %fusion.9, bf16[1,1280,256]{2,1,0:T(8,128)(2,1)S(1)} %copy-done.9), kind=kLoop, calls=%fused_computation.22 | loop fusion | flops 3932160 | bytes 5242880 | tf_op jit(solution)/shard_map/stack | solution.py:153
  (132 shorter events, 52.9 us)
Async XLA Ops:
  0.6 9.6 %copy-start.20 = (f32[2,1,2,1280]{3,2,1,0:T(2,128)S(1)}, f32[2,1,2,1280]{3,2,1,0:T(2,128)}, u32[]{:S(2)}) copy-start(f32[2,1,2,1280]{3,2,1,0:T(2,128)} %param.11) | copy-start | bytes 61444
  1.5 22.2 %copy-start = (bf16[2,1,2,1280,256]{4,3,2,1,0:T(8,128)(2,1)S(1)}, bf16[2,1,2,1280,256]{4,3,2,1,0:T(8,128)(2,1)}, u32[]{:S(2)}) copy-start(bf16[2,1,2,1280,256]{4,3,2,1,0:T(8,128)(2,1)} %param.9) | copy-start | bytes 7864324
  2.2 17.0 %all-to-all-start = ((bf16[16,3,256,16]{2,3,1,0:T(8,128)(2,1)}), bf16[16,3,256,16]{2,3,1,0:T(8,128)(2,1)S(1)}, u32[]{:S(2)}, u32[]{:S(2)}) async-start(bf16[16,3,256,16]{2,3,1,0:T(8,128)(2,1)} %broadcast_in_dim.25), calls=%async_computation | async-start | bytes 786432 | tf_op jit(solution)/shard_map/all_to_all | solution.py:17
  19.8 11.3 %all-to-all-start.2 = ((f32[16,2,2]{2,1,0:T(2,128)}), f32[16,2,2]{2,1,0:T(2,128)S(1)}, u32[]{:S(2)}, u32[]{:S(2)}) async-start(f32[16,2,2]{2,1,0:T(2,128)} %broadcast_in_dim.26), calls=%async_computation.2 | async-start | bytes 32768 | tf_op jit(solution)/shard_map/all_to_all | solution.py:17
  27.9 17.2 %copy-start.6 = (f32[1,3,256,16]{2,3,1,0:T(8,128)S(1)}, f32[1,3,256,16]{2,3,1,0:T(8,128)}, u32[]{:S(2)}) copy-start(f32[1,3,256,16]{2,3,1,0:T(8,128)} %param.12) | copy-start | bytes 147460
  28.0 17.2 %copy-start.13 = (f32[1,3,256,16]{2,3,1,0:T(8,128)S(1)}, f32[1,3,256,16]{2,3,1,0:T(8,128)}, u32[]{:S(2)}) copy-start(f32[1,3,256,16]{2,3,1,0:T(8,128)} %param.13) | copy-start | bytes 147460
  31.1 14.0 %all-to-all-start.1 = ((bf16[16,3,256,16]{2,3,1,0:T(8,128)(2,1)}), bf16[16,3,256,16]{2,3,1,0:T(8,128)(2,1)S(1)}, u32[]{:S(2)}, u32[]{:S(2)}) async-start(bf16[16,3,256,16]{2,3,1,0:T(8,128)(2,1)} %maximum_bitcast_fusion), calls=%async_computation.1 | async-start | bytes 786432 | tf_op jit(solution)/shard_map/all_to_all | solution.py:41
  45.3 31.0 %copy-start.21 = (f32[3,16]{1,0:T(4,128)}, f32[3,16]{1,0:T(4,128)S(1)}, u32[]{:S(2)}) copy-start(f32[3,16]{1,0:T(4,128)S(1)} %fusion.141) | copy-start | bytes 580
  62.6 19.7 %copy-start.17 = (f32[3,256,16]{1,2,0:T(8,128)S(1)}, f32[3,256,16]{1,2,0:T(8,128)}, u32[]{:S(2)}) copy-start(f32[3,256,16]{1,2,0:T(8,128)} %param.14) | copy-start | bytes 147460
  63.4 12.9 %all-to-all-start.4 = ((bf16[16,3,256,16]{2,3,1,0:T(8,128)(2,1)}), bf16[16,3,256,16]{2,3,1,0:T(8,128)(2,1)S(1)}, u32[]{:S(2)}, u32[]{:S(2)}) async-start(bf16[16,3,256,16]{2,3,1,0:T(8,128)(2,1)} %maximum_bitcast_fusion.1), calls=%async_computation.4 | async-start | bytes 786432 | tf_op jit(solution)/shard_map/all_to_all | solution.py:41
  77.1 21.1 %copy-start.24 = (f32[3,16]{1,0:T(4,128)}, f32[3,16]{1,0:T(4,128)S(1)}, u32[]{:S(2)}) copy-start(f32[3,16]{1,0:T(4,128)S(1)} %fusion.142) | copy-start | bytes 580
  77.1 5.1 %collective-permute-start = (bf16[3,256,16]{1,2,0:T(8,128)(2,1)S(1)}, bf16[3,256,16]{1,2,0:T(8,128)(2,1)S(1)}, u32[]{:S(2)}, u32[]{:S(2)}) collective-permute-start(bf16[3,256,16]{1,2,0:T(8,128)(2,1)S(1)} %multiply_convert_fusion.24), channel_id=1, source_target_pairs={{0,16},{16,32},{32,48},{48,64},{64,80},{80,96},{96,112},{112,128},... | collective-permute-start | bytes 73736 | tf_op jit(solution)/shard_map/ppermute | solution.py:53
  82.3 15.8 %copy-start.19 = (bf16[3,256,16]{1,2,0:T(8,128)(2,1)}, bf16[3,256,16]{1,2,0:T(8,128)(2,1)S(1)}, u32[]{:S(2)}) copy-start(bf16[3,256,16]{1,2,0:T(8,128)(2,1)S(1)} %collective-permute-done) | copy-start | bytes 73732
  83.1 15.0 %all-to-all-start.6 = ((bf16[16,3,256,16]{2,3,1,0:T(8,128)(2,1)}), bf16[16,3,256,16]{2,3,1,0:T(8,128)(2,1)S(1)}, u32[]{:S(2)}, u32[]{:S(2)}) async-start(bf16[16,3,256,16]{2,3,1,0:T(8,128)(2,1)} %broadcast_in_dim.31), calls=%async_computation.6 | async-start | bytes 786432 | tf_op jit(solution)/shard_map/all_to_all | solution.py:17
  103.3 8.1 %copy-start.22 = (f32[3,16]{1,0:T(4,128)S(1)}, f32[3,16]{1,0:T(4,128)}, u32[]{:S(2)}) copy-start(f32[3,16]{1,0:T(4,128)} %copy-done.21) | copy-start | bytes 580
  103.3 8.1 %copy-start.25 = (f32[3,16]{1,0:T(4,128)S(1)}, f32[3,16]{1,0:T(4,128)}, u32[]{:S(2)}) copy-start(f32[3,16]{1,0:T(4,128)} %copy-done.24) | copy-start | bytes 580
  103.3 13.5 %all-to-all-start.7 = ((bf16[16,3,256,16]{2,3,1,0:T(8,128)(2,1)}), bf16[16,3,256,16]{2,3,1,0:T(8,128)(2,1)S(1)}, u32[]{:S(2)}, u32[]{:S(2)}) async-start(bf16[16,3,256,16]{2,3,1,0:T(8,128)(2,1)} %maximum_bitcast_fusion.2), calls=%async_computation.7 | async-start | bytes 786432 | tf_op jit(solution)/shard_map/all_to_all | solution.py:41
  109.5 12.1 %collective-permute-start.1 = (bf16[3,256,16]{1,2,0:T(8,128)(2,1)}, bf16[3,256,16]{1,2,0:T(8,128)(2,1)}, u32[]{:S(2)}, u32[]{:S(2)}) collective-permute-start(bf16[3,256,16]{1,2,0:T(8,128)(2,1)} %get-tuple-element.51), channel_id=1, source_target_pairs={{0,16},{16,32},{32,48},{48,64},{64,80},{80,96},{96,112},{112,128},... | collective-permute-start | bytes 73736 | tf_op jit(solution)/shard_map/ppermute | solution.py:53
  117.6 19.0 %copy-start.11 = (bf16[1,256,16,16]{1,3,2,0:T(8,128)(2,1)S(1)}, bf16[1,256,16,16]{1,3,2,0:T(8,128)(2,1)}, u32[]{:S(2)}) copy-start(bf16[1,256,16,16]{1,3,2,0:T(8,128)(2,1)} %copy-done.10) | copy-start | bytes 393220
  117.6 14.5 %all-to-all-start.5 = ((bf16[16,3,256,16]{2,3,1,0:T(8,128)(2,1)}), bf16[16,3,256,16]{2,3,1,0:T(8,128)(2,1)S(1)}, u32[]{:S(2)}, u32[]{:S(2)}) async-start(bf16[16,3,256,16]{2,3,1,0:T(8,128)(2,1)} %broadcast_in_dim.30), calls=%async_computation.5 | async-start | bytes 786432 | tf_op jit(solution)/shard_map/all_to_all | solution.py:17
  122.9 9.9 %copy-start.15 = (f32[3,256,16]{1,2,0:T(8,128)}, f32[3,256,16]{1,2,0:T(8,128)S(1)}, u32[]{:S(2)}) copy-start(f32[3,256,16]{1,2,0:T(8,128)S(1)} %get-tuple-element.27) | copy-start | bytes 147460
  132.8 13.3 %all-to-all-start.8 = ((bf16[16,3,256,16]{2,3,1,0:T(8,128)(2,1)}), bf16[16,3,256,16]{2,3,1,0:T(8,128)(2,1)S(1)}, u32[]{:S(2)}, u32[]{:S(2)}) async-start(bf16[16,3,256,16]{2,3,1,0:T(8,128)(2,1)} %broadcast_in_dim.32), calls=%async_computation.8 | async-start | bytes 786432 | tf_op jit(solution)/shard_map/all_to_all | solution.py:17
  151.3 13.1 %all-to-all-start.9 = ((bf16[16,3,256,16]{2,3,1,0:T(8,128)(2,1)}), bf16[16,3,256,16]{2,3,1,0:T(8,128)(2,1)S(1)}, u32[]{:S(2)}, u32[]{:S(2)}) async-start(bf16[16,3,256,16]{2,3,1,0:T(8,128)(2,1)} %maximum_bitcast_fusion.3), calls=%async_computation.9 | async-start | bytes 786432 | tf_op jit(solution)/shard_map/all_to_all | solution.py:41
  166.7 12.9 %all-to-all-start.10 = ((bf16[16,3,256,16]{2,3,1,0:T(8,128)(2,1)}), bf16[16,3,256,16]{2,3,1,0:T(8,128)(2,1)S(1)}, u32[]{:S(2)}, u32[]{:S(2)}) async-start(bf16[16,3,256,16]{2,3,1,0:T(8,128)(2,1)} %broadcast_in_dim.33), calls=%async_computation.10 | async-start | bytes 786432 | tf_op jit(solution)/shard_map/all_to_all | solution.py:17
  (14 other events, 46.2 us)
where the time goes:
time: 189 us; the launch traced here: 187 us
  waiting for transfers between devices  68.9 us (36%)
  starting transfers between devices  46 us (24%)
  matrix products  32.4 us (17%)
  blocking collectives  12.6 us (7%)
  other arithmetic  12.4 us (7%)
  local copies, waits for them, and re-layouts  11 us (6%)
  between operations  3.89 us (2%)
    all_to_all x6, waiting for transfers between devices, from_everyone(): lax.all_to_all(jnp.broadcast_to(array[None], (length, *array.shape)), axi...  40.4 us
    all_to_all x6, starting transfers between devices, from_everyone(): lax.all_to_all(jnp.broadcast_to(array[None], (length, *array.shape)), axi...  26 us
    all_to_all x4, waiting for transfers between devices, sent_and_summed(): lax.all_to_all(tiles, axis, split_axis=0, concat_axis=0, tiled=True)  25.3 us
    all_to_all x4, starting transfers between devices, sent_and_summed(): lax.all_to_all(tiles, axis, split_axis=0, concat_axis=0, tiled=True)  16.2 us
    all_to_all x1, blocking collectives, from_everyone(): lax.all_to_all(jnp.broadcast_to(array[None], (length, *array.shape)), axi...  12.6 us
    dot_general x4, matrix products, apply_fast(): jnp.dot(hidden, usable_weights[1], preferred_element_type=jnp.float32)  11.5 us
    dot_general x4, matrix products, apply_fast(): jnp.dot(query_rows, usable_weights[0], preferred_element_type=jnp.float32)  7.86 us
    broadcast_in_dim x7, local copies, waits for them, and re-layouts, from_everyone(): jnp.broadcast_to(array[None], (length, *array.shape))  4.51 us
  transfers between devices with their start and end apart: 12, of which 11 were waited for; matrix products, arithmetic and copies ran while one was open for 13% of the time, Pallas kernels for 0%

commit v1 on v0

v1 whole, which is shorter than its diff:
```python
import functools

import jax
import jax.numpy as jnp
from jax import lax
from jax.experimental import pallas as pl
from jax.experimental.pallas import tpu as pltpu
from jax.sharding import Mesh
from jax.sharding import PartitionSpec as P

TOK = ("tok_0", "tok_1")

momentum_decay = 0.9
learn_rate = 0.05
epsilon = 1e-06

f32, bf16 = jnp.float32, jnp.bfloat16
VMEM_LIMIT = 24 * 1024 * 1024

NN = (((1,), (0,)), ((), ()))
NT = (((1,), (1,)), ((), ()))


def dot(a, b, dims):
    return lax.dot_general(a, b, dims, preferred_element_type=f32)


def sigmoid(a):
    return 0.5 * jnp.tanh(0.5 * a) + 0.5


def matrix(gathered_ref, index, share):
    tiles = gathered_ref[:, index * share : (index + 1) * share, :]
    return tiles.reshape(-1, tiles.shape[-1])


def whole(*shape):
    return pl.BlockSpec(shape, lambda *_: (0,) * len(shape))


def params(**more):
    return pltpu.CompilerParams(vmem_limit_bytes=VMEM_LIMIT, **more)


def spread_kernel(weights_ref, message_ref):
    message_ref[...] = jnp.broadcast_to(weights_ref[...].astype(bf16)[None], message_ref.shape)


def spread(weights, parties):
    rows, width = weights.shape
    return pl.pallas_call(
        spread_kernel,
        out_shape=jax.ShapeDtypeStruct((parties, rows, width), bf16),
        compiler_params=params(),
        name="spread",
    )(weights)


def grads_kernel(block, tile, gathered_ref, rate_ref, key_ref, value_ref, message_ref, left_ref, acc_ref):
    parties, _, width = message_ref.shape
    share = width // parties
    step = pl.program_id(0)

    @pl.when(step == 0)
    def _():
        left_ref[...] = matrix(gathered_ref, 1, share).astype(f32).T.astype(bf16)
        acc_ref[...] = jnp.zeros_like(acc_ref)

    keys, values = key_ref[...], value_ref[...]
    rate = rate_ref[block : block + 1, pl.ds(pl.multiple_of(step * tile, tile), tile)]
    pre_gate = dot(matrix(gathered_ref, 0, share), keys, NT)
    pre_up = dot(matrix(gathered_ref, 2, share), keys, NT)
    back = dot(left_ref[...], values, NT) * -rate
    sig = sigmoid(pre_gate)
    active = pre_gate * sig
    slope = sig + active * (1.0 - sig)
    back_up = (back * active).astype(bf16)
    back_gate = (back * pre_up * slope).astype(bf16)
    hidden = (active * pre_up * rate).astype(bf16)
    acc_ref[0] += dot(back_gate, keys, NN)
    acc_ref[1] += dot(hidden, values, NN)
    acc_ref[2] += dot(back_up, keys, NN)

    @pl.when(step == pl.num_programs(0) - 1)
    def _():
        grads = (acc_ref[0], -acc_ref[1].T, acc_ref[2])
        for index, grad in enumerate(grads):
            message_ref[:, index * share : (index + 1) * share, :] = (
                grad.astype(bf16).reshape(parties, share, width)
            )
        rates = rate_ref[block : block + 1, :]
        square = jnp.sum(rates * rates, axis=1, keepdims=True)
        high = square.astype(bf16).astype(f32)
        row = lax.broadcasted_iota(jnp.int32, (share, width), 0)
        extra = jnp.where(row == 0, high, jnp.where(row == 1, square - high, 0.0))
        message_ref[:, 3 * share :, :] = jnp.broadcast_to(
            extra.astype(bf16)[None], (parties, share, width)
        )


def grads(gathered, rates, keys, values, wave_step, block):
    parties, rows, width = gathered.shape
    blocks, count = keys.shape[2], keys.shape[3]
    tile = 256
    rows_of = pl.BlockSpec(
        (None, None, None, tile, width), lambda i: (wave_step, 0, block, i, 0)
    )
    return pl.pallas_call(
        functools.partial(grads_kernel, wave_step * blocks + block, tile),
        grid=(count // tile,),
        in_specs=[whole(*gathered.shape), whole(*rates.shape), rows_of, rows_of],
        out_specs=whole(parties, rows + rows // 3, width),
        out_shape=jax.ShapeDtypeStruct((parties, rows + rows // 3, width), bf16),
        scratch_shapes=[pltpu.VMEM((width, width), bf16), pltpu.VMEM((3, width, width), f32)],
        compiler_params=params(),
        cost_estimate=pl.CostEstimate(
            flops=12 * count * width * width, bytes_accessed=4 * count * width, transcendentals=0
        ),
        name="grads",
    )(gathered, rates, keys, values)


def update_kernel(arrived_ref, weights_ref, moment_ref, new_weights_ref, new_moment_ref, message_ref, *packed):
    rows = weights_ref.shape[0]
    gradients = jnp.sum(arrived_ref[:, :rows, :].astype(f32), axis=0)
    square = jnp.sum(jnp.sum(arrived_ref[:, rows:, :].astype(f32), axis=0), axis=0, keepdims=True)
    weights = weights_ref[...]
    moment = momentum_decay * moment_ref[...] + gradients * lax.rsqrt(square)
    stepped = weights - learn_rate * moment
    rescale = jnp.sqrt(
        jnp.sum(weights * weights, axis=1, keepdims=True)
        / (jnp.sum(stepped * stepped, axis=1, keepdims=True) + epsilon)
    )
    weights = stepped * rescale
    new_weights_ref[...] = weights
    new_moment_ref[...] = moment
    rounded = weights.astype(bf16)
    message_ref[...] = jnp.broadcast_to(rounded[None], message_ref.shape)
    if packed:
        packed[0][:rows, :] = rounded
        packed[0][rows:, :] = moment.astype(bf16)


def update(arrived, weights, moment, pack):
    rows, width = weights.shape
    state = jax.ShapeDtypeStruct((rows, width), f32)
    out_shape = [state, state, jax.ShapeDtypeStruct((arrived.shape[0], rows, width), bf16)]
    if pack:
        out_shape.append(jax.ShapeDtypeStruct((2 * rows, width), bf16))
    return pl.pallas_call(
        update_kernel, out_shape=out_shape, compiler_params=params(), name="update"
    )(arrived, weights, moment)


def enter_kernel(first_ref, passed_ref, fresh_weights_ref, fresh_moment_ref, weights_ref, moment_ref, message_ref):
    rows = weights_ref.shape[0]
    first = first_ref[0] == 1
    passed = passed_ref[...].astype(f32)
    weights = jnp.where(first, fresh_weights_ref[...], passed[:rows])
    weights_ref[...] = weights
    moment_ref[...] = jnp.where(first, fresh_moment_ref[...], passed[rows:])
    message_ref[...] = jnp.broadcast_to(weights.astype(bf16)[None], message_ref.shape)


def enter(first, passed, fresh_weights, fresh_moment, parties):
    rows, width = fresh_weights.shape
    state = jax.ShapeDtypeStruct((rows, width), f32)
    vmem = pl.BlockSpec(memory_space=pltpu.VMEM)
    return pl.pallas_call(
        enter_kernel,
        in_specs=[pl.BlockSpec(memory_space=pltpu.SMEM), vmem, vmem, vmem],
        out_shape=[state, state, jax.ShapeDtypeStruct((parties, rows, width), bf16)],
        compiler_params=params(),
        name="enter",
    )(first, passed, fresh_weights, fresh_moment)


def apply_kernel(gathered_ref, query_ref, *refs):
    result_ref = refs[-1]
    share = gathered_ref.shape[1] // 3
    queries = query_ref[...]
    pre_gate = dot(queries, matrix(gathered_ref, 0, share), NT)
    pre_up = dot(queries, matrix(gathered_ref, 2, share), NT)
    hidden = (pre_gate * sigmoid(pre_gate) * pre_up).astype(bf16)
    result_ref[...] = dot(hidden, matrix(gathered_ref, 1, share), NT).astype(bf16)


def apply_fast(gathered, queries, results, wave_step, block):
    count, width = queries.shape[3:]
    tile = 256
    rows_of = pl.BlockSpec(
        (None, None, None, tile, width), lambda i: (wave_step, 0, block, i, 0)
    )
    given = [gathered, queries]
    in_specs = [whole(*gathered.shape), rows_of]
    if results is not None:
        given.append(results)
        in_specs.append(pl.BlockSpec(memory_space=pl.ANY))
    return pl.pallas_call(
        apply_kernel,
        grid=(count // tile,),
        in_specs=in_specs,
        out_specs=rows_of,
        out_shape=jax.ShapeDtypeStruct(queries.shape, bf16),
        input_output_aliases={} if results is None else {2: 0},
        compiler_params=params(),
        cost_estimate=pl.CostEstimate(
            flops=6 * count * width * width, bytes_accessed=4 * count * width, transcendentals=0
        ),
        name="apply",
    )(*given)


def exchanged(tiles):
    return lax.all_to_all(tiles, TOK, split_axis=0, concat_axis=0, tiled=True)


def passed_on(array):
    length = lax.axis_size("seg")
    return lax.ppermute(array, "seg", [(i, i + 1) for i in range(length - 1)])


def columns_first(state):
    return jnp.swapaxes(state, 1, 2).reshape(-1, state.shape[1])


def rows_first(state, share):
    return jnp.swapaxes(state.reshape(-1, share, state.shape[1]), 1, 2)


def body(
    queries, key_vectors, values, token_rates, fast_weights, momenta, fresh_weights, fresh_momenta
):
    sections, _, blocks, count, _ = queries.shape
    parties = lax.axis_size(TOK)
    share = fast_weights.shape[3]
    rates = token_rates.reshape(sections * blocks, count)
    first = (lax.axis_index("seg") == 0).astype(jnp.int32).reshape(1)
    weights, moment = columns_first(fast_weights[0]), columns_first(momenta[0])
    fresh_weights, fresh_moment = columns_first(fresh_weights), columns_first(fresh_momenta)
    gathered = exchanged(spread(weights, parties))
    results = None
    for wave_step in range(sections):
        for block in range(blocks):
            leaving = block == blocks - 1 and wave_step < sections - 1
            arrived = exchanged(grads(gathered, rates, key_vectors, values, wave_step, block))
            weights, moment, message, *packed = update(arrived, weights, moment, leaving)
            gathered = exchanged(message)
            results = apply_fast(gathered, queries, results, wave_step, block)
            if leaving:
                weights, moment, message = enter(
                    first, passed_on(packed[0]), fresh_weights, fresh_moment, parties
                )
                gathered = exchanged(message)
    return (results, rows_first(weights, share)[None], rows_first(moment, share)[None])


def solution(mesh):
    finer = Mesh(mesh.devices.reshape(mesh.shape["seg"], 4, 4), ("seg", "tok_0", "tok_1"))
    placed = (
        P(None, "seg", None, TOK, None),
        P(None, "seg", None, TOK, None),
        P(None, "seg", None, TOK, None),
        P(None, "seg", None, TOK),
        P("seg", None, None, TOK),
        P("seg", None, None, TOK),
        P(None, None, TOK),
        P(None, None, TOK),
    )
    return jax.shard_map(
        body,
        mesh=finer,
        in_specs=placed,
        out_specs=(
            P(None, "seg", None, TOK, None),
            P("seg", None, None, TOK),
            P("seg", None, None, TOK),
        ),
        check_vma=False,
    )
```

time: 189 us -> 173 us (0.915)
  blocking collectives: 12.6 us -> 95 us
  waiting for transfers between devices: 68.9 us -> 19 us
  matrix products: 32.4 us -> 0 us
  Pallas kernels: 0 us -> 29.8 us
  starting transfers between devices: 46 us -> 17.4 us
  other arithmetic: 12.4 us -> 0 us
  between operations: 3.89 us -> 0.78 us
    all_to_all x1 -> x7, blocking collectives: 12.6 us -> 95 us  [exchanged(): return lax.all_to_all(tiles, TOK, split_axis=0, concat_axis=0, tiled=True)]
    all_to_all x10 -> x3, waiting for transfers between devices: 65.7 us -> 15.6 us  [exchanged(): return lax.all_to_all(tiles, TOK, split_axis=0, concat_axis=0, tiled=True)]
    dot_general x32 -> x0, matrix products: 32.4 us -> none  [the longest x4 11.5 us: apply_fast(): jnp.dot(hidden, usable_weights[1], preferred_element_type=jnp.float32)]
    pallas_call x0 -> x14, Pallas kernels: none -> 29.8 us  [the longest x4 14.6 us: apply_fast(): pl.pallas_call(apply_kernel, grid=(count // tile,), in_specs=in_specs, ou...]
    all_to_all x10 -> x3, starting transfers between devices: 42.2 us -> 15.5 us  [exchanged(): return lax.all_to_all(tiles, TOK, split_axis=0, concat_axis=0, tiled=True)]
    broadcast_in_dim x7 -> x0, local copies, waits for them, and re-layouts: 4.51 us -> none  [from_everyone(): jnp.broadcast_to(array[None], (length, *array.shape))]
    unnamed x52 -> x30, local copies, waits for them, and re-layouts: 4.23 us -> 8.59 us
    reduce_sum x10 -> x0, other arithmetic: 4 us -> none  [the longest x4 2.91 us: update(): jnp.sum(stepped * stepped, axis=1, keepdims=True) + epsilon]
  transfers between devices with their start and end apart: 12 -> 4, of which waited for: 11 -> 3; matrix products, arithmetic and copies ran while one was open for 13% -> 0% of each run, Pallas kernels for 0% -> 7%
where the time goes in v1:
time: 173 us; the launch traced here: 171 us
  blocking collectives  95 us (55%)
  Pallas kernels  29.8 us (17%)
  waiting for transfers between devices  19 us (11%)
  starting transfers between devices  17.4 us (10%)
  local copies, waits for them, and re-layouts  9.34 us (5%)
    all_to_all x7, blocking collectives, exchanged(): return lax.all_to_all(tiles, TOK, split_axis=0, concat_axis=0, tiled=True)  95 us
    all_to_all x3, waiting for transfers between devices, exchanged(): return lax.all_to_all(tiles, TOK, split_axis=0, concat_axis=0, tiled=True)  15.6 us
    all_to_all x3, starting transfers between devices, exchanged(): return lax.all_to_all(tiles, TOK, split_axis=0, concat_axis=0, tiled=True)  15.5 us
    pallas_call x4, Pallas kernels, apply_fast(): pl.pallas_call(apply_kernel, grid=(count // tile,), in_specs=in_specs, ou...  14.6 us
    pallas_call x4, Pallas kernels, grads(): pl.pallas_call(functools.partial(grads_kernel, wave_step * blocks + block...  12.4 us
    unnamed x30, local copies, waits for them, and re-layouts  8.59 us
    ppermute x1, waiting for transfers between devices, passed_on(): return lax.ppermute(array, 'seg', [(i, i + 1) for i in range(length - 1)])  3.47 us
  transfers between devices with their start and end apart: 4, of which 3 were waited for; matrix products, arithmetic and copies ran while one was open for 0% of the time, Pallas kernels for 7%

profile of v1, /device:TPU:96, one launch (start us, length us, event | category | flops | bytes accessed | tf_op | source)
XLA Modules:
  0.0 171.4 jit_solution(11258288694163750732)
XLA Ops:
  2.2 7.0 %all-to-all-start = ((bf16[16,48,256]{2,1,0:T(8,128)(2,1)}), bf16[16,48,256]{2,1,0:T(8,128)(2,1)S(1)}, u32[]{:S(2)}, u32[]{:S(2)}) async-start(bf16[16,48,256]{2,1,0:T(8,128)(2,1)} %spread.1), calls=%async_computation | async-start | bytes 786432 | tf_op jit(solution)/shard_map/all_to_all | solution.py:215
  10.0 9.1 %all-to-all-done.gathered_ref = bf16[16,48,256]{2,1,0:T(8,128)(2,1)S(1)} async-done(((bf16[16,48,256]{2,1,0:T(8,128)(2,1)}), bf16[16,48,256]{2,1,0:T(8,128)(2,1)S(1)}, u32[]{:S(2)}, u32[]{:S(2)}) %all-to-all-start) | async-done | bytes 393248 | tf_op jit(solution)/shard_map/all_to_all | solution.py:215
  19.1 1.7 %copy-done = bf16[2,1,2,1280,256]{4,3,2,1,0:T(8,128)(2,1)S(1)} copy-done((bf16[2,1,2,1280,256]{4,3,2,1,0:T(8,128)(2,1)S(1)}, bf16[2,1,2,1280,256]{4,3,2,1,0:T(8,128)(2,1)}, u32[]{:S(2)}) %copy-start) | copy-done | bytes 2621464
  22.6 3.1 %grads.4 = bf16[16,64,256]{2,1,0:T(8,128)(2,1)S(1)} custom-call(bf16[16,48,256]{2,1,0:T(8,128)(2,1)S(1)} %all-to-all-done.gathered_ref, f32[4,1280]{1,0:T(4,128)S(1)} %reshape.35.rate_ref, bf16[2,1,2,1280,256]{4,3,2,1,0:T(8,128)(2,1)S(1)} %copy-done, bf16[2,1,2,1280,256]{4,3,2,1,0:T(8,128)(2,1)S(1)} %copy-done.2), custom_call_target="tpu_custom_call" | custom-call | flops 1006632960 | bytes 1310720 | tf_op jit(solution)/shard_map/grads/pallas_call | solution.py:108
  25.7 13.8 %all_to_all.50.arrived_ref = bf16[16,64,256]{2,1,0:T(8,128)(2,1)S(1)} all-to-all(bf16[16,64,256]{2,1,0:T(8,128)(2,1)S(1)} %grads.4), channel_id=1, replica_groups=mesh['seg'=16,'tok_0'=4,'tok_1'=4] {'tok_0','tok_1'}, dimensions={0} | all-to-all | bytes 1048576 | tf_op jit(solution)/shard_map/all_to_all | solution.py:215
  39.7 12.4 %all_to_all.51.gathered_ref = bf16[16,48,256]{2,1,0:T(8,128)(2,1)S(1)} all-to-all(bf16[16,48,256]{2,1,0:T(8,128)(2,1)S(1)} %get-tuple-element.17), channel_id=1, replica_groups=mesh['seg'=16,'tok_0'=4,'tok_1'=4] {'tok_0','tok_1'}, dimensions={0} | all-to-all | bytes 786432 | tf_op jit(solution)/shard_map/all_to_all | solution.py:215
  52.1 3.1 %grads.5 = bf16[16,64,256]{2,1,0:T(8,128)(2,1)S(1)} custom-call(bf16[16,48,256]{2,1,0:T(8,128)(2,1)S(1)} %all_to_all.51.gathered_ref, f32[4,1280]{1,0:T(4,128)S(1)} %reshape.35.rate_ref, bf16[2,1,2,1280,256]{4,3,2,1,0:T(8,128)(2,1)S(1)} %copy-done.1, bf16[2,1,2,1280,256]{4,3,2,1,0:T(8,128)(2,1)S(1)} %copy-done.3), custom_call_target="tpu_custom_call" | custom-call | flops 1006632960 | bytes 1310720 | tf_op jit(solution)/shard_map/grads/pallas_call | solution.py:108
  55.2 13.6 %all_to_all.52.arrived_ref = bf16[16,64,256]{2,1,0:T(8,128)(2,1)S(1)} all-to-all(bf16[16,64,256]{2,1,0:T(8,128)(2,1)S(1)} %grads.5), channel_id=1, replica_groups=mesh['seg'=16,'tok_0'=4,'tok_1'=4] {'tok_0','tok_1'}, dimensions={0} | all-to-all | bytes 1048576 | tf_op jit(solution)/shard_map/all_to_all | solution.py:215
  70.4 1.9 %collective-permute-start = (bf16[96,256]{1,0:T(8,128)(2,1)S(1)}, bf16[96,256]{1,0:T(8,128)(2,1)S(1)}, u32[]{:S(2)}, u32[]{:S(2)}) collective-permute-start(bf16[96,256]{1,0:T(8,128)(2,1)S(1)} %get-tuple-element.20), channel_id=1, source_target_pairs={{0,16},{16,32},{32,48},{48,64},{64,80},{80,96},{96,112},{112,128},... | collective-permute-start | bytes 147464 | tf_op jit(solution)/shard_map/ppermute | solution.py:220
  72.3 3.5 %collective-permute-done.passed_ref = bf16[96,256]{1,0:T(8,128)(2,1)S(1)} collective-permute-done((bf16[96,256]{1,0:T(8,128)(2,1)S(1)}, bf16[96,256]{1,0:T(8,128)(2,1)S(1)}, u32[]{:S(2)}, u32[]{:S(2)}) %collective-permute-start) | collective-permute-done | bytes 49184 | tf_op jit(solution)/shard_map/ppermute | solution.py:220
  75.9 14.3 %all_to_all.53.gathered_ref = bf16[16,48,256]{2,1,0:T(8,128)(2,1)S(1)} all-to-all(bf16[16,48,256]{2,1,0:T(8,128)(2,1)S(1)} %get-tuple-element.21), channel_id=1, replica_groups=mesh['seg'=16,'tok_0'=4,'tok_1'=4] {'tok_0','tok_1'}, dimensions={0} | all-to-all | bytes 786432 | tf_op jit(solution)/shard_map/all_to_all | solution.py:215
  90.2 1.7 %copy-done.4 = bf16[2,1,2,1280,256]{4,3,2,1,0:T(8,128)(2,1)S(1)} copy-done((bf16[2,1,2,1280,256]{4,3,2,1,0:T(8,128)(2,1)S(1)}, bf16[2,1,2,1280,256]{4,3,2,1,0:T(8,128)(2,1)}, u32[]{:S(2)}) %copy-start.4) | copy-done | bytes 2621464
  91.9 3.1 %grads.6 = bf16[16,64,256]{2,1,0:T(8,128)(2,1)S(1)} custom-call(bf16[16,48,256]{2,1,0:T(8,128)(2,1)S(1)} %all_to_all.53.gathered_ref, f32[4,1280]{1,0:T(4,128)S(1)} %reshape.35.rate_ref, bf16[2,1,2,1280,256]{4,3,2,1,0:T(8,128)(2,1)S(1)} %copy-done.1, bf16[2,1,2,1280,256]{4,3,2,1,0:T(8,128)(2,1)S(1)} %copy-done.4), custom_call_target="tpu_custom_call" | custom-call | flops 1006632960 | bytes 1310720 | tf_op jit(solution)/shard_map/grads/pallas_call | solution.py:108
  95.0 14.5 %all_to_all.54.arrived_ref = bf16[16,64,256]{2,1,0:T(8,128)(2,1)S(1)} all-to-all(bf16[16,64,256]{2,1,0:T(8,128)(2,1)S(1)} %grads.6), channel_id=1, replica_groups=mesh['seg'=16,'tok_0'=4,'tok_1'=4] {'tok_0','tok_1'}, dimensions={0} | all-to-all | bytes 1048576 | tf_op jit(solution)/shard_map/all_to_all | solution.py:215
  109.7 12.4 %all_to_all.55.gathered_ref = bf16[16,48,256]{2,1,0:T(8,128)(2,1)S(1)} all-to-all(bf16[16,48,256]{2,1,0:T(8,128)(2,1)S(1)} %get-tuple-element.24), channel_id=1, replica_groups=mesh['seg'=16,'tok_0'=4,'tok_1'=4] {'tok_0','tok_1'}, dimensions={0} | all-to-all | bytes 786432 | tf_op jit(solution)/shard_map/all_to_all | solution.py:215
  122.2 3.1 %grads.7 = bf16[16,64,256]{2,1,0:T(8,128)(2,1)S(1)} custom-call(bf16[16,48,256]{2,1,0:T(8,128)(2,1)S(1)} %all_to_all.55.gathered_ref, f32[4,1280]{1,0:T(4,128)S(1)} %reshape.35.rate_ref, bf16[2,1,2,1280,256]{4,3,2,1,0:T(8,128)(2,1)S(1)} %copy-done.1, bf16[2,1,2,1280,256]{4,3,2,1,0:T(8,128)(2,1)S(1)} %copy-done.5), custom_call_target="tpu_custom_call" | custom-call | flops 1006632960 | bytes 1310720 | tf_op jit(solution)/shard_map/grads/pallas_call | solution.py:108
  125.3 14.0 %all_to_all.56.arrived_ref = bf16[16,64,256]{2,1,0:T(8,128)(2,1)} all-to-all(bf16[16,64,256]{2,1,0:T(8,128)(2,1)S(1)} %grads.7), channel_id=1, replica_groups=mesh['seg'=16,'tok_0'=4,'tok_1'=4] {'tok_0','tok_1'}, dimensions={0} | all-to-all | bytes 1048576 | tf_op jit(solution)/shard_map/all_to_all | solution.py:215
  139.3 4.2 %all-to-all-start.9 = ((bf16[16,48,256]{2,1,0:T(8,128)(2,1)}), bf16[16,48,256]{2,1,0:T(8,128)(2,1)}, u32[]{:S(2)}, u32[]{:S(2)}) async-start(bf16[16,48,256]{2,1,0:T(8,128)(2,1)} %copy-done.8), calls=%async_computation.9 | async-start | bytes 786432 | tf_op jit(solution)/shard_map/all_to_all | solution.py:215
  146.1 6.5 %all-to-all-done.9.gathered_ref = bf16[16,48,256]{2,1,0:T(8,128)(2,1)} async-done(((bf16[16,48,256]{2,1,0:T(8,128)(2,1)}), bf16[16,48,256]{2,1,0:T(8,128)(2,1)}, u32[]{:S(2)}, u32[]{:S(2)}) %all-to-all-start.9) | async-done | bytes 393248 | tf_op jit(solution)/shard_map/all_to_all | solution.py:215
  152.6 4.2 %all-to-all-start.8 = ((bf16[16,48,256]{2,1,0:T(8,128)(2,1)}), bf16[16,48,256]{2,1,0:T(8,128)(2,1)}, u32[]{:S(2)}, u32[]{:S(2)}) async-start(bf16[16,48,256]{2,1,0:T(8,128)(2,1)} %copy-done.9), calls=%async_computation.8 | async-start | bytes 786432 | tf_op jit(solution)/shard_map/all_to_all | solution.py:215
  156.8 3.2 %apply.4.refs_0_ = bf16[2,1,2,1280,256]{4,3,2,1,0:T(8,128)(2,1)} custom-call(bf16[16,48,256]{2,1,0:T(8,128)(2,1)S(1)} %all_to_all.51.gathered_ref, bf16[2,1,2,1280,256]{4,3,2,1,0:T(8,128)(2,1)S(1)} %copy-done.6), custom_call_target="tpu_custom_call" | custom-call | flops 503316480 | bytes 1310720 | tf_op jit(solution)/shard_map/apply/pallas_call | solution.py:199
  160.0 4.1 %apply.5.refs_0_ = bf16[2,1,2,1280,256]{4,3,2,1,0:T(8,128)(2,1)} custom-call(bf16[16,48,256]{2,1,0:T(8,128)(2,1)} %all-to-all-done.9.gathered_ref, bf16[2,1,2,1280,256]{4,3,2,1,0:T(8,128)(2,1)S(1)} %copy-done.6, bf16[2,1,2,1280,256]{4,3,2,1,0:T(8,128)(2,1)} %apply.4.refs_0_), custom_call_target="tpu_custom_call", output_to_operand_aliasing={{}: (2, {})} | custom-call | flops 503316480 | bytes 1310720 | tf_op jit(solution)/shard_map/apply/pallas_call | solution.py:199
  164.1 3.1 %apply.6.refs_0_ = bf16[2,1,2,1280,256]{4,3,2,1,0:T(8,128)(2,1)} custom-call(bf16[16,48,256]{2,1,0:T(8,128)(2,1)S(1)} %all_to_all.55.gathered_ref, bf16[2,1,2,1280,256]{4,3,2,1,0:T(8,128)(2,1)S(1)} %copy-done.6, bf16[2,1,2,1280,256]{4,3,2,1,0:T(8,128)(2,1)} %apply.5.refs_0_), custom_call_target="tpu_custom_call", output_to_operand_aliasing={{}: (2, {})} | custom-call | flops 503316480 | bytes 1310720 | tf_op jit(solution)/shard_map/apply/pallas_call | solution.py:199
  167.3 4.1 %apply.7 = bf16[2,1,2,1280,256]{4,3,2,1,0:T(8,128)(2,1)} custom-call(bf16[16,48,256]{2,1,0:T(8,128)(2,1)} %all-to-all-done.8.gathered_ref, bf16[2,1,2,1280,256]{4,3,2,1,0:T(8,128)(2,1)S(1)} %copy-done.6, bf16[2,1,2,1280,256]{4,3,2,1,0:T(8,128)(2,1)} %apply.6.refs_0_), custom_call_target="tpu_custom_call", output_to_operand_aliasing={{}: (2, {})} | custom-call | flops 503316480 | bytes 1310720 | tf_op jit(solution)/shard_map/apply/pallas_call | solution.py:199
  (36 shorter events, 8.7 us)
Async XLA Ops:
  0.6 0.8 copy-start.10
  2.2 16.9 %all-to-all-start = ((bf16[16,48,256]{2,1,0:T(8,128)(2,1)}), bf16[16,48,256]{2,1,0:T(8,128)(2,1)S(1)}, u32[]{:S(2)}, u32[]{:S(2)}) async-start(bf16[16,48,256]{2,1,0:T(8,128)(2,1)} %spread.1), calls=%async_computation | async-start | bytes 786432 | tf_op jit(solution)/shard_map/all_to_all | solution.py:215
  19.1 1.7 %copy-start = (bf16[2,1,2,1280,256]{4,3,2,1,0:T(8,128)(2,1)S(1)}, bf16[2,1,2,1280,256]{4,3,2,1,0:T(8,128)(2,1)}, u32[]{:S(2)}) copy-start(bf16[2,1,2,1280,256]{4,3,2,1,0:T(8,128)(2,1)} %key_ref.7) | copy-start | bytes 7864324
  20.8 1.7 %copy-start.2 = (bf16[2,1,2,1280,256]{4,3,2,1,0:T(8,128)(2,1)S(1)}, bf16[2,1,2,1280,256]{4,3,2,1,0:T(8,128)(2,1)}, u32[]{:S(2)}) copy-start(bf16[2,1,2,1280,256]{4,3,2,1,0:T(8,128)(2,1)} %value_ref.7) | copy-start | bytes 7864324
  22.5 17.0 %copy-start.11 = (f32[1,3,256,16]{2,3,1,0:T(8,128)S(1)}, f32[1,3,256,16]{2,3,1,0:T(8,128)}, u32[]{:S(2)}) copy-start(f32[1,3,256,16]{2,3,1,0:T(8,128)} %param.12) | copy-start | bytes 147460
  22.6 17.0 %copy-start.12 = (f32[1,3,256,16]{2,3,1,0:T(8,128)S(1)}, f32[1,3,256,16]{2,3,1,0:T(8,128)}, u32[]{:S(2)}) copy-start(f32[1,3,256,16]{2,3,1,0:T(8,128)} %param.13) | copy-start | bytes 147460
  22.6 29.5 %copy-start.1 = (bf16[2,1,2,1280,256]{4,3,2,1,0:T(8,128)(2,1)S(1)}, bf16[2,1,2,1280,256]{4,3,2,1,0:T(8,128)(2,1)}, u32[]{:S(2)}) copy-start(bf16[2,1,2,1280,256]{4,3,2,1,0:T(8,128)(2,1)} %key_ref.7) | copy-start | bytes 7864324
  22.6 29.5 %copy-start.3 = (bf16[2,1,2,1280,256]{4,3,2,1,0:T(8,128)(2,1)S(1)}, bf16[2,1,2,1280,256]{4,3,2,1,0:T(8,128)(2,1)}, u32[]{:S(2)}) copy-start(bf16[2,1,2,1280,256]{4,3,2,1,0:T(8,128)(2,1)} %value_ref.7) | copy-start | bytes 7864324
  52.1 23.7 %copy-start.13 = (f32[3,256,16]{1,2,0:T(8,128)S(1)}, f32[3,256,16]{1,2,0:T(8,128)}, u32[]{:S(2)}) copy-start(f32[3,256,16]{1,2,0:T(8,128)} %param.14) | copy-start | bytes 147460
  52.1 23.7 %copy-start.14 = (f32[3,256,16]{1,2,0:T(8,128)S(1)}, f32[3,256,16]{1,2,0:T(8,128)}, u32[]{:S(2)}) copy-start(f32[3,256,16]{1,2,0:T(8,128)} %param.15) | copy-start | bytes 147460
  69.7 0.7 copy-start.8
  70.4 5.4 %collective-permute-start = (bf16[96,256]{1,0:T(8,128)(2,1)S(1)}, bf16[96,256]{1,0:T(8,128)(2,1)S(1)}, u32[]{:S(2)}, u32[]{:S(2)}) collective-permute-start(bf16[96,256]{1,0:T(8,128)(2,1)S(1)} %get-tuple-element.20), channel_id=1, source_target_pairs={{0,16},{16,32},{32,48},{48,64},{64,80},{80,96},{96,112},{112,128},... | collective-permute-start | bytes 147464 | tf_op jit(solution)/shard_map/ppermute | solution.py:220
  90.2 1.7 %copy-start.4 = (bf16[2,1,2,1280,256]{4,3,2,1,0:T(8,128)(2,1)S(1)}, bf16[2,1,2,1280,256]{4,3,2,1,0:T(8,128)(2,1)}, u32[]{:S(2)}) copy-start(bf16[2,1,2,1280,256]{4,3,2,1,0:T(8,128)(2,1)} %value_ref.7) | copy-start | bytes 7864324
  91.9 30.3 %copy-start.5 = (bf16[2,1,2,1280,256]{4,3,2,1,0:T(8,128)(2,1)S(1)}, bf16[2,1,2,1280,256]{4,3,2,1,0:T(8,128)(2,1)}, u32[]{:S(2)}) copy-start(bf16[2,1,2,1280,256]{4,3,2,1,0:T(8,128)(2,1)} %value_ref.7) | copy-start | bytes 7864324
  125.3 31.6 %copy-start.6 = (bf16[2,1,2,1280,256]{4,3,2,1,0:T(8,128)(2,1)S(1)}, bf16[2,1,2,1280,256]{4,3,2,1,0:T(8,128)(2,1)}, u32[]{:S(2)}) copy-start(bf16[2,1,2,1280,256]{4,3,2,1,0:T(8,128)(2,1)} %query_ref.7) | copy-start | bytes 7864324
  139.3 13.4 %all-to-all-start.9 = ((bf16[16,48,256]{2,1,0:T(8,128)(2,1)}), bf16[16,48,256]{2,1,0:T(8,128)(2,1)}, u32[]{:S(2)}, u32[]{:S(2)}) async-start(bf16[16,48,256]{2,1,0:T(8,128)(2,1)} %copy-done.8), calls=%async_computation.9 | async-start | bytes 786432 | tf_op jit(solution)/shard_map/all_to_all | solution.py:215
  143.5 1.0 copy-start.7
  145.3 0.8 copy-start.9
  152.6 14.7 %all-to-all-start.8 = ((bf16[16,48,256]{2,1,0:T(8,128)(2,1)}), bf16[16,48,256]{2,1,0:T(8,128)(2,1)}, u32[]{:S(2)}, u32[]{:S(2)}) async-start(bf16[16,48,256]{2,1,0:T(8,128)(2,1)} %copy-done.9), calls=%async_computation.8 | async-start | bytes 786432 | tf_op jit(solution)/shard_map/all_to_all | solution.py:215

commit v2 on v1

v2 whole, which is shorter than its diff:
```python
import functools

import jax
import jax.numpy as jnp
from jax import lax
from jax.experimental import pallas as pl
from jax.experimental.pallas import tpu as pltpu
from jax.sharding import Mesh
from jax.sharding import PartitionSpec as P

TOK = ("tok_0", "tok_1")

momentum_decay = 0.9
learn_rate = 0.05
epsilon = 1e-06

f32, bf16 = jnp.float32, jnp.bfloat16
VMEM_LIMIT = 16 * 1024 * 1024

NN = (((1,), (0,)), ((), ()))
NT = (((1,), (1,)), ((), ()))


def dot(a, b, dims):
    return lax.dot_general(a, b, dims, preferred_element_type=f32)


def sigmoid(a):
    return 0.5 * jnp.tanh(0.5 * a) + 0.5


def matrix(gathered_ref, index, share):
    tiles = gathered_ref[:, index * share : (index + 1) * share, :]
    return tiles.reshape(-1, tiles.shape[-1])


def params(**more):
    return pltpu.CompilerParams(vmem_limit_bytes=VMEM_LIMIT, **more)


def in_vmem(*shape, dtype=f32):
    return pltpu.VMEM(shape, dtype)


VMEM = pl.BlockSpec(memory_space=pltpu.VMEM)
HBM = pl.BlockSpec(memory_space=pltpu.HBM)
ANY = pl.BlockSpec(memory_space=pl.ANY)
SMEM = pl.BlockSpec(memory_space=pltpu.SMEM)


TOKEN = jax.ShapeDtypeStruct((8, 128), f32)


def in_hbm(array):
    return pltpu.with_memory_space_constraint(array, pltpu.HBM)


def spread_kernel(weights_ref, message_ref, token_ref):
    message_ref[...] = jnp.broadcast_to(weights_ref[...].astype(bf16)[None], message_ref.shape)
    token_ref[...] = jnp.zeros_like(token_ref)


def spread(weights, parties):
    rows, width = weights.shape
    return pl.pallas_call(
        spread_kernel,
        in_specs=[VMEM],
        out_specs=[VMEM] * 2,
        out_shape=[in_vmem(parties, rows, width, dtype=bf16), TOKEN],
        compiler_params=params(),
        name="spread",
    )(weights)


def stage_kernel(place, count, *refs):
    sources, targets, sems = refs[1 : 1 + count], refs[1 + count : 1 + 2 * count], refs[-1]
    copies = [
        pltpu.make_async_copy(source.at[*place], target, sems.at[index])
        for index, (source, target) in enumerate(zip(sources, targets))
    ]
    for copy in copies:
        copy.start()
    for copy in copies:
        copy.wait()


def stage(token, place, *arrays):
    return pl.pallas_call(
        functools.partial(stage_kernel, place, len(arrays)),
        in_specs=[VMEM] + [HBM] * len(arrays),
        out_specs=[VMEM] * len(arrays),
        out_shape=[in_vmem(*array.shape[3:], dtype=array.dtype) for array in arrays],
        scratch_shapes=[pltpu.SemaphoreType.DMA((len(arrays),))],
        compiler_params=params(),
        cost_estimate=pl.CostEstimate(
            flops=0, bytes_accessed=len(arrays) * arrays[0].size, transcendentals=0
        ),
        name="stage",
    )(token, *(in_hbm(array) for array in arrays))


def grads_kernel(
    block, tile, offset, gathered_ref, rate_ref, key_rows, value_rows, message_ref, left_ref, back_ref
):
    parties, rows, width = message_ref.shape
    share = width // parties
    count = key_rows.shape[0]
    base = offset // share
    left_ref[...] = matrix(gathered_ref, base + 1, share).astype(f32).T.astype(bf16)
    gate, up = matrix(gathered_ref, base, share), matrix(gathered_ref, base + 2, share)
    for start in range(0, count, tile):
        span = slice(start, start + tile)
        keys, values = key_rows[span, :], value_rows[span, :]
        rate = rate_ref[block : block + 1, span]
        pre_gate = dot(gate, keys, NT)
        pre_up = dot(up, keys, NT)
        back = dot(left_ref[...], values, NT) * -rate
        sig = sigmoid(pre_gate)
        active = pre_gate * sig
        slope = sig + active * (1.0 - sig)
        back_ref[0, :, span] = (back * pre_up * slope).astype(bf16)
        back_ref[1, :, span] = (active * pre_up * rate).astype(bf16)
        back_ref[2, :, span] = (back * active).astype(bf16)
    keys, values = key_rows[...], value_rows[...]
    gradients = (
        dot(back_ref[0], keys, NN),
        -dot(back_ref[1], values, NN).T,
        dot(back_ref[2], keys, NN),
    )
    for index, gradient in enumerate(gradients):
        message_ref[:, index * share : (index + 1) * share, :] = gradient.astype(bf16).reshape(
            parties, share, width
        )
    if rows > 3 * share:
        rates = rate_ref[...]
        squares = jnp.sum(rates * rates, axis=1, keepdims=True)
        row = lax.broadcasted_iota(jnp.int32, (share, width), 0)
        extra = jnp.zeros((share, width), f32)
        for index in range(rates.shape[0]):
            square = squares[index : index + 1, :]
            high = square.astype(bf16).astype(f32)
            extra = jnp.where(row == 2 * index, high, extra)
            extra = jnp.where(row == 2 * index + 1, square - high, extra)
        message_ref[:, 3 * share :, :] = jnp.broadcast_to(
            extra.astype(bf16)[None], (parties, share, width)
        )


def grads(gathered, offset, rates, keys, values, index):
    parties, _, width = gathered.shape
    share = width // parties
    count = keys.shape[0]
    rows = (4 if index == 0 else 3) * share
    return pl.pallas_call(
        functools.partial(grads_kernel, index, 256, offset),
        in_specs=[VMEM] * 4,
        out_specs=VMEM,
        out_shape=in_vmem(parties, rows, width, dtype=bf16),
        scratch_shapes=[pltpu.VMEM((width, width), bf16), pltpu.VMEM((3, width, count), bf16)],
        compiler_params=params(),
        cost_estimate=pl.CostEstimate(
            flops=12 * count * width * width, bytes_accessed=4 * count * width, transcendentals=0
        ),
        name="grads",
    )(gathered, rates, keys, values)


def update_kernel(index, waits, *refs):
    arrived_ref, weights_ref, moment_ref = refs[:3]
    refs = refs[3:]
    rows = weights_ref.shape[0]
    gradients = jnp.sum(arrived_ref[:, :rows, :].astype(f32), axis=0)
    if index == 0:
        squares = jnp.sum(arrived_ref[:, rows:, :].astype(f32), axis=0)
        refs[-2][...] = squares
    else:
        squares, refs = refs[0][...], refs[1:]
    new_weights_ref, new_moment_ref, message_ref = refs[waits : waits + 3]
    token_ref = refs[-1]
    token_ref[...] = jnp.zeros_like(token_ref)
    square = squares[2 * index : 2 * index + 1, :] + squares[2 * index + 1 : 2 * index + 2, :]
    weights = weights_ref[...]
    moment = momentum_decay * moment_ref[...] + gradients * lax.rsqrt(square)
    stepped = weights - learn_rate * moment
    rescale = jnp.sqrt(
        jnp.sum(weights * weights, axis=1, keepdims=True)
        / (jnp.sum(stepped * stepped, axis=1, keepdims=True) + epsilon)
    )
    weights = stepped * rescale
    new_weights_ref[...] = weights
    new_moment_ref[...] = moment
    rounded = weights.astype(bf16)
    if len(message_ref.shape) == 3:
        message_ref[...] = jnp.broadcast_to(rounded[None], message_ref.shape)
    else:
        message_ref[:rows, :] = rounded
        message_ref[rows:, :] = moment.astype(bf16)


def update(index, arrived, weights, moment, squares, token, leaving):
    rows, width = weights.shape
    given, in_specs = [arrived, weights, moment], [VMEM] * 3
    if index > 0:
        given.append(squares)
        in_specs.append(VMEM)
    if token is not None:
        given.append(token)
        in_specs.append(VMEM)
    out_shape = [in_vmem(rows, width), in_vmem(rows, width)]
    if leaving:
        out_shape.append(in_vmem(2 * rows, width, dtype=bf16))
    else:
        out_shape.append(in_vmem(arrived.shape[0], rows, width, dtype=bf16))
    if index == 0:
        out_shape.append(in_vmem(arrived.shape[1] - rows, width))
    out_shape.append(TOKEN)
    return pl.pallas_call(
        functools.partial(update_kernel, index, int(token is not None)),
        in_specs=in_specs,
        out_specs=[VMEM] * len(out_shape),
        out_shape=out_shape,
        compiler_params=params(),
        name="update",
    )(*given)


def enter_kernel(
    first_ref,
    passed_ref,
    own_ref,
    fresh_weights_ref,
    fresh_moment_ref,
    weights_ref,
    moment_ref,
    message_ref,
    token_ref,
):
    token_ref[...] = jnp.zeros_like(token_ref)
    rows = weights_ref.shape[0]
    first = first_ref[0] == 1
    passed = passed_ref[...].astype(f32)
    weights = jnp.where(first, fresh_weights_ref[...], passed[:rows])
    weights_ref[...] = weights
    moment_ref[...] = jnp.where(first, fresh_moment_ref[...], passed[rows:])
    shape = (message_ref.shape[0], *weights.shape)
    message_ref[:, :rows, :] = jnp.broadcast_to(weights.astype(bf16)[None], shape)
    message_ref[:, rows:, :] = jnp.broadcast_to(own_ref[:rows, :][None], shape)


def enter(first, passed, own, fresh_weights, fresh_moment, parties):
    rows, width = fresh_weights.shape
    return pl.pallas_call(
        enter_kernel,
        in_specs=[SMEM] + [VMEM] * 4,
        out_specs=[VMEM] * 4,
        out_shape=[
            in_vmem(rows, width),
            in_vmem(rows, width),
            in_vmem(parties, 2 * rows, width, dtype=bf16),
            TOKEN,
        ],
        compiler_params=params(),
        name="enter",
    )(first, passed, own, fresh_weights, fresh_moment)


def apply_kernel(place, offset, staged, gathered_ref, query_ref, *refs):
    out_ref, token_ref, query_rows, held_ref, sems = refs[-5:]
    token_ref[...] = jnp.zeros_like(token_ref)
    width = query_rows.shape[-1]
    share = width // gathered_ref.shape[0]
    base = offset // share
    if staged:
        queries = query_ref[...]
    else:
        copy = pltpu.make_async_copy(query_ref.at[*place], query_rows, sems.at[0])
        copy.start()
        copy.wait()
        queries = query_rows[...]
    pre_gate = dot(queries, matrix(gathered_ref, base, share), NT)
    pre_up = dot(queries, matrix(gathered_ref, base + 2, share), NT)
    hidden = (pre_gate * sigmoid(pre_gate) * pre_up).astype(bf16)
    held_ref[...] = dot(hidden, matrix(gathered_ref, base + 1, share), NT).astype(bf16)
    copy = pltpu.make_async_copy(held_ref, out_ref.at[*place], sems.at[1])
    copy.start()
    copy.wait()


def apply_fast(gathered, offset, queries, results, shape, wave_step, block):
    count, width = shape[3:]
    staged = len(queries.shape) == 2
    given, in_specs = [gathered, queries], [VMEM, VMEM if staged else HBM]
    if results is not None:
        given.append(results)
        in_specs.append(HBM)
    return pl.pallas_call(
        functools.partial(apply_kernel, (wave_step, 0, block), offset, staged),
        in_specs=in_specs,
        out_specs=[HBM, VMEM],
        out_shape=[jax.ShapeDtypeStruct(shape, bf16), TOKEN],
        input_output_aliases={} if results is None else {2: 0},
        scratch_shapes=[
            pltpu.VMEM((count, width), bf16),
            pltpu.VMEM((count, width), bf16),
            pltpu.SemaphoreType.DMA((2,)),
        ],
        compiler_params=params(),
        cost_estimate=pl.CostEstimate(
            flops=6 * count * width * width, bytes_accessed=4 * count * width, transcendentals=0
        ),
        name="apply",
    )(*given)


def exchanged(tiles):
    return lax.all_to_all(tiles, TOK, split_axis=0, concat_axis=0, tiled=True)


def passed_on(array):
    length = lax.axis_size("seg")
    return lax.ppermute(array, "seg", [(i, i + 1) for i in range(length - 1)])


def columns_first(state):
    return jnp.swapaxes(state, 1, 2).reshape(-1, state.shape[1])


def rows_first(state, share):
    return jnp.swapaxes(state.reshape(-1, share, state.shape[1]), 1, 2)


def body(
    queries, key_vectors, values, token_rates, fast_weights, momenta, fresh_weights, fresh_momenta
):
    sections, _, blocks, count, _ = queries.shape
    parties = lax.axis_size(TOK)
    share = fast_weights.shape[3]
    rates = token_rates.reshape(sections * blocks, count)
    first = (lax.axis_index("seg") == 0).astype(jnp.int32).reshape(1)
    weights, moment = columns_first(fast_weights[0]), columns_first(momenta[0])
    fresh_weights, fresh_moment = columns_first(fresh_weights), columns_first(fresh_momenta)
    message, token = spread(weights, parties)
    gathered, offset = exchanged(message), 0
    results = squares = applied = pending = None
    rows = weights.shape[0]
    for wave_step in range(sections):
        for block in range(blocks):
            index = wave_step * blocks + block
            leaving = block == blocks - 1 and wave_step < sections - 1
            rows_here = stage(token, (wave_step, 0, block), key_vectors, values)
            arrived = exchanged(grads(gathered, offset, rates, *rows_here, index))
            if pending is not None:
                results, applied = apply_fast(
                    gathered, pending[0], in_hbm(queries), results, queries.shape, *pending[1:]
                )
            weights, moment, message, *more, token = update(
                index, arrived, weights, moment, squares, applied, leaving
            )
            squares = more[0] if more else squares
            offset = 0
            pending = (0, wave_step, block)
            if leaving:
                weights, moment, message, token = enter(
                    first, passed_on(message), message, fresh_weights, fresh_moment, parties
                )
                pending = (rows, wave_step, block)
            gathered = exchanged(message)
    (last_rows,) = stage(token, (sections - 1, 0, blocks - 1), queries)
    results, _ = apply_fast(gathered, pending[0], last_rows, results, queries.shape, *pending[1:])
    return (results, rows_first(weights, share)[None], rows_first(moment, share)[None])


def solution(mesh):
    finer = Mesh(mesh.devices.reshape(mesh.shape["seg"], 4, 4), ("seg", "tok_0", "tok_1"))
    placed = (
        P(None, "seg", None, TOK, None),
        P(None, "seg", None, TOK, None),
        P(None, "seg", None, TOK, None),
        P(None, "seg", None, TOK),
        P("seg", None, None, TOK),
        P("seg", None, None, TOK),
        P(None, None, TOK),
        P(None, None, TOK),
    )
    return jax.shard_map(
        body,
        mesh=finer,
        in_specs=placed,
        out_specs=(
            P(None, "seg", None, TOK, None),
            P("seg", None, None, TOK),
            P("seg", None, None, TOK),
        ),
        check_vma=False,
    )
```

time: 173 us -> 152 us (0.88)
  blocking collectives: 95 us -> 13.8 us
  waiting for transfers between devices: 19 us -> 68 us
  starting transfers between devices: 17.4 us -> 34.8 us
  local copies, waits for them, and re-layouts: 9.34 us -> 2.81 us
    all_to_all x7 -> x1, blocking collectives: 95 us -> 13.8 us  [exchanged(): return lax.all_to_all(tiles, TOK, split_axis=0, concat_axis=0, tiled=True)]
    all_to_all x3 -> x8, waiting for transfers between devices: 15.6 us -> 64.5 us  [exchanged(): return lax.all_to_all(tiles, TOK, split_axis=0, concat_axis=0, tiled=True)]
    all_to_all x3 -> x8, starting transfers between devices: 15.5 us -> 32.9 us  [exchanged(): return lax.all_to_all(tiles, TOK, split_axis=0, concat_axis=0, tiled=True)]
    unnamed x30 -> x12, local copies, waits for them, and re-layouts: 8.59 us -> 2.06 us
    pallas_call x14 -> x19, Pallas kernels: 29.8 us -> 30.7 us  [the longest x4 10.6 us: apply_fast(): pl.pallas_call(functools.partial(apply_kernel, (wave_step, 0, block), off...]
  transfers between devices with their start and end apart: 4 -> 9, of which waited for: 3 -> 9; matrix products, arithmetic and copies ran while one was open for 0% -> 1% of each run, Pallas kernels for 7% -> 10%
where the time goes in v2:
time: 152 us; the launch traced here: 151 us
  waiting for transfers between devices  68 us (45%)
  starting transfers between devices  34.8 us (23%)
  Pallas kernels  30.7 us (20%)
  blocking collectives  13.8 us (9%)
  local copies, waits for them, and re-layouts  2.81 us (2%)
    all_to_all x8, waiting for transfers between devices, exchanged(): return lax.all_to_all(tiles, TOK, split_axis=0, concat_axis=0, tiled=True)  64.5 us
    all_to_all x8, starting transfers between devices, exchanged(): return lax.all_to_all(tiles, TOK, split_axis=0, concat_axis=0, tiled=True)  32.9 us
    all_to_all x1, blocking collectives, exchanged(): return lax.all_to_all(tiles, TOK, split_axis=0, concat_axis=0, tiled=True)  13.8 us
    pallas_call x4, Pallas kernels, apply_fast(): pl.pallas_call(functools.partial(apply_kernel, (wave_step, 0, block), off...  10.6 us
    pallas_call x4, Pallas kernels, grads(): pl.pallas_call(functools.partial(grads_kernel, index, 256, offset), in_sp...  8.51 us
    pallas_call x5, Pallas kernels, stage(): pl.pallas_call(functools.partial(stage_kernel, place, len(arrays)), in_sp...  6.32 us
    pallas_call x4, Pallas kernels, update(): pl.pallas_call(functools.partial(update_kernel, index, int(token is not N...  3.57 us
    ppermute x1, waiting for transfers between devices, passed_on(): return lax.ppermute(array, 'seg', [(i, i + 1) for i in range(length - 1)])  3.47 us
  transfers between devices with their start and end apart: 9, of which 9 were waited for; matrix products, arithmetic and copies ran while one was open for 1% of the time, Pallas kernels for 10%

profile of v2, /device:TPU:96, one launch (start us, length us, event | category | flops | bytes accessed | tf_op | source)
XLA Modules:
  0.0 151.0 jit_solution(3364442896611466116)
XLA Ops:
  2.2 7.0 %all-to-all-start = ((bf16[16,48,256]{2,1,0:T(8,128)(2,1)}), bf16[16,48,256]{2,1,0:T(8,128)(2,1)S(1)}, u32[]{:S(2)}, u32[]{:S(2)}) async-start(bf16[16,48,256]{2,1,0:T(8,128)(2,1)} %get-tuple-element.38), calls=%async_computation | async-start | bytes 786432 | tf_op jit(solution)/shard_map/all_to_all | solution.py:316
  11.3 7.7 %all-to-all-done.gathered_ref = bf16[16,48,256]{2,1,0:T(8,128)(2,1)S(1)} async-done(((bf16[16,48,256]{2,1,0:T(8,128)(2,1)}), bf16[16,48,256]{2,1,0:T(8,128)(2,1)S(1)}, u32[]{:S(2)}, u32[]{:S(2)}) %all-to-all-start) | async-done | bytes 393248 | tf_op jit(solution)/shard_map/all_to_all | solution.py:316
  20.6 13.8 %all_to_all.45.refs_0_ = bf16[16,64,256]{2,1,0:T(8,128)(2,1)S(1)} all-to-all(bf16[16,64,256]{2,1,0:T(8,128)(2,1)S(1)} %grads.4), channel_id=1, replica_groups=mesh['seg'=16,'tok_0'=4,'tok_1'=4] {'tok_0','tok_1'}, dimensions={0} | all-to-all | bytes 1048576 | tf_op jit(solution)/shard_map/all_to_all | solution.py:316
  35.3 3.6 %all-to-all-start.2 = ((bf16[16,48,256]{2,1,0:T(8,128)(2,1)}), bf16[16,48,256]{2,1,0:T(8,128)(2,1)S(1)}, u32[]{:S(2)}, u32[]{:S(2)}) async-start(bf16[16,48,256]{2,1,0:T(8,128)(2,1)} %get-tuple-element.42), calls=%async_computation.2 | async-start | bytes 786432 | tf_op jit(solution)/shard_map/all_to_all | solution.py:316
  40.2 7.8 %all-to-all-done.2.gathered_ref = bf16[16,48,256]{2,1,0:T(8,128)(2,1)S(1)} async-done(((bf16[16,48,256]{2,1,0:T(8,128)(2,1)}), bf16[16,48,256]{2,1,0:T(8,128)(2,1)S(1)}, u32[]{:S(2)}, u32[]{:S(2)}) %all-to-all-start.2) | async-done | bytes 393248 | tf_op jit(solution)/shard_map/all_to_all | solution.py:316
  48.0 2.3 %grads.5 = bf16[16,48,256]{2,1,0:T(8,128)(2,1)} custom-call(bf16[16,48,256]{2,1,0:T(8,128)(2,1)S(1)} %all-to-all-done.2.gathered_ref, f32[4,1280]{1,0:T(4,128)S(1)} %reshape.35.rate_ref, bf16[1280,256]{1,0:T(8,128)(2,1)S(1)} %get-tuple-element.44.key_rows, bf16[1280,256]{1,0:T(8,128)(2,1)S(1)} %get-tuple-element.45.value_rows), custom_call_target="tpu_custom_call" | custom-call | flops 1006632960 | bytes 1310720 | tf_op jit(solution)/shard_map/grads/pallas_call | solution.py:154
  50.3 3.9 %all-to-all-start.3 = ((bf16[16,48,256]{2,1,0:T(8,128)(2,1)}), bf16[16,48,256]{2,1,0:T(8,128)(2,1)S(1)}, u32[]{:S(2)}, u32[]{:S(2)}) async-start(bf16[16,48,256]{2,1,0:T(8,128)(2,1)} %grads.5), calls=%async_computation.3 | async-start | bytes 786432 | tf_op jit(solution)/shard_map/all_to_all | solution.py:316
  54.2 2.8 %apply.4 = (bf16[2,1,2,1280,256]{4,3,2,1,0:T(8,128)(2,1)}, f32[8,128]{1,0:T(8,128)S(1)}) custom-call(bf16[16,48,256]{2,1,0:T(8,128)(2,1)S(1)} %all-to-all-done.2.gathered_ref, bf16[2,1,2,1280,256]{4,3,2,1,0:T(8,128)(2,1)} %refs_1_.9), custom_call_target="tpu_custom_call" | custom-call | flops 503316480 | bytes 1310720 | tf_op jit(solution)/shard_map/apply/pallas_call | solution.py:296
  57.0 6.4 %all-to-all-done.3.refs_0_ = bf16[16,48,256]{2,1,0:T(8,128)(2,1)S(1)} async-done(((bf16[16,48,256]{2,1,0:T(8,128)(2,1)}), bf16[16,48,256]{2,1,0:T(8,128)(2,1)S(1)}, u32[]{:S(2)}, u32[]{:S(2)}) %all-to-all-start.3) | async-done | bytes 393248 | tf_op jit(solution)/shard_map/all_to_all | solution.py:316
  66.0 3.5 %collective-permute-done.passed_ref = bf16[96,256]{1,0:T(8,128)(2,1)S(1)} collective-permute-done((bf16[96,256]{1,0:T(8,128)(2,1)S(1)}, bf16[96,256]{1,0:T(8,128)(2,1)S(1)}, u32[]{:S(2)}, u32[]{:S(2)}) %collective-permute-start) | collective-permute-done | bytes 49184 | tf_op jit(solution)/shard_map/ppermute | solution.py:321
  70.5 3.7 %all-to-all-start.4 = ((bf16[16,96,256]{2,1,0:T(8,128)(2,1)}), bf16[16,96,256]{2,1,0:T(8,128)(2,1)S(1)}, u32[]{:S(2)}, u32[]{:S(2)}) async-start(bf16[16,96,256]{2,1,0:T(8,128)(2,1)} %get-tuple-element.51), calls=%async_computation.4 | async-start | bytes 1572864 | tf_op jit(solution)/shard_map/all_to_all | solution.py:316
  75.5 14.7 %all-to-all-done.4.gathered_ref = bf16[16,96,256]{2,1,0:T(8,128)(2,1)S(1)} async-done(((bf16[16,96,256]{2,1,0:T(8,128)(2,1)}), bf16[16,96,256]{2,1,0:T(8,128)(2,1)S(1)}, u32[]{:S(2)}, u32[]{:S(2)}) %all-to-all-start.4) | async-done | bytes 786464 | tf_op jit(solution)/shard_map/all_to_all | solution.py:316
  90.2 2.3 %grads.6 = bf16[16,48,256]{2,1,0:T(8,128)(2,1)} custom-call(bf16[16,96,256]{2,1,0:T(8,128)(2,1)S(1)} %all-to-all-done.4.gathered_ref, f32[4,1280]{1,0:T(4,128)S(1)} %reshape.35.rate_ref, bf16[1280,256]{1,0:T(8,128)(2,1)S(1)} %get-tuple-element.53.key_rows, bf16[1280,256]{1,0:T(8,128)(2,1)S(1)} %get-tuple-element.54.value_rows), custom_call_target="tpu_custom_call" | custom-call | flops 1006632960 | bytes 1310720 | tf_op jit(solution)/shard_map/grads/pallas_call | solution.py:154
  92.6 3.6 %all-to-all-start.5 = ((bf16[16,48,256]{2,1,0:T(8,128)(2,1)}), bf16[16,48,256]{2,1,0:T(8,128)(2,1)S(1)}, u32[]{:S(2)}, u32[]{:S(2)}) async-start(bf16[16,48,256]{2,1,0:T(8,128)(2,1)} %grads.6), calls=%async_computation.5 | async-start | bytes 786432 | tf_op jit(solution)/shard_map/all_to_all | solution.py:316
  96.1 2.8 %apply.5 = (bf16[2,1,2,1280,256]{4,3,2,1,0:T(8,128)(2,1)}, f32[8,128]{1,0:T(8,128)S(1)}) custom-call(bf16[16,96,256]{2,1,0:T(8,128)(2,1)S(1)} %all-to-all-done.4.gathered_ref, bf16[2,1,2,1280,256]{4,3,2,1,0:T(8,128)(2,1)} %refs_1_.9, bf16[2,1,2,1280,256]{4,3,2,1,0:T(8,128)(2,1)} %get-tuple-element.57.refs_0_), custom_call_target="tpu_custom_call", output_to_operand_aliasing={{0}: (2, {})} | custom-call | flops 503316480 | bytes 1310720 | tf_op jit(solution)/shard_map/apply/pallas_call | solution.py:296
  98.9 7.0 %all-to-all-done.5.refs_0_ = bf16[16,48,256]{2,1,0:T(8,128)(2,1)S(1)} async-done(((bf16[16,48,256]{2,1,0:T(8,128)(2,1)}), bf16[16,48,256]{2,1,0:T(8,128)(2,1)S(1)}, u32[]{:S(2)}, u32[]{:S(2)}) %all-to-all-start.5) | async-done | bytes 393248 | tf_op jit(solution)/shard_map/all_to_all | solution.py:316
  106.9 3.7 %all-to-all-start.6 = ((bf16[16,48,256]{2,1,0:T(8,128)(2,1)}), bf16[16,48,256]{2,1,0:T(8,128)(2,1)S(1)}, u32[]{:S(2)}, u32[]{:S(2)}) async-start(bf16[16,48,256]{2,1,0:T(8,128)(2,1)} %get-tuple-element.59), calls=%async_computation.6 | async-start | bytes 786432 | tf_op jit(solution)/shard_map/all_to_all | solution.py:316
  111.9 7.8 %all-to-all-done.6.gathered_ref = bf16[16,48,256]{2,1,0:T(8,128)(2,1)S(1)} async-done(((bf16[16,48,256]{2,1,0:T(8,128)(2,1)}), bf16[16,48,256]{2,1,0:T(8,128)(2,1)S(1)}, u32[]{:S(2)}, u32[]{:S(2)}) %all-to-all-start.6) | async-done | bytes 393248 | tf_op jit(solution)/shard_map/all_to_all | solution.py:316
  119.8 2.3 %grads.7 = bf16[16,48,256]{2,1,0:T(8,128)(2,1)} custom-call(bf16[16,48,256]{2,1,0:T(8,128)(2,1)S(1)} %all-to-all-done.6.gathered_ref, f32[4,1280]{1,0:T(4,128)S(1)} %reshape.35.rate_ref, bf16[1280,256]{1,0:T(8,128)(2,1)S(1)} %get-tuple-element.61.key_rows, bf16[1280,256]{1,0:T(8,128)(2,1)S(1)} %get-tuple-element.62.value_rows), custom_call_target="tpu_custom_call" | custom-call | flops 1006632960 | bytes 1310720 | tf_op jit(solution)/shard_map/grads/pallas_call | solution.py:154
  122.1 3.7 %all-to-all-start.7 = ((bf16[16,48,256]{2,1,0:T(8,128)(2,1)}), bf16[16,48,256]{2,1,0:T(8,128)(2,1)S(1)}, u32[]{:S(2)}, u32[]{:S(2)}) async-start(bf16[16,48,256]{2,1,0:T(8,128)(2,1)} %grads.7), calls=%async_computation.7 | async-start | bytes 786432 | tf_op jit(solution)/shard_map/all_to_all | solution.py:316
  125.8 2.8 %apply.6 = (bf16[2,1,2,1280,256]{4,3,2,1,0:T(8,128)(2,1)}, f32[8,128]{1,0:T(8,128)S(1)}) custom-call(bf16[16,48,256]{2,1,0:T(8,128)(2,1)S(1)} %all-to-all-done.6.gathered_ref, bf16[2,1,2,1280,256]{4,3,2,1,0:T(8,128)(2,1)} %refs_1_.9, bf16[2,1,2,1280,256]{4,3,2,1,0:T(8,128)(2,1)} %get-tuple-element.65.refs_0_), custom_call_target="tpu_custom_call", output_to_operand_aliasing={{0}: (2, {})} | custom-call | flops 503316480 | bytes 1310720 | tf_op jit(solution)/shard_map/apply/pallas_call | solution.py:296
  128.6 6.3 %all-to-all-done.7.refs_0_ = bf16[16,48,256]{2,1,0:T(8,128)(2,1)S(1)} async-done(((bf16[16,48,256]{2,1,0:T(8,128)(2,1)}), bf16[16,48,256]{2,1,0:T(8,128)(2,1)S(1)}, u32[]{:S(2)}, u32[]{:S(2)}) %all-to-all-start.7) | async-done | bytes 393248 | tf_op jit(solution)/shard_map/all_to_all | solution.py:316
  135.9 3.7 %all-to-all-start.8 = ((bf16[16,48,256]{2,1,0:T(8,128)(2,1)}), bf16[16,48,256]{2,1,0:T(8,128)(2,1)S(1)}, u32[]{:S(2)}, u32[]{:S(2)}) async-start(bf16[16,48,256]{2,1,0:T(8,128)(2,1)} %get-tuple-element.67), calls=%async_computation.8 | async-start | bytes 786432 | tf_op jit(solution)/shard_map/all_to_all | solution.py:316
  141.9 6.8 %all-to-all-done.8.gathered_ref = bf16[16,48,256]{2,1,0:T(8,128)(2,1)S(1)} async-done(((bf16[16,48,256]{2,1,0:T(8,128)(2,1)}), bf16[16,48,256]{2,1,0:T(8,128)(2,1)S(1)}, u32[]{:S(2)}, u32[]{:S(2)}) %all-to-all-start.8) | async-done | bytes 393248 | tf_op jit(solution)/shard_map/all_to_all | solution.py:316
  (27 shorter events, 20.1 us)
Async XLA Ops:
  0.6 0.8 copy-start
  2.2 16.9 %all-to-all-start = ((bf16[16,48,256]{2,1,0:T(8,128)(2,1)}), bf16[16,48,256]{2,1,0:T(8,128)(2,1)S(1)}, u32[]{:S(2)}, u32[]{:S(2)}) async-start(bf16[16,48,256]{2,1,0:T(8,128)(2,1)} %get-tuple-element.38), calls=%async_computation | async-start | bytes 786432 | tf_op jit(solution)/shard_map/all_to_all | solution.py:316
  11.3 23.1 %copy-start.1 = (f32[1,3,256,16]{2,3,1,0:T(8,128)S(1)}, f32[1,3,256,16]{2,3,1,0:T(8,128)}, u32[]{:S(2)}) copy-start(f32[1,3,256,16]{2,3,1,0:T(8,128)} %param.12) | copy-start | bytes 147460
  11.3 23.1 %copy-start.2 = (f32[1,3,256,16]{2,3,1,0:T(8,128)S(1)}, f32[1,3,256,16]{2,3,1,0:T(8,128)}, u32[]{:S(2)}) copy-start(f32[1,3,256,16]{2,3,1,0:T(8,128)} %param.13) | copy-start | bytes 147460
  35.3 12.6 %all-to-all-start.2 = ((bf16[16,48,256]{2,1,0:T(8,128)(2,1)}), bf16[16,48,256]{2,1,0:T(8,128)(2,1)S(1)}, u32[]{:S(2)}, u32[]{:S(2)}) async-start(bf16[16,48,256]{2,1,0:T(8,128)(2,1)} %get-tuple-element.42), calls=%async_computation.2 | async-start | bytes 786432 | tf_op jit(solution)/shard_map/all_to_all | solution.py:316
  50.3 19.2 %copy-start.3 = (f32[3,256,16]{1,2,0:T(8,128)S(1)}, f32[3,256,16]{1,2,0:T(8,128)}, u32[]{:S(2)}) copy-start(f32[3,256,16]{1,2,0:T(8,128)} %param.14) | copy-start | bytes 147460
  50.3 19.2 %copy-start.4 = (f32[3,256,16]{1,2,0:T(8,128)S(1)}, f32[3,256,16]{1,2,0:T(8,128)}, u32[]{:S(2)}) copy-start(f32[3,256,16]{1,2,0:T(8,128)} %param.15) | copy-start | bytes 147460
  50.3 13.0 %all-to-all-start.3 = ((bf16[16,48,256]{2,1,0:T(8,128)(2,1)}), bf16[16,48,256]{2,1,0:T(8,128)(2,1)S(1)}, u32[]{:S(2)}, u32[]{:S(2)}) async-start(bf16[16,48,256]{2,1,0:T(8,128)(2,1)} %grads.5), calls=%async_computation.3 | async-start | bytes 786432 | tf_op jit(solution)/shard_map/all_to_all | solution.py:316
  64.1 5.4 %collective-permute-start = (bf16[96,256]{1,0:T(8,128)(2,1)S(1)}, bf16[96,256]{1,0:T(8,128)(2,1)S(1)}, u32[]{:S(2)}, u32[]{:S(2)}) collective-permute-start(bf16[96,256]{1,0:T(8,128)(2,1)S(1)} %get-tuple-element.50.own_ref), channel_id=1, source_target_pairs={{0,16},{16,32},{32,48},{48,64},{64,80},{80,96},{96,112},{112,128},... | collective-permute-start | bytes 147464 | tf_op jit(solution)/shard_map/ppermute | solution.py:321
  70.5 19.8 %all-to-all-start.4 = ((bf16[16,96,256]{2,1,0:T(8,128)(2,1)}), bf16[16,96,256]{2,1,0:T(8,128)(2,1)S(1)}, u32[]{:S(2)}, u32[]{:S(2)}) async-start(bf16[16,96,256]{2,1,0:T(8,128)(2,1)} %get-tuple-element.51), calls=%async_computation.4 | async-start | bytes 1572864 | tf_op jit(solution)/shard_map/all_to_all | solution.py:316
  92.6 13.4 %all-to-all-start.5 = ((bf16[16,48,256]{2,1,0:T(8,128)(2,1)}), bf16[16,48,256]{2,1,0:T(8,128)(2,1)S(1)}, u32[]{:S(2)}, u32[]{:S(2)}) async-start(bf16[16,48,256]{2,1,0:T(8,128)(2,1)} %grads.6), calls=%async_computation.5 | async-start | bytes 786432 | tf_op jit(solution)/shard_map/all_to_all | solution.py:316
  106.9 12.9 %all-to-all-start.6 = ((bf16[16,48,256]{2,1,0:T(8,128)(2,1)}), bf16[16,48,256]{2,1,0:T(8,128)(2,1)S(1)}, u32[]{:S(2)}, u32[]{:S(2)}) async-start(bf16[16,48,256]{2,1,0:T(8,128)(2,1)} %get-tuple-element.59), calls=%async_computation.6 | async-start | bytes 786432 | tf_op jit(solution)/shard_map/all_to_all | solution.py:316
  122.1 12.9 %all-to-all-start.7 = ((bf16[16,48,256]{2,1,0:T(8,128)(2,1)}), bf16[16,48,256]{2,1,0:T(8,128)(2,1)S(1)}, u32[]{:S(2)}, u32[]{:S(2)}) async-start(bf16[16,48,256]{2,1,0:T(8,128)(2,1)} %grads.7), calls=%async_computation.7 | async-start | bytes 786432 | tf_op jit(solution)/shard_map/all_to_all | solution.py:316
  135.9 12.9 %all-to-all-start.8 = ((bf16[16,48,256]{2,1,0:T(8,128)(2,1)}), bf16[16,48,256]{2,1,0:T(8,128)(2,1)S(1)}, u32[]{:S(2)}, u32[]{:S(2)}) async-start(bf16[16,48,256]{2,1,0:T(8,128)(2,1)} %get-tuple-element.67), calls=%async_computation.8 | async-start | bytes 786432 | tf_op jit(solution)/shard_map/all_to_all | solution.py:316

commit v3 on v2

v3 whole, which is shorter than its diff:
```python
import functools

import jax
import jax.numpy as jnp
from jax import lax
from jax.experimental import pallas as pl
from jax.experimental.pallas import tpu as pltpu
from jax.sharding import Mesh
from jax.sharding import PartitionSpec as P

TOK = ("tok_0", "tok_1")

momentum_decay = 0.9
learn_rate = 0.05
epsilon = 1e-06

f32, bf16 = jnp.float32, jnp.bfloat16
VMEM_LIMIT = 16 * 1024 * 1024

NN = (((1,), (0,)), ((), ()))
NT = (((1,), (1,)), ((), ()))


def dot(a, b, dims):
    return lax.dot_general(a, b, dims, preferred_element_type=f32)


def sigmoid(a):
    return 0.5 * jnp.tanh(0.5 * a) + 0.5


def matrix(gathered_ref, index, share):
    tiles = gathered_ref[:, index * share : (index + 1) * share, :]
    return tiles.reshape(-1, tiles.shape[-1])


def params(**more):
    return pltpu.CompilerParams(vmem_limit_bytes=VMEM_LIMIT, **more)


def in_vmem(*shape, dtype=f32):
    return pltpu.VMEM(shape, dtype)


VMEM = pl.BlockSpec(memory_space=pltpu.VMEM)
HBM = pl.BlockSpec(memory_space=pltpu.HBM)
SMEM = pl.BlockSpec(memory_space=pltpu.SMEM)


TOKEN = jax.ShapeDtypeStruct((8, 128), f32)


def in_hbm(array):
    return pltpu.with_memory_space_constraint(array, pltpu.HBM)


def started(sources, targets, places, sems):
    copies = [
        pltpu.make_async_copy(source.at[*place], target, sems.at[index])
        for index, (source, target, place) in enumerate(zip(sources, targets, places))
    ]
    for copy in copies:
        copy.start()
    return copies


def rows_in_vmem(array):
    return in_vmem(*array.shape[3:], dtype=array.dtype)


def stage_kernel(places, *refs):
    count = len(places)
    token_ref, sems = refs[-2:]
    copies = started(refs[1 : 1 + count], refs[1 + count : 1 + 2 * count], places, sems)
    token_ref[...] = jnp.zeros_like(token_ref)
    for copy in copies:
        copy.wait()


def stage(token, place, *arrays):
    count = len(arrays)
    return pl.pallas_call(
        functools.partial(stage_kernel, [place] * count),
        in_specs=[VMEM] + [HBM] * count,
        out_specs=[VMEM] * (count + 1),
        out_shape=[rows_in_vmem(array) for array in arrays] + [TOKEN],
        scratch_shapes=[pltpu.SemaphoreType.DMA((count,))],
        compiler_params=params(),
        cost_estimate=pl.CostEstimate(
            flops=0, bytes_accessed=count * arrays[0].size, transcendentals=0
        ),
        name="stage",
    )(token, *(in_hbm(array) for array in arrays))


def begin_kernel(place, weights_ref, key_ref, value_ref, message_ref, key_rows, value_rows, token_ref, sems):
    copies = started((key_ref, value_ref), (key_rows, value_rows), [place] * 2, sems)
    message_ref[...] = jnp.broadcast_to(weights_ref[...].astype(bf16)[None], message_ref.shape)
    token_ref[...] = jnp.zeros_like(token_ref)
    for copy in copies:
        copy.wait()


def begin(weights, place, keys, values, parties):
    rows, width = weights.shape
    return pl.pallas_call(
        functools.partial(begin_kernel, place),
        in_specs=[VMEM, HBM, HBM],
        out_specs=[VMEM] * 4,
        out_shape=[
            in_vmem(parties, rows, width, dtype=bf16),
            rows_in_vmem(keys),
            rows_in_vmem(values),
            TOKEN,
        ],
        scratch_shapes=[pltpu.SemaphoreType.DMA((2,))],
        compiler_params=params(),
        name="begin",
    )(weights, in_hbm(keys), in_hbm(values))


def grads_kernel(
    place, tile, gathered_ref, rate_ref, key_rows, value_rows, message_ref, token_ref, left_ref, back_ref
):
    parties, rows, width = message_ref.shape
    share = width // parties
    count = key_rows.shape[0]
    section, block = place
    token_ref[...] = jnp.zeros_like(token_ref)
    left_ref[...] = matrix(gathered_ref, 1, share).astype(f32).T.astype(bf16)
    gate, up = matrix(gathered_ref, 0, share), matrix(gathered_ref, 2, share)
    for start in range(0, count, tile):
        span = slice(start, start + tile)
        keys, values = key_rows[span, :], value_rows[span, :]
        rate = rate_ref[section, 0, block : block + 1, span]
        pre_gate = dot(gate, keys, NT)
        pre_up = dot(up, keys, NT)
        back = dot(left_ref[...], values, NT) * -rate
        sig = sigmoid(pre_gate)
        active = pre_gate * sig
        slope = sig + active * (1.0 - sig)
        back_ref[0, :, span] = (back * pre_up * slope).astype(bf16)
        back_ref[1, :, span] = (active * pre_up * rate).astype(bf16)
        back_ref[2, :, span] = (back * active).astype(bf16)
    keys, values = key_rows[...], value_rows[...]
    gradients = (
        dot(back_ref[0], keys, NN),
        -dot(back_ref[1], values, NN).T,
        dot(back_ref[2], keys, NN),
    )
    for index, gradient in enumerate(gradients):
        message_ref[:, index * share : (index + 1) * share, :] = gradient.astype(bf16).reshape(
            parties, share, width
        )
    if rows > 3 * share:
        row = lax.broadcasted_iota(jnp.int32, (share, width), 0)
        extra = jnp.zeros((share, width), f32)
        blocks = rate_ref.shape[2]
        for index in range(rate_ref.shape[0] * blocks):
            each = index % blocks
            rates = rate_ref[index // blocks, 0, each : each + 1, :]
            square = jnp.sum(rates * rates, axis=1, keepdims=True)
            high = square.astype(bf16).astype(f32)
            extra = jnp.where(row == 2 * index, high, extra)
            extra = jnp.where(row == 2 * index + 1, square - high, extra)
        message_ref[:, 3 * share :, :] = jnp.broadcast_to(
            extra.astype(bf16)[None], (parties, share, width)
        )


def grads(gathered, rates, keys, values, place):
    parties, _, width = gathered.shape
    share = width // parties
    count = keys.shape[0]
    rows = (4 if place == (0, 0) else 3) * share
    return pl.pallas_call(
        functools.partial(grads_kernel, place, 256),
        in_specs=[VMEM] * 4,
        out_specs=[VMEM] * 2,
        out_shape=[in_vmem(parties, rows, width, dtype=bf16), TOKEN],
        scratch_shapes=[pltpu.VMEM((width, width), bf16), pltpu.VMEM((3, width, count), bf16)],
        compiler_params=params(),
        cost_estimate=pl.CostEstimate(
            flops=12 * count * width * width, bytes_accessed=4 * count * width, transcendentals=0
        ),
        name="grads",
    )(gathered, rates, keys, values)


def update_kernel(index, *refs):
    arrived_ref, weights_ref, moment_ref = refs[:3]
    refs = refs[3:]
    rows = weights_ref.shape[0]
    gradients = jnp.sum(arrived_ref[:, :rows, :].astype(f32), axis=0)
    if index == 0:
        squares = jnp.sum(arrived_ref[:, rows:, :].astype(f32), axis=0)
        refs[-1][...] = squares
    else:
        squares, refs = refs[0][...], refs[1:]
    square = squares[2 * index : 2 * index + 1, :] + squares[2 * index + 1 : 2 * index + 2, :]
    weights = weights_ref[...]
    moment = momentum_decay * moment_ref[...] + gradients * lax.rsqrt(square)
    stepped = weights - learn_rate * moment
    rescale = jnp.sqrt(
        jnp.sum(weights * weights, axis=1, keepdims=True)
        / (jnp.sum(stepped * stepped, axis=1, keepdims=True) + epsilon)
    )
    weights = stepped * rescale
    rounded = weights.astype(bf16)
    message_ref = refs[1]
    if len(message_ref.shape) == 3:
        message_ref[...] = jnp.broadcast_to(rounded[None], message_ref.shape)
        refs[2][...] = weights
        refs[3][...] = moment
    else:
        message_ref[:rows, :] = rounded
        message_ref[rows:, :] = moment.astype(bf16)


def update(index, arrived, weights, moment, squares, token, leaving):
    rows, width = weights.shape
    given, in_specs = [arrived, weights, moment], [VMEM] * 3
    if index > 0:
        given.append(squares)
        in_specs.append(VMEM)
    given.append(token)
    in_specs.append(VMEM)
    if leaving:
        out_shape = [in_vmem(2 * rows, width, dtype=bf16)]
    else:
        out_shape = [in_vmem(arrived.shape[0], rows, width, dtype=bf16)]
        out_shape += [in_vmem(rows, width)] * 2
    if index == 0:
        out_shape.append(in_vmem(arrived.shape[1] - rows, width))
    return pl.pallas_call(
        functools.partial(update_kernel, index),
        in_specs=in_specs,
        out_specs=[VMEM] * len(out_shape),
        out_shape=out_shape,
        compiler_params=params(),
        name="update",
    )(*given)


def enter_kernel(
    first_ref, passed_ref, own_ref, fresh_weights_ref, fresh_moment_ref, weights_ref, moment_ref, message_ref
):
    rows = weights_ref.shape[0]
    first = first_ref[0] == 1
    passed = passed_ref[...].astype(f32)
    weights = jnp.where(first, fresh_weights_ref[...], passed[:rows])
    weights_ref[...] = weights
    moment_ref[...] = jnp.where(first, fresh_moment_ref[...], passed[rows:])
    shape = (message_ref.shape[0], *weights.shape)
    message_ref[:, :rows, :] = jnp.broadcast_to(weights.astype(bf16)[None], shape)
    message_ref[:, rows:, :] = jnp.broadcast_to(own_ref[:rows, :][None], shape)


def enter(first, passed, own, fresh_weights, fresh_moment, parties):
    rows, width = fresh_weights.shape
    return pl.pallas_call(
        enter_kernel,
        in_specs=[SMEM] + [VMEM] * 4,
        out_specs=[VMEM] * 3,
        out_shape=[
            in_vmem(rows, width),
            in_vmem(rows, width),
            in_vmem(parties, 2 * rows, width, dtype=bf16),
        ],
        compiler_params=params(),
        name="enter",
    )(first, passed, own, fresh_weights, fresh_moment)


def apply_kernel(place, base, ahead, staged, aliased, gathered_ref, query_ref, *refs):
    count = len(ahead)
    sources, refs = refs[:count], refs[count + aliased :]
    out_ref, token_ref, targets = refs[0], refs[1], refs[2 : 2 + count]
    query_rows, held_ref, sems = refs[2 + count :]
    token_ref[...] = jnp.zeros_like(token_ref)
    share = query_rows.shape[-1] // gathered_ref.shape[0]
    copies = []
    if not staged:
        copies += started([query_ref], [query_rows], [place], sems)
    copies += started(sources, targets, ahead, sems.at[pl.ds(2, max(count, 1))])
    if staged:
        queries = query_ref[...]
    else:
        copies.pop(0).wait()
        queries = query_rows[...]
    pre_gate = dot(queries, matrix(gathered_ref, base + 0, share), NT)
    pre_up = dot(queries, matrix(gathered_ref, base + 2, share), NT)
    hidden = (pre_gate * sigmoid(pre_gate) * pre_up).astype(bf16)
    held_ref[...] = dot(hidden, matrix(gathered_ref, base + 1, share), NT).astype(bf16)
    copies.append(pltpu.make_async_copy(held_ref, out_ref.at[*place], sems.at[1]))
    copies[-1].start()
    for copy in copies:
        copy.wait()


def apply_fast(gathered, base, queries, place, results, shape, ahead=()):
    count, width = shape[3:]
    staged = len(queries.shape) == 2
    given = [gathered, queries if staged else in_hbm(queries)]
    given += [in_hbm(array) for array, _ in ahead]
    in_specs = [VMEM, VMEM if staged else HBM] + [HBM] * len(ahead)
    if results is not None:
        given.append(results)
        in_specs.append(HBM)
    return pl.pallas_call(
        functools.partial(
            apply_kernel, place, base, [where for _, where in ahead], staged, int(results is not None)
        ),
        in_specs=in_specs,
        out_specs=[HBM] + [VMEM] * (1 + len(ahead)),
        out_shape=[jax.ShapeDtypeStruct(shape, bf16), TOKEN]
        + [rows_in_vmem(array) for array, _ in ahead],
        input_output_aliases={} if results is None else {len(given) - 1: 0},
        scratch_shapes=[
            pltpu.VMEM((count, width), bf16),
            pltpu.VMEM((count, width), bf16),
            pltpu.SemaphoreType.DMA((2 + max(len(ahead), 1),)),
        ],
        compiler_params=params(),
        cost_estimate=pl.CostEstimate(
            flops=6 * count * width * width, bytes_accessed=4 * count * width, transcendentals=0
        ),
        name="apply",
    )(*given)


def exchanged(tiles):
    return lax.all_to_all(tiles, TOK, split_axis=0, concat_axis=0, tiled=True)


def passed_on(array):
    length = lax.axis_size("seg")
    return lax.ppermute(array, "seg", [(i, i + 1) for i in range(length - 1)])


def columns_first(state):
    return jnp.swapaxes(state, 1, 2).reshape(-1, state.shape[1])


def rows_first(state, share):
    return jnp.swapaxes(state.reshape(-1, share, state.shape[1]), 1, 2)


def body(
    queries, key_vectors, values, token_rates, fast_weights, momenta, fresh_weights, fresh_momenta
):
    sections, _, blocks, count, _ = queries.shape
    parties = lax.axis_size(TOK)
    share = fast_weights.shape[3]
    first = (lax.axis_index("seg") == 0).astype(jnp.int32).reshape(1)
    weights, moment = columns_first(fast_weights[0]), columns_first(momenta[0])
    fresh_weights, fresh_moment = columns_first(fresh_weights), columns_first(fresh_momenta)
    shape = queries.shape
    places = [(section, 0, block) for section in range(sections) for block in range(blocks)]
    message, *staged, _ = begin(weights, places[0], key_vectors, values, parties)
    gathered, base = exchanged(message), 0
    results = squares = None
    for index, place in enumerate(places):
        last = index == len(places) - 1
        leaving = not last and place[2] == blocks - 1
        message, token = grads(gathered, token_rates, *staged, (place[0], place[2]))
        arrived = exchanged(message)
        if last:
            ahead = ((queries, place),)
        else:
            ahead = ((key_vectors, places[index + 1]), (values, places[index + 1]))
        if index == 0:
            *staged, token = stage(token, ahead[0][1], *(array for array, _ in ahead))
        else:
            results, token, *staged = apply_fast(
                gathered, base, queries, places[index - 1], results, shape, ahead
            )
        message, *state = update(index, arrived, weights, moment, squares, token, leaving)
        base = 0
        if leaving:
            weights, moment, message = enter(
                first, passed_on(message), message, fresh_weights, fresh_moment, parties
            )
            base = 3
        else:
            weights, moment, squares = (*state, squares)[:3]
        gathered = exchanged(message)
    results, *_ = apply_fast(gathered, base, staged[0], places[-1], results, shape)
    return (results, rows_first(weights, share)[None], rows_first(moment, share)[None])


def solution(mesh):
    finer = Mesh(mesh.devices.reshape(mesh.shape["seg"], 4, 4), ("seg", "tok_0", "tok_1"))
    placed = (
        P(None, "seg", None, TOK, None),
        P(None, "seg", None, TOK, None),
        P(None, "seg", None, TOK, None),
        P(None, "seg", None, TOK),
        P("seg", None, None, TOK),
        P("seg", None, None, TOK),
        P(None, None, TOK),
        P(None, None, TOK),
    )
    return jax.shard_map(
        body,
        mesh=finer,
        in_specs=placed,
        out_specs=(
            P(None, "seg", None, TOK, None),
            P("seg", None, None, TOK),
            P("seg", None, None, TOK),
        ),
        check_vma=False,
    )
```

time: 152 us -> 149 us (0.980)
  blocking collectives: 13.8 us -> 60.3 us
  waiting for transfers between devices: 68 us -> 39.6 us
  starting transfers between devices: 34.8 us -> 20.6 us
  Pallas kernels: 30.7 us -> 24.5 us
    all_to_all x1 -> x4, blocking collectives: 13.8 us -> 60.3 us  [exchanged(): return lax.all_to_all(tiles, TOK, split_axis=0, concat_axis=0, tiled=True)]
    all_to_all x8 -> x5, waiting for transfers between devices: 64.5 us -> 36.1 us  [exchanged(): return lax.all_to_all(tiles, TOK, split_axis=0, concat_axis=0, tiled=True)]
    all_to_all x8 -> x5, starting transfers between devices: 32.9 us -> 18.6 us  [exchanged(): return lax.all_to_all(tiles, TOK, split_axis=0, concat_axis=0, tiled=True)]
    pallas_call x18 -> x14, Pallas kernels: 29.8 us -> 24.4 us  [the longest x4 10.7 us: apply_fast(): pl.pallas_call(functools.partial(apply_kernel, place, base, [where for _,...]
  transfers between devices with their start and end apart: 9 -> 6, of which waited for: 9 -> 6; matrix products, arithmetic and copies ran while one was open for 1% -> 1% of each run, Pallas kernels for 10% -> 7%
where the time goes in v3:
time: 149 us; the launch traced here: 148 us
  blocking collectives  60.3 us (40%)
  waiting for transfers between devices  39.6 us (27%)
  Pallas kernels  24.5 us (16%)
  starting transfers between devices  20.6 us (14%)
  local copies, waits for them, and re-layouts  2.06 us (1%)
    all_to_all x4, blocking collectives, exchanged(): return lax.all_to_all(tiles, TOK, split_axis=0, concat_axis=0, tiled=True)  60.3 us
    all_to_all x5, waiting for transfers between devices, exchanged(): return lax.all_to_all(tiles, TOK, split_axis=0, concat_axis=0, tiled=True)  36.1 us
    all_to_all x5, starting transfers between devices, exchanged(): return lax.all_to_all(tiles, TOK, split_axis=0, concat_axis=0, tiled=True)  18.6 us
    pallas_call x4, Pallas kernels, apply_fast(): pl.pallas_call(functools.partial(apply_kernel, place, base, [where for _,...  10.7 us
    pallas_call x4, Pallas kernels, grads(): pl.pallas_call(functools.partial(grads_kernel, place, 256), in_specs=[VME...  9.04 us
    ppermute x1, waiting for transfers between devices, passed_on(): return lax.ppermute(array, 'seg', [(i, i + 1) for i in range(length - 1)])  3.47 us
  transfers between devices with their start and end apart: 6, of which 6 were waited for; matrix products, arithmetic and copies ran while one was open for 1% of the time, Pallas kernels for 7%

profile of v3, /device:TPU:96, one launch (start us, length us, event | category | flops | bytes accessed | tf_op | source)
XLA Modules:
  0.0 147.8 jit_solution(13300647106640042988)
XLA Ops:
  3.3 16.7 %all_to_all.45.gathered_ref = bf16[16,48,256]{2,1,0:T(8,128)(2,1)S(1)} all-to-all(bf16[16,48,256]{2,1,0:T(8,128)(2,1)S(1)} %get-tuple-element.39), channel_id=1, replica_groups=mesh['seg'=16,'tok_0'=4,'tok_1'=4] {'tok_0','tok_1'}, dimensions={0} | all-to-all | bytes 786432 | tf_op jit(solution)/shard_map/all_to_all | solution.py:333
  20.0 2.4 %grads.4 = (bf16[16,64,256]{2,1,0:T(8,128)(2,1)}, f32[8,128]{1,0:T(8,128)S(1)}) custom-call(bf16[16,48,256]{2,1,0:T(8,128)(2,1)S(1)} %all_to_all.45.gathered_ref, f32[2,1,2,1280]{3,2,1,0:T(2,128)S(1)} %copy-done.5, bf16[1280,256]{1,0:T(8,128)(2,1)S(1)} %get-tuple-element.40.key_rows, bf16[1280,256]{1,0:T(8,128)(2,1)S(1)} %get-tuple-element.41.value_rows), custom_call_target="tpu_custom_call" | custom-call | flops 1006632960 | bytes 1310720 | tf_op jit(solution)/shard_map/grads/pallas_call | solution.py:176
  22.4 3.7 %all-to-all-start.1 = ((bf16[16,64,256]{2,1,0:T(8,128)(2,1)}), bf16[16,64,256]{2,1,0:T(8,128)(2,1)S(1)}, u32[]{:S(2)}, u32[]{:S(2)}) async-start(bf16[16,64,256]{2,1,0:T(8,128)(2,1)} %get-tuple-element.42), calls=%async_computation.1 | async-start | bytes 1048576 | tf_op jit(solution)/shard_map/all_to_all | solution.py:333
  27.4 8.9 %all-to-all-done.1.refs_0_ = bf16[16,64,256]{2,1,0:T(8,128)(2,1)S(1)} async-done(((bf16[16,64,256]{2,1,0:T(8,128)(2,1)}), bf16[16,64,256]{2,1,0:T(8,128)(2,1)S(1)}, u32[]{:S(2)}, u32[]{:S(2)}) %all-to-all-start.1) | async-done | bytes 524320 | tf_op jit(solution)/shard_map/all_to_all | solution.py:333
  36.6 12.4 %all_to_all.46.gathered_ref = bf16[16,48,256]{2,1,0:T(8,128)(2,1)S(1)} all-to-all(bf16[16,48,256]{2,1,0:T(8,128)(2,1)S(1)} %get-tuple-element.45), channel_id=1, replica_groups=mesh['seg'=16,'tok_0'=4,'tok_1'=4] {'tok_0','tok_1'}, dimensions={0} | all-to-all | bytes 786432 | tf_op jit(solution)/shard_map/all_to_all | solution.py:333
  49.0 2.2 %grads.5 = (bf16[16,48,256]{2,1,0:T(8,128)(2,1)}, f32[8,128]{1,0:T(8,128)}) custom-call(bf16[16,48,256]{2,1,0:T(8,128)(2,1)S(1)} %all_to_all.46.gathered_ref, f32[2,1,2,1280]{3,2,1,0:T(2,128)S(1)} %copy-done.5, bf16[1280,256]{1,0:T(8,128)(2,1)S(1)} %get-tuple-element.46.key_rows, bf16[1280,256]{1,0:T(8,128)(2,1)S(1)} %get-tuple-element.47.value_rows), custom_call_target="tpu_custom_call" | custom-call | flops 1006632960 | bytes 1310720 | tf_op jit(solution)/shard_map/grads/pallas_call | solution.py:176
  51.2 3.7 %all-to-all-start.3 = ((bf16[16,48,256]{2,1,0:T(8,128)(2,1)}), bf16[16,48,256]{2,1,0:T(8,128)(2,1)S(1)}, u32[]{:S(2)}, u32[]{:S(2)}) async-start(bf16[16,48,256]{2,1,0:T(8,128)(2,1)} %get-tuple-element.48), calls=%async_computation.3 | async-start | bytes 786432 | tf_op jit(solution)/shard_map/all_to_all | solution.py:333
  54.9 2.8 %apply.4 = (bf16[2,1,2,1280,256]{4,3,2,1,0:T(8,128)(2,1)}, f32[8,128]{1,0:T(8,128)S(1)}, bf16[1280,256]{1,0:T(8,128)(2,1)S(1)}, bf16[1280,256]{1,0:T(8,128)(2,1)S(1)}) custom-call(bf16[16,48,256]{2,1,0:T(8,128)(2,1)S(1)} %all_to_all.46.gathered_ref, bf16[2,1,2,1280,256]{4,3,2,1,0:T(8,128)(2,1)} %refs_0_.5, bf16[2,1,2,1280,256]{4,3,2,1,0:T(8,128)(2,1)} %refs_0_.4, ...), custom_call_target="tpu_custom_call" | custom-call | flops 503316480 | bytes 1310720 | tf_op jit(solution)/shard_map/apply/pallas_call | solution.py:310
  57.8 6.3 %all-to-all-done.3.refs_0_ = bf16[16,48,256]{2,1,0:T(8,128)(2,1)S(1)} async-done(((bf16[16,48,256]{2,1,0:T(8,128)(2,1)}), bf16[16,48,256]{2,1,0:T(8,128)(2,1)S(1)}, u32[]{:S(2)}, u32[]{:S(2)}) %all-to-all-start.3) | async-done | bytes 393248 | tf_op jit(solution)/shard_map/all_to_all | solution.py:333
  64.2 1.9 %collective-permute-start = (bf16[96,256]{1,0:T(8,128)(2,1)S(1)}, bf16[96,256]{1,0:T(8,128)(2,1)S(1)}, u32[]{:S(2)}, u32[]{:S(2)}) collective-permute-start(bf16[96,256]{1,0:T(8,128)(2,1)S(1)} %update.5.own_ref), channel_id=1, source_target_pairs={{0,16},{16,32},{32,48},{48,64},{64,80},{80,96},{96,112},{112,128},... | collective-permute-start | bytes 147464 | tf_op jit(solution)/shard_map/ppermute | solution.py:338
  66.2 3.5 %collective-permute-done.passed_ref = bf16[96,256]{1,0:T(8,128)(2,1)S(1)} collective-permute-done((bf16[96,256]{1,0:T(8,128)(2,1)S(1)}, bf16[96,256]{1,0:T(8,128)(2,1)S(1)}, u32[]{:S(2)}, u32[]{:S(2)}) %collective-permute-start) | collective-permute-done | bytes 49184 | tf_op jit(solution)/shard_map/ppermute | solution.py:338
  69.7 18.6 %all_to_all.47.gathered_ref = bf16[16,96,256]{2,1,0:T(8,128)(2,1)S(1)} all-to-all(bf16[16,96,256]{2,1,0:T(8,128)(2,1)S(1)} %get-tuple-element.53), channel_id=1, replica_groups=mesh['seg'=16,'tok_0'=4,'tok_1'=4] {'tok_0','tok_1'}, dimensions={0} | all-to-all | bytes 1572864 | tf_op jit(solution)/shard_map/all_to_all | solution.py:333
  88.3 2.2 %grads.6 = (bf16[16,48,256]{2,1,0:T(8,128)(2,1)}, f32[8,128]{1,0:T(8,128)}) custom-call(bf16[16,96,256]{2,1,0:T(8,128)(2,1)S(1)} %all_to_all.47.gathered_ref, f32[2,1,2,1280]{3,2,1,0:T(2,128)S(1)} %copy-done.5, bf16[1280,256]{1,0:T(8,128)(2,1)S(1)} %get-tuple-element.54.key_rows, bf16[1280,256]{1,0:T(8,128)(2,1)S(1)} %get-tuple-element.55.value_rows), custom_call_target="tpu_custom_call" | custom-call | flops 1006632960 | bytes 1310720 | tf_op jit(solution)/shard_map/grads/pallas_call | solution.py:176
  90.5 3.8 %all-to-all-start.5 = ((bf16[16,48,256]{2,1,0:T(8,128)(2,1)}), bf16[16,48,256]{2,1,0:T(8,128)(2,1)S(1)}, u32[]{:S(2)}, u32[]{:S(2)}) async-start(bf16[16,48,256]{2,1,0:T(8,128)(2,1)} %get-tuple-element.56), calls=%async_computation.5 | async-start | bytes 786432 | tf_op jit(solution)/shard_map/all_to_all | solution.py:333
  94.3 2.8 %apply.5 = (bf16[2,1,2,1280,256]{4,3,2,1,0:T(8,128)(2,1)}, f32[8,128]{1,0:T(8,128)S(1)}, bf16[1280,256]{1,0:T(8,128)(2,1)S(1)}, bf16[1280,256]{1,0:T(8,128)(2,1)S(1)}) custom-call(bf16[16,96,256]{2,1,0:T(8,128)(2,1)S(1)} %all_to_all.47.gathered_ref, bf16[2,1,2,1280,256]{4,3,2,1,0:T(8,128)(2,1)} %refs_0_.5, ...), custom_call_target="tpu_custom_call", output_to_operand_aliasing={{0}: (4, {})} | custom-call | flops 503316480 | bytes 1310720 | tf_op jit(solution)/shard_map/apply/pallas_call | solution.py:310
  97.1 6.7 %all-to-all-done.5.refs_0_ = bf16[16,48,256]{2,1,0:T(8,128)(2,1)S(1)} async-done(((bf16[16,48,256]{2,1,0:T(8,128)(2,1)}), bf16[16,48,256]{2,1,0:T(8,128)(2,1)S(1)}, u32[]{:S(2)}, u32[]{:S(2)}) %all-to-all-start.5) | async-done | bytes 393248 | tf_op jit(solution)/shard_map/all_to_all | solution.py:333
  104.0 12.6 %all_to_all.48.gathered_ref = bf16[16,48,256]{2,1,0:T(8,128)(2,1)S(1)} all-to-all(bf16[16,48,256]{2,1,0:T(8,128)(2,1)S(1)} %get-tuple-element.61), channel_id=1, replica_groups=mesh['seg'=16,'tok_0'=4,'tok_1'=4] {'tok_0','tok_1'}, dimensions={0} | all-to-all | bytes 786432 | tf_op jit(solution)/shard_map/all_to_all | solution.py:333
  116.7 2.2 %grads.7 = (bf16[16,48,256]{2,1,0:T(8,128)(2,1)}, f32[8,128]{1,0:T(8,128)}) custom-call(bf16[16,48,256]{2,1,0:T(8,128)(2,1)S(1)} %all_to_all.48.gathered_ref, f32[2,1,2,1280]{3,2,1,0:T(2,128)S(1)} %copy-done.5, bf16[1280,256]{1,0:T(8,128)(2,1)S(1)} %get-tuple-element.62.key_rows, bf16[1280,256]{1,0:T(8,128)(2,1)S(1)} %get-tuple-element.63.value_rows), custom_call_target="tpu_custom_call" | custom-call | flops 1006632960 | bytes 1310720 | tf_op jit(solution)/shard_map/grads/pallas_call | solution.py:176
  118.9 3.7 %all-to-all-start.7 = ((bf16[16,48,256]{2,1,0:T(8,128)(2,1)}), bf16[16,48,256]{2,1,0:T(8,128)(2,1)S(1)}, u32[]{:S(2)}, u32[]{:S(2)}) async-start(bf16[16,48,256]{2,1,0:T(8,128)(2,1)} %get-tuple-element.64), calls=%async_computation.7 | async-start | bytes 786432 | tf_op jit(solution)/shard_map/all_to_all | solution.py:333
  122.6 2.8 %apply.6 = (bf16[2,1,2,1280,256]{4,3,2,1,0:T(8,128)(2,1)}, f32[8,128]{1,0:T(8,128)S(1)}, bf16[1280,256]{1,0:T(8,128)(2,1)S(1)}) custom-call(bf16[16,48,256]{2,1,0:T(8,128)(2,1)S(1)} %all_to_all.48.gathered_ref, bf16[2,1,2,1280,256]{4,3,2,1,0:T(8,128)(2,1)} %refs_0_.5, bf16[2,1,2,1280,256]{4,3,2,1,0:T(8,128)(2,1)} %refs_0_.5, ...), custom_call_target="tpu_custom_call", output_to_operand_aliasing={{0}: (3, {})} | custom-call | flops 503316480 | bytes 1310720 | tf_op jit(solution)/shard_map/apply/pallas_call | solution.py:310
  125.4 6.3 %all-to-all-done.7.refs_0_ = bf16[16,48,256]{2,1,0:T(8,128)(2,1)S(1)} async-done(((bf16[16,48,256]{2,1,0:T(8,128)(2,1)}), bf16[16,48,256]{2,1,0:T(8,128)(2,1)S(1)}, u32[]{:S(2)}, u32[]{:S(2)}) %all-to-all-start.7) | async-done | bytes 393248 | tf_op jit(solution)/shard_map/all_to_all | solution.py:333
  132.7 3.7 %all-to-all-start.8 = ((bf16[16,48,256]{2,1,0:T(8,128)(2,1)}), bf16[16,48,256]{2,1,0:T(8,128)(2,1)S(1)}, u32[]{:S(2)}, u32[]{:S(2)}) async-start(bf16[16,48,256]{2,1,0:T(8,128)(2,1)} %get-tuple-element.69), calls=%async_computation.8 | async-start | bytes 786432 | tf_op jit(solution)/shard_map/all_to_all | solution.py:333
  137.6 7.9 %all-to-all-done.8.gathered_ref = bf16[16,48,256]{2,1,0:T(8,128)(2,1)S(1)} async-done(((bf16[16,48,256]{2,1,0:T(8,128)(2,1)}), bf16[16,48,256]{2,1,0:T(8,128)(2,1)S(1)}, u32[]{:S(2)}, u32[]{:S(2)}) %all-to-all-start.8) | async-done | bytes 393248 | tf_op jit(solution)/shard_map/all_to_all | solution.py:333
  145.5 2.3 %apply.7 = (bf16[2,1,2,1280,256]{4,3,2,1,0:T(8,128)(2,1)}, f32[8,128]{1,0:T(8,128)}) custom-call(bf16[16,48,256]{2,1,0:T(8,128)(2,1)S(1)} %all-to-all-done.8.gathered_ref, bf16[1280,256]{1,0:T(8,128)(2,1)S(1)} %get-tuple-element.70.query_ref, bf16[2,1,2,1280,256]{4,3,2,1,0:T(8,128)(2,1)} %get-tuple-element.71.refs_0_), custom_call_target="tpu_custom_call", output_to_operand_aliasing={{0}: (2, {})} | custom-call | flops 503316480 | bytes 1310720 | tf_op jit(solution)/shard_map/apply/pallas_call | solution.py:310
  (21 shorter events, 6.8 us)
Async XLA Ops:
  0.6 0.8 copy-start
  1.4 18.6 %copy-start.5 = (f32[2,1,2,1280]{3,2,1,0:T(2,128)S(1)}, f32[2,1,2,1280]{3,2,1,0:T(2,128)}, u32[]{:S(2)}) copy-start(f32[2,1,2,1280]{3,2,1,0:T(2,128)} %rate_ref.7) | copy-start | bytes 61444
  22.4 14.0 %all-to-all-start.1 = ((bf16[16,64,256]{2,1,0:T(8,128)(2,1)}), bf16[16,64,256]{2,1,0:T(8,128)(2,1)S(1)}, u32[]{:S(2)}, u32[]{:S(2)}) async-start(bf16[16,64,256]{2,1,0:T(8,128)(2,1)} %get-tuple-element.42), calls=%async_computation.1 | async-start | bytes 1048576 | tf_op jit(solution)/shard_map/all_to_all | solution.py:333
  26.1 10.3 %copy-start.1 = (f32[1,3,256,16]{2,3,1,0:T(8,128)S(1)}, f32[1,3,256,16]{2,3,1,0:T(8,128)}, u32[]{:S(2)}) copy-start(f32[1,3,256,16]{2,3,1,0:T(8,128)} %param.12) | copy-start | bytes 147460
  26.1 10.3 %copy-start.2 = (f32[1,3,256,16]{2,3,1,0:T(8,128)S(1)}, f32[1,3,256,16]{2,3,1,0:T(8,128)}, u32[]{:S(2)}) copy-start(f32[1,3,256,16]{2,3,1,0:T(8,128)} %param.13) | copy-start | bytes 147460
  51.2 12.9 %all-to-all-start.3 = ((bf16[16,48,256]{2,1,0:T(8,128)(2,1)}), bf16[16,48,256]{2,1,0:T(8,128)(2,1)S(1)}, u32[]{:S(2)}, u32[]{:S(2)}) async-start(bf16[16,48,256]{2,1,0:T(8,128)(2,1)} %get-tuple-element.48), calls=%async_computation.3 | async-start | bytes 786432 | tf_op jit(solution)/shard_map/all_to_all | solution.py:333
  54.9 14.7 %copy-start.3 = (f32[3,256,16]{1,2,0:T(8,128)S(1)}, f32[3,256,16]{1,2,0:T(8,128)}, u32[]{:S(2)}) copy-start(f32[3,256,16]{1,2,0:T(8,128)} %param.14) | copy-start | bytes 147460
  54.9 14.7 %copy-start.4 = (f32[3,256,16]{1,2,0:T(8,128)S(1)}, f32[3,256,16]{1,2,0:T(8,128)}, u32[]{:S(2)}) copy-start(f32[3,256,16]{1,2,0:T(8,128)} %param.15) | copy-start | bytes 147460
  64.2 5.4 %collective-permute-start = (bf16[96,256]{1,0:T(8,128)(2,1)S(1)}, bf16[96,256]{1,0:T(8,128)(2,1)S(1)}, u32[]{:S(2)}, u32[]{:S(2)}) collective-permute-start(bf16[96,256]{1,0:T(8,128)(2,1)S(1)} %update.5.own_ref), channel_id=1, source_target_pairs={{0,16},{16,32},{32,48},{48,64},{64,80},{80,96},{96,112},{112,128},... | collective-permute-start | bytes 147464 | tf_op jit(solution)/shard_map/ppermute | solution.py:338
  90.5 13.3 %all-to-all-start.5 = ((bf16[16,48,256]{2,1,0:T(8,128)(2,1)}), bf16[16,48,256]{2,1,0:T(8,128)(2,1)S(1)}, u32[]{:S(2)}, u32[]{:S(2)}) async-start(bf16[16,48,256]{2,1,0:T(8,128)(2,1)} %get-tuple-element.56), calls=%async_computation.5 | async-start | bytes 786432 | tf_op jit(solution)/shard_map/all_to_all | solution.py:333
  118.9 12.9 %all-to-all-start.7 = ((bf16[16,48,256]{2,1,0:T(8,128)(2,1)}), bf16[16,48,256]{2,1,0:T(8,128)(2,1)S(1)}, u32[]{:S(2)}, u32[]{:S(2)}) async-start(bf16[16,48,256]{2,1,0:T(8,128)(2,1)} %get-tuple-element.64), calls=%async_computation.7 | async-start | bytes 786432 | tf_op jit(solution)/shard_map/all_to_all | solution.py:333
  132.7 12.9 %all-to-all-start.8 = ((bf16[16,48,256]{2,1,0:T(8,128)(2,1)}), bf16[16,48,256]{2,1,0:T(8,128)(2,1)S(1)}, u32[]{:S(2)}, u32[]{:S(2)}) async-start(bf16[16,48,256]{2,1,0:T(8,128)(2,1)} %get-tuple-element.69), calls=%async_computation.8 | async-start | bytes 786432 | tf_op jit(solution)/shard_map/all_to_all | solution.py:333

commit v4 on v3

--- a/solution.py
+++ b/solution.py
@@ -68,59 +68,59 @@
     return in_vmem(*array.shape[3:], dtype=array.dtype)
 
 
+def spread_kernel(weights_ref, message_ref, token_ref, held_ref, sem):
+    copy = pltpu.make_async_copy(weights_ref, held_ref, sem)
+    copy.start()
+    token_ref[...] = jnp.zeros_like(token_ref)
+    copy.wait()
+    message_ref[...] = jnp.broadcast_to(held_ref[...].astype(bf16)[None], message_ref.shape)
+
+
+def spread(weights, parties):
+    rows, width = weights.shape
+    return pl.pallas_call(
+        spread_kernel,
+        in_specs=[HBM],
+        out_specs=[VMEM] * 2,
+        out_shape=[in_vmem(parties, rows, width, dtype=bf16), TOKEN],
+        scratch_shapes=[pltpu.VMEM((rows, width), f32), pltpu.SemaphoreType.DMA],
+        compiler_params=params(),
+        name="spread",
+    )(in_hbm(weights))
+
+
 def stage_kernel(places, *refs):
     count = len(places)
     token_ref, sems = refs[-2:]
-    copies = started(refs[1 : 1 + count], refs[1 + count : 1 + 2 * count], places, sems)
+    copies = started(refs[1 : 1 + count], refs[-2 - count : -2], places, sems)
     token_ref[...] = jnp.zeros_like(token_ref)
+    handed = refs[1 + count : -2 - count]
+    for source, target in zip(handed[: len(handed) // 2], handed[len(handed) // 2 :]):
+        target[...] = source[...]
     for copy in copies:
         copy.wait()
 
 
-def stage(token, place, *arrays):
+def stage(token, place, arrays, handed=()):
     count = len(arrays)
     return pl.pallas_call(
         functools.partial(stage_kernel, [place] * count),
-        in_specs=[VMEM] + [HBM] * count,
-        out_specs=[VMEM] * (count + 1),
-        out_shape=[rows_in_vmem(array) for array in arrays] + [TOKEN],
+        in_specs=[VMEM] + [HBM] * count + [VMEM] * len(handed),
+        out_specs=[VMEM] * (len(handed) + count + 1),
+        out_shape=[in_vmem(*array.shape, dtype=array.dtype) for array in handed]
+        + [rows_in_vmem(array) for array in arrays]
+        + [TOKEN],
         scratch_shapes=[pltpu.SemaphoreType.DMA((count,))],
         compiler_params=params(),
         cost_estimate=pl.CostEstimate(
             flops=0, bytes_accessed=count * arrays[0].size, transcendentals=0
         ),
         name="stage",
-    )(token, *(in_hbm(array) for array in arrays))
-
-
-def begin_kernel(place, weights_ref, key_ref, value_ref, message_ref, key_rows, value_rows, token_ref, sems):
-    copies = started((key_ref, value_ref), (key_rows, value_rows), [place] * 2, sems)
-    message_ref[...] = jnp.broadcast_to(weights_ref[...].astype(bf16)[None], message_ref.shape)
-    token_ref[...] = jnp.zeros_like(token_ref)
-    for copy in copies:
-        copy.wait()
-
-
-def begin(weights, place, keys, values, parties):
-    rows, width = weights.shape
-    return pl.pallas_call(
-        functools.partial(begin_kernel, place),
-        in_specs=[VMEM, HBM, HBM],
-        out_specs=[VMEM] * 4,
-        out_shape=[
-            in_vmem(parties, rows, width, dtype=bf16),
-            rows_in_vmem(keys),
-            rows_in_vmem(values),
-            TOKEN,
-        ],
-        scratch_shapes=[pltpu.SemaphoreType.DMA((2,))],
-        compiler_params=params(),
-        name="begin",
-    )(weights, in_hbm(keys), in_hbm(values))
+    )(token, *(in_hbm(array) for array in arrays), *handed)
 
 
 def grads_kernel(
-    place, tile, gathered_ref, rate_ref, key_rows, value_rows, message_ref, token_ref, left_ref, back_ref
+    place, tile, gathered_ref, rate_ref, key_rows, value_rows, message_ref, token_ref, left_ref, back_ref, held_ref, sems
 ):
     parties, rows, width = message_ref.shape
     share = width // parties
@@ -142,16 +142,18 @@
         back_ref[0, :, span] = (back * pre_up * slope).astype(bf16)
         back_ref[1, :, span] = (active * pre_up * rate).astype(bf16)
         back_ref[2, :, span] = (back * active).astype(bf16)
-    keys, values = key_rows[...], value_rows[...]
-    gradients = (
-        dot(back_ref[0], keys, NN),
-        -dot(back_ref[1], values, NN).T,
-        dot(back_ref[2], keys, NN),
-    )
-    for index, gradient in enumerate(gradients):
-        message_ref[:, index * share : (index + 1) * share, :] = gradient.astype(bf16).reshape(
-            parties, share, width
+    copies = []
+
+    def send(index, tiles):
+        part = pl.ds(index * share, share)
+        held_ref[:, index * share : (index + 1) * share, :] = tiles
+        copies.append(
+            pltpu.make_async_copy(
+                held_ref.at[:, part, :], message_ref.at[:, part, :], sems.at[index]
+            )
         )
+        copies[-1].start()
+
     if rows > 3 * share:
         row = lax.broadcasted_iota(jnp.int32, (share, width), 0)
         extra = jnp.zeros((share, width), f32)
@@ -163,9 +165,14 @@
             high = square.astype(bf16).astype(f32)
             extra = jnp.where(row == 2 * index, high, extra)
             extra = jnp.where(row == 2 * index + 1, square - high, extra)
-        message_ref[:, 3 * share :, :] = jnp.broadcast_to(
-            extra.astype(bf16)[None], (parties, share, width)
-        )
+        send(3, jnp.broadcast_to(extra.astype(bf16)[None], (parties, share, width)))
+    keys, values = key_rows[...], value_rows[...]
+    shape = (parties, share, width)
+    send(1, -dot(back_ref[1], values, NN).T.astype(bf16).reshape(shape))
+    send(0, dot(back_ref[0], keys, NN).astype(bf16).reshape(shape))
+    send(2, dot(back_ref[2], keys, NN).astype(bf16).reshape(shape))
+    for copy in copies:
+        copy.wait()
 
 
 def grads(gathered, rates, keys, values, place):
@@ -176,9 +183,14 @@
     return pl.pallas_call(
         functools.partial(grads_kernel, place, 256),
         in_specs=[VMEM] * 4,
-        out_specs=[VMEM] * 2,
-        out_shape=[in_vmem(parties, rows, width, dtype=bf16), TOKEN],
-        scratch_shapes=[pltpu.VMEM((width, width), bf16), pltpu.VMEM((3, width, count), bf16)],
+        out_specs=[HBM, VMEM],
+        out_shape=[jax.ShapeDtypeStruct((parties, rows, width), bf16), TOKEN],
+        scratch_shapes=[
+            pltpu.VMEM((width, width), bf16),
+            pltpu.VMEM((3, width, count), bf16),
+            pltpu.VMEM((parties, rows, width), bf16),
+            pltpu.SemaphoreType.DMA((4,)),
+        ],
         compiler_params=params(),
         cost_estimate=pl.CostEstimate(
             flops=12 * count * width * width, bytes_accessed=4 * count * width, transcendentals=0
@@ -243,7 +255,7 @@
 
 
 def enter_kernel(
-    first_ref, passed_ref, own_ref, fresh_weights_ref, fresh_moment_ref, weights_ref, moment_ref, message_ref
+    first_ref, passed_ref, fresh_weights_ref, fresh_moment_ref, weights_ref, moment_ref, message_ref
 ):
     rows = weights_ref.shape[0]
     first = first_ref[0] == 1
@@ -251,65 +263,82 @@
     weights = jnp.where(first, fresh_weights_ref[...], passed[:rows])
     weights_ref[...] = weights
     moment_ref[...] = jnp.where(first, fresh_moment_ref[...], passed[rows:])
-    shape = (message_ref.shape[0], *weights.shape)
-    message_ref[:, :rows, :] = jnp.broadcast_to(weights.astype(bf16)[None], shape)
-    message_ref[:, rows:, :] = jnp.broadcast_to(own_ref[:rows, :][None], shape)
-
-
-def enter(first, passed, own, fresh_weights, fresh_moment, parties):
+    message_ref[...] = jnp.broadcast_to(weights.astype(bf16)[None], message_ref.shape)
+
+
+def enter(first, passed, fresh_weights, fresh_moment, parties):
     rows, width = fresh_weights.shape
     return pl.pallas_call(
         enter_kernel,
-        in_specs=[SMEM] + [VMEM] * 4,
+        in_specs=[SMEM] + [VMEM] * 3,
         out_specs=[VMEM] * 3,
         out_shape=[
             in_vmem(rows, width),
             in_vmem(rows, width),
-            in_vmem(parties, 2 * rows, width, dtype=bf16),
+            in_vmem(parties, rows, width, dtype=bf16),
         ],
         compiler_params=params(),
         name="enter",
-    )(first, passed, own, fresh_weights, fresh_moment)
-
-
-def apply_kernel(place, base, ahead, staged, aliased, gathered_ref, query_ref, *refs):
+    )(first, passed, fresh_weights, fresh_moment)
+
+
+def apply_kernel(place, ahead, staged, aliased, parts, chosen, gathered_ref, query_ref, wait_ref, *refs):
     count = len(ahead)
+    if chosen:
+        other_ref, flag_ref = refs[:2]
+        refs = refs[2:]
+
+        gathered_ref = jnp.where(flag_ref[0] == 1, other_ref[...], gathered_ref[...])
+
     sources, refs = refs[:count], refs[count + aliased :]
     out_ref, token_ref, targets = refs[0], refs[1], refs[2 : 2 + count]
-    query_rows, held_ref, sems = refs[2 + count :]
+    query_rows, held_ref, sems, ahead_sems = refs[2 + count :]
     token_ref[...] = jnp.zeros_like(token_ref)
-    share = query_rows.shape[-1] // gathered_ref.shape[0]
-    copies = []
+    length, width = query_rows.shape
+    share = width // gathered_ref.shape[0]
     if not staged:
-        copies += started([query_ref], [query_rows], [place], sems)
-    copies += started(sources, targets, ahead, sems.at[pl.ds(2, max(count, 1))])
-    if staged:
-        queries = query_ref[...]
-    else:
-        copies.pop(0).wait()
-        queries = query_rows[...]
-    pre_gate = dot(queries, matrix(gathered_ref, base + 0, share), NT)
-    pre_up = dot(queries, matrix(gathered_ref, base + 2, share), NT)
-    hidden = (pre_gate * sigmoid(pre_gate) * pre_up).astype(bf16)
-    held_ref[...] = dot(hidden, matrix(gathered_ref, base + 1, share), NT).astype(bf16)
-    copies.append(pltpu.make_async_copy(held_ref, out_ref.at[*place], sems.at[1]))
-    copies[-1].start()
+        (first,) = started([query_ref], [query_rows], [place], sems.at[pl.ds(parts, 1)])
+    copies = started(sources, targets, ahead, ahead_sems)
+    if not staged:
+        first.wait()
+    rows_ref = query_ref if staged else query_rows
+    size = length // parts
+    for part in range(parts):
+        queries = rows_ref[part * size : (part + 1) * size, :]
+        pre_gate = dot(queries, matrix(gathered_ref, 0, share), NT)
+        pre_up = dot(queries, matrix(gathered_ref, 2, share), NT)
+        hidden = (pre_gate * sigmoid(pre_gate) * pre_up).astype(bf16)
+        held_ref[part * size : (part + 1) * size, :] = dot(
+            hidden, matrix(gathered_ref, 1, share), NT
+        ).astype(bf16)
+        span = pl.ds(part * size, size)
+        copies.append(
+            pltpu.make_async_copy(held_ref.at[span, :], out_ref.at[*place].at[span, :], sems.at[part])
+        )
+        copies[-1].start()
     for copy in copies:
         copy.wait()
 
 
-def apply_fast(gathered, base, queries, place, results, shape, ahead=()):
+def apply_fast(gathered, queries, place, results, shape, token, ahead=(), parts=1, instead=()):
     count, width = shape[3:]
     staged = len(queries.shape) == 2
-    given = [gathered, queries if staged else in_hbm(queries)]
-    given += [in_hbm(array) for array, _ in ahead]
-    in_specs = [VMEM, VMEM if staged else HBM] + [HBM] * len(ahead)
+    given = [gathered, queries if staged else in_hbm(queries), token]
+    given += [*instead, *(in_hbm(array) for array, _ in ahead)]
+    in_specs = [VMEM, VMEM if staged else HBM, VMEM]
+    in_specs += [VMEM, SMEM][: len(instead)] + [HBM] * len(ahead)
     if results is not None:
         given.append(results)
         in_specs.append(HBM)
     return pl.pallas_call(
         functools.partial(
-            apply_kernel, place, base, [where for _, where in ahead], staged, int(results is not None)
+            apply_kernel,
+            place,
+            [where for _, where in ahead],
+            staged,
+            int(results is not None),
+            parts,
+            bool(instead),
         ),
         in_specs=in_specs,
         out_specs=[HBM] + [VMEM] * (1 + len(ahead)),
@@ -319,7 +348,8 @@
         scratch_shapes=[
             pltpu.VMEM((count, width), bf16),
             pltpu.VMEM((count, width), bf16),
-            pltpu.SemaphoreType.DMA((2 + max(len(ahead), 1),)),
+            pltpu.SemaphoreType.DMA((parts + 1,)),
+            pltpu.SemaphoreType.DMA((max(len(ahead), 1),)),
         ],
         compiler_params=params(),
         cost_estimate=pl.CostEstimate(
@@ -336,6 +366,11 @@
 def passed_on(array):
     length = lax.axis_size("seg")
     return lax.ppermute(array, "seg", [(i, i + 1) for i in range(length - 1)])
+
+
+def handed_back(array):
+    length = lax.axis_size("seg")
+    return lax.ppermute(array, "seg", [(i + 1, i) for i in range(length - 1)])
 
 
 def columns_first(state):
@@ -352,14 +387,17 @@
     sections, _, blocks, count, _ = queries.shape
     parties = lax.axis_size(TOK)
     share = fast_weights.shape[3]
-    first = (lax.axis_index("seg") == 0).astype(jnp.int32).reshape(1)
+    place_in_chain = lax.axis_index("seg")
+    first = (place_in_chain == 0).astype(jnp.int32).reshape(1)
+    is_last = place_in_chain == lax.axis_size("seg") - 1
     weights, moment = columns_first(fast_weights[0]), columns_first(momenta[0])
     fresh_weights, fresh_moment = columns_first(fresh_weights), columns_first(fresh_momenta)
-    shape = queries.shape
+    rows, shape = weights.shape[0], queries.shape
     places = [(section, 0, block) for section in range(sections) for block in range(blocks)]
-    message, *staged, _ = begin(weights, places[0], key_vectors, values, parties)
-    gathered, base = exchanged(message), 0
-    results = squares = None
+    message, token = spread(weights, parties)
+    *staged, _ = stage(token, places[0], (key_vectors, values))
+    gathered = exchanged(message)
+    results = squares = left = owed = None
     for index, place in enumerate(places):
         last = index == len(places) - 1
         leaving = not last and place[2] == blocks - 1
@@ -370,22 +408,42 @@
         else:
             ahead = ((key_vectors, places[index + 1]), (values, places[index + 1]))
         if index == 0:
-            *staged, token = stage(token, ahead[0][1], *(array for array, _ in ahead))
+            *staged, token = stage(token, places[1], (key_vectors, values))
+        elif left is not None:
+            handed, *staged, token = stage(
+                token, places[index + 1], (key_vectors, values), (gathered,)
+            )
+            back = handed_back(handed)
+            own = lax.cond(
+                is_last,
+                lambda mine: exchanged(jnp.broadcast_to(mine[None], (parties, *mine.shape))),
+                lambda mine: jnp.zeros((parties, *mine.shape), bf16),
+                left[:rows],
+            )
+            owed, left = (back, places[index - 1], own), None
         else:
             results, token, *staged = apply_fast(
-                gathered, base, queries, places[index - 1], results, shape, ahead
+                gathered, queries, places[index - 1], results, shape, token, ahead
             )
         message, *state = update(index, arrived, weights, moment, squares, token, leaving)
-        base = 0
         if leaving:
+            left = message
             weights, moment, message = enter(
-                first, passed_on(message), message, fresh_weights, fresh_moment, parties
+                first, passed_on(message), fresh_weights, fresh_moment, parties
             )
-            base = 3
         else:
             weights, moment, squares = (*state, squares)[:3]
         gathered = exchanged(message)
-    results, *_ = apply_fast(gathered, base, staged[0], places[-1], results, shape)
+    results, token = apply_fast(
+        owed[0],
+        queries,
+        owed[1],
+        results,
+        shape,
+        weights,
+        instead=(owed[2], is_last.astype(jnp.int32).reshape(1)),
+    )
+    results, _ = apply_fast(gathered, staged[0], places[-1], results, shape, token, parts=2)
     return (results, rows_first(weights, share)[None], rows_first(moment, share)[None])
 
 

time: 149 us -> 146 us (0.980)
  blocking collectives: 60.3 us -> 39.8 us
  starting transfers between devices: 20.6 us -> 29.3 us
  waiting for transfers between devices: 39.6 us -> 45 us
  Pallas kernels: 24.5 us -> 28.1 us
    all_to_all x4 -> x3, blocking collectives: 60.3 us -> 39.8 us  [exchanged(): return lax.all_to_all(tiles, TOK, split_axis=0, concat_axis=0, tiled=True)]
    all_to_all x5 -> x6, starting transfers between devices: 18.6 us -> 25.5 us  [exchanged(): return lax.all_to_all(tiles, TOK, split_axis=0, concat_axis=0, tiled=True)]
    all_to_all x5 -> x6, waiting for transfers between devices: 36.1 us -> 41.3 us  [exchanged(): return lax.all_to_all(tiles, TOK, split_axis=0, concat_axis=0, tiled=True)]
    pallas_call x1 -> x3, Pallas kernels: 1.33 us -> 4.53 us  [stage(): pl.pallas_call(functools.partial(stage_kernel, [place] * count), in_specs...]
    ppermute x0 -> x1, starting transfers between devices: none -> 1.92 us  [handed_back(): return lax.ppermute(array, 'seg', [(i + 1, i) for i in range(length - 1)])]
  transfers between devices with their start and end apart: 6 -> 8, of which waited for: 6 -> 7; matrix products, arithmetic and copies ran while one was open for 1% -> 1% of each run, Pallas kernels for 7% -> 10%
where the time goes in v4:
time: 146 us; the launch traced here: 144 us
  waiting for transfers between devices  45 us (31%)
  blocking collectives  39.8 us (27%)
  starting transfers between devices  29.3 us (20%)
  Pallas kernels  28.1 us (19%)
    all_to_all x6, waiting for transfers between devices, exchanged(): return lax.all_to_all(tiles, TOK, split_axis=0, concat_axis=0, tiled=True)  41.3 us
    all_to_all x3, blocking collectives, exchanged(): return lax.all_to_all(tiles, TOK, split_axis=0, concat_axis=0, tiled=True)  39.8 us
    all_to_all x6, starting transfers between devices, exchanged(): return lax.all_to_all(tiles, TOK, split_axis=0, concat_axis=0, tiled=True)  25.5 us
    pallas_call x4, Pallas kernels, apply_fast(): pl.pallas_call(functools.partial(apply_kernel, place, [where for _, where...  10.7 us
    pallas_call x4, Pallas kernels, grads(): pl.pallas_call(functools.partial(grads_kernel, place, 256), in_specs=[VME...  9.13 us
    pallas_call x3, Pallas kernels, stage(): pl.pallas_call(functools.partial(stage_kernel, [place] * count), in_specs...  4.53 us
    ppermute x1, waiting for transfers between devices, passed_on(): return lax.ppermute(array, 'seg', [(i, i + 1) for i in range(length - 1)])  3.63 us
  transfers between devices with their start and end apart: 8, of which 7 were waited for; matrix products, arithmetic and copies ran while one was open for 1% of the time, Pallas kernels for 10%

profile of v4, /device:TPU:96, one launch (start us, length us, event | category | flops | bytes accessed | tf_op | source)
XLA Modules:
  0.0 144.4 jit_solution(15640140372999047607)
XLA Ops:
  2.2 7.0 %all-to-all-start.1 = ((bf16[16,48,256]{2,1,0:T(8,128)(2,1)}), bf16[16,48,256]{2,1,0:T(8,128)(2,1)S(1)}, u32[]{:S(2)}, u32[]{:S(2)}) async-start(bf16[16,48,256]{2,1,0:T(8,128)(2,1)} %get-tuple-element.50), calls=%async_computation.1 | async-start | bytes 786432 | tf_op jit(solution)/shard_map/all_to_all | solution.py:363
  11.2 7.9 %all-to-all-done.1.gathered_ref = bf16[16,48,256]{2,1,0:T(8,128)(2,1)S(1)} async-done(((bf16[16,48,256]{2,1,0:T(8,128)(2,1)}), bf16[16,48,256]{2,1,0:T(8,128)(2,1)S(1)}, u32[]{:S(2)}, u32[]{:S(2)}) %all-to-all-start.1) | async-done | bytes 393248 | tf_op jit(solution)/shard_map/all_to_all | solution.py:363
  19.1 2.3 %grads.4 = (bf16[16,64,256]{2,1,0:T(8,128)(2,1)}, f32[8,128]{1,0:T(8,128)S(1)}) custom-call(bf16[16,48,256]{2,1,0:T(8,128)(2,1)S(1)} %all-to-all-done.1.gathered_ref, f32[2,1,2,1280]{3,2,1,0:T(2,128)S(1)} %copy-done.4, bf16[1280,256]{1,0:T(8,128)(2,1)S(1)} %get-tuple-element.52.key_rows, bf16[1280,256]{1,0:T(8,128)(2,1)S(1)} %get-tuple-element.53.value_rows), custom_call_target="tpu_custom_call" | custom-call | flops 1006632960 | bytes 1310720 | tf_op jit(solution)/shard_map/grads/pallas_call | solution.py:183
  21.4 3.7 %all-to-all-start.2 = ((bf16[16,64,256]{2,1,0:T(8,128)(2,1)}), bf16[16,64,256]{2,1,0:T(8,128)(2,1)S(1)}, u32[]{:S(2)}, u32[]{:S(2)}) async-start(bf16[16,64,256]{2,1,0:T(8,128)(2,1)} %get-tuple-element.54), calls=%async_computation.2 | async-start | bytes 1048576 | tf_op jit(solution)/shard_map/all_to_all | solution.py:363
  26.5 8.9 %all-to-all-done.2.refs_0_ = bf16[16,64,256]{2,1,0:T(8,128)(2,1)S(1)} async-done(((bf16[16,64,256]{2,1,0:T(8,128)(2,1)}), bf16[16,64,256]{2,1,0:T(8,128)(2,1)S(1)}, u32[]{:S(2)}, u32[]{:S(2)}) %all-to-all-start.2) | async-done | bytes 524320 | tf_op jit(solution)/shard_map/all_to_all | solution.py:363
  35.7 12.4 %all_to_all.50.gathered_ref = bf16[16,48,256]{2,1,0:T(8,128)(2,1)S(1)} all-to-all(bf16[16,48,256]{2,1,0:T(8,128)(2,1)S(1)} %get-tuple-element.57), channel_id=1, replica_groups=mesh['seg'=16,'tok_0'=4,'tok_1'=4] {'tok_0','tok_1'}, dimensions={0} | all-to-all | bytes 786432 | tf_op jit(solution)/shard_map/all_to_all | solution.py:363
  48.0 2.3 %grads.5 = (bf16[16,48,256]{2,1,0:T(8,128)(2,1)}, f32[8,128]{1,0:T(8,128)S(1)}) custom-call(bf16[16,48,256]{2,1,0:T(8,128)(2,1)S(1)} %all_to_all.50.gathered_ref, f32[2,1,2,1280]{3,2,1,0:T(2,128)S(1)} %copy-done.4, bf16[1280,256]{1,0:T(8,128)(2,1)S(1)} %get-tuple-element.58.key_rows, bf16[1280,256]{1,0:T(8,128)(2,1)S(1)} %get-tuple-element.59.value_rows), custom_call_target="tpu_custom_call" | custom-call | flops 1006632960 | bytes 1310720 | tf_op jit(solution)/shard_map/grads/pallas_call | solution.py:183
  50.3 3.7 %all-to-all-start.4 = ((bf16[16,48,256]{2,1,0:T(8,128)(2,1)}), bf16[16,48,256]{2,1,0:T(8,128)(2,1)S(1)}, u32[]{:S(2)}, u32[]{:S(2)}) async-start(bf16[16,48,256]{2,1,0:T(8,128)(2,1)} %get-tuple-element.60), calls=%async_computation.4 | async-start | bytes 786432 | tf_op jit(solution)/shard_map/all_to_all | solution.py:363
  54.1 3.0 %apply.4 = (bf16[2,1,2,1280,256]{4,3,2,1,0:T(8,128)(2,1)}, f32[8,128]{1,0:T(8,128)S(1)}, bf16[1280,256]{1,0:T(8,128)(2,1)S(1)}, bf16[1280,256]{1,0:T(8,128)(2,1)S(1)}) custom-call(bf16[16,48,256]{2,1,0:T(8,128)(2,1)S(1)} %all_to_all.50.gathered_ref, bf16[2,1,2,1280,256]{4,3,2,1,0:T(8,128)(2,1)} %query_ref.5, f32[8,128]{1,0:T(8,128)S(1)} %get-tuple-element.64.wait_ref, ...), custom_call_target="tpu_custom_call" | custom-call | flops 503316480 | bytes 1310720 | tf_op jit(solution)/shard_map/apply/pallas_call | solution.py:333
  57.1 6.1 %all-to-all-done.4.refs_0_ = bf16[16,48,256]{2,1,0:T(8,128)(2,1)S(1)} async-done(((bf16[16,48,256]{2,1,0:T(8,128)(2,1)}), bf16[16,48,256]{2,1,0:T(8,128)(2,1)S(1)}, u32[]{:S(2)}, u32[]{:S(2)}) %all-to-all-start.4) | async-done | bytes 393248 | tf_op jit(solution)/shard_map/all_to_all | solution.py:363
  66.0 3.6 %collective-permute-done.passed_ref = bf16[96,256]{1,0:T(8,128)(2,1)S(1)} collective-permute-done((bf16[96,256]{1,0:T(8,128)(2,1)}, bf16[96,256]{1,0:T(8,128)(2,1)S(1)}, u32[]{:S(2)}, u32[]{:S(2)}) %collective-permute-start) | collective-permute-done | bytes 49184 | tf_op jit(solution)/shard_map/ppermute | solution.py:368
  69.6 14.8 %all_to_all.51.gathered_ref.refs_3_ = bf16[16,48,256]{2,1,0:T(8,128)(2,1)S(1)} all-to-all(bf16[16,48,256]{2,1,0:T(8,128)(2,1)S(1)} %get-tuple-element.66), channel_id=1, replica_groups=mesh['seg'=16,'tok_0'=4,'tok_1'=4] {'tok_0','tok_1'}, dimensions={0} | all-to-all | bytes 786432 | tf_op jit(solution)/shard_map/all_to_all | solution.py:363
  84.4 2.2 %grads.6 = (bf16[16,48,256]{2,1,0:T(8,128)(2,1)}, f32[8,128]{1,0:T(8,128)S(1)}) custom-call(bf16[16,48,256]{2,1,0:T(8,128)(2,1)S(1)} %all_to_all.51.gathered_ref.refs_3_, f32[2,1,2,1280]{3,2,1,0:T(2,128)S(1)} %copy-done.4, bf16[1280,256]{1,0:T(8,128)(2,1)S(1)} %get-tuple-element.67.key_rows, bf16[1280,256]{1,0:T(8,128)(2,1)S(1)} %get-tuple-element.68.value_rows), custom_call_target="tpu_custom_call" | custom-call | flops 1006632960 | bytes 1310720 | tf_op jit(solution)/shard_map/grads/pallas_call | solution.py:183
  86.6 3.6 %all-to-all-start.6 = ((bf16[16,48,256]{2,1,0:T(8,128)(2,1)}), bf16[16,48,256]{2,1,0:T(8,128)(2,1)S(1)}, u32[]{:S(2)}, u32[]{:S(2)}) async-start(bf16[16,48,256]{2,1,0:T(8,128)(2,1)} %get-tuple-element.69), calls=%async_computation.6 | async-start | bytes 786432 | tf_op jit(solution)/shard_map/all_to_all | solution.py:363
  91.5 8.5 %all-to-all-done.6.refs_0_ = bf16[16,48,256]{2,1,0:T(8,128)(2,1)S(1)} async-done(((bf16[16,48,256]{2,1,0:T(8,128)(2,1)}), bf16[16,48,256]{2,1,0:T(8,128)(2,1)S(1)}, u32[]{:S(2)}, u32[]{:S(2)}) %all-to-all-start.6) | async-done | bytes 393248 | tf_op jit(solution)/shard_map/all_to_all | solution.py:363
  100.1 12.6 %all_to_all.52.gathered_ref = bf16[16,48,256]{2,1,0:T(8,128)(2,1)S(1)} all-to-all(bf16[16,48,256]{2,1,0:T(8,128)(2,1)S(1)} %get-tuple-element.74), channel_id=1, replica_groups=mesh['seg'=16,'tok_0'=4,'tok_1'=4] {'tok_0','tok_1'}, dimensions={0} | all-to-all | bytes 786432 | tf_op jit(solution)/shard_map/all_to_all | solution.py:363
  112.8 2.3 %grads.7 = (bf16[16,48,256]{2,1,0:T(8,128)(2,1)}, f32[8,128]{1,0:T(8,128)S(1)}) custom-call(bf16[16,48,256]{2,1,0:T(8,128)(2,1)S(1)} %all_to_all.52.gathered_ref, f32[2,1,2,1280]{3,2,1,0:T(2,128)S(1)} %copy-done.4, bf16[1280,256]{1,0:T(8,128)(2,1)S(1)} %get-tuple-element.75.key_rows, bf16[1280,256]{1,0:T(8,128)(2,1)S(1)} %get-tuple-element.76.value_rows), custom_call_target="tpu_custom_call" | custom-call | flops 1006632960 | bytes 1310720 | tf_op jit(solution)/shard_map/grads/pallas_call | solution.py:183
  115.1 3.7 %all-to-all-start.8 = ((bf16[16,48,256]{2,1,0:T(8,128)(2,1)}), bf16[16,48,256]{2,1,0:T(8,128)(2,1)S(1)}, u32[]{:S(2)}, u32[]{:S(2)}) async-start(bf16[16,48,256]{2,1,0:T(8,128)(2,1)} %get-tuple-element.77), calls=%async_computation.8 | async-start | bytes 786432 | tf_op jit(solution)/shard_map/all_to_all | solution.py:363
  120.8 2.8 %apply.5 = (bf16[2,1,2,1280,256]{4,3,2,1,0:T(8,128)(2,1)}, f32[8,128]{1,0:T(8,128)S(1)}, bf16[1280,256]{1,0:T(8,128)(2,1)S(1)}) custom-call(bf16[16,48,256]{2,1,0:T(8,128)(2,1)S(1)} %all_to_all.52.gathered_ref, bf16[2,1,2,1280,256]{4,3,2,1,0:T(8,128)(2,1)} %query_ref.5, f32[8,128]{1,0:T(8,128)S(1)} %get-tuple-element.80.wait_ref, ...), custom_call_target="tpu_custom_call", output_to_operand_aliasing={{0}: (4, {})} | custom-call | flops 503316480 | bytes 1310720 | tf_op jit(solution)/shard_map/apply/pallas_call | solution.py:333
  123.6 4.4 %all-to-all-done.8.refs_0_ = bf16[16,48,256]{2,1,0:T(8,128)(2,1)S(1)} async-done(((bf16[16,48,256]{2,1,0:T(8,128)(2,1)}), bf16[16,48,256]{2,1,0:T(8,128)(2,1)S(1)}, u32[]{:S(2)}, u32[]{:S(2)}) %all-to-all-start.8) | async-done | bytes 393248 | tf_op jit(solution)/shard_map/all_to_all | solution.py:363
  128.9 3.7 %all-to-all-start.9 = ((bf16[16,48,256]{2,1,0:T(8,128)(2,1)}), bf16[16,48,256]{2,1,0:T(8,128)(2,1)S(1)}, u32[]{:S(2)}, u32[]{:S(2)}) async-start(bf16[16,48,256]{2,1,0:T(8,128)(2,1)} %get-tuple-element.83), calls=%async_computation.9 | async-start | bytes 786432 | tf_op jit(solution)/shard_map/all_to_all | solution.py:363
  133.9 2.8 %apply.6 = (bf16[2,1,2,1280,256]{4,3,2,1,0:T(8,128)(2,1)}, f32[8,128]{1,0:T(8,128)S(1)}) custom-call(bf16[16,48,256]{2,1,0:T(8,128)(2,1)S(1)} %collective-permute-done.1.gathered_ref, bf16[2,1,2,1280,256]{4,3,2,1,0:T(8,128)(2,1)} %query_ref.5, f32[48,256]{1,0:T(8,128)S(1)} %get-tuple-element.86.wait_ref, ...), custom_call_target="tpu_custom_call", output_to_operand_aliasing={{0}: (5, {})} | custom-call | flops 503316480 | bytes 1310720 | tf_op jit(solution)/shard_map/apply/pallas_call | solution.py:333
  136.6 5.6 %all-to-all-done.9.gathered_ref = bf16[16,48,256]{2,1,0:T(8,128)(2,1)S(1)} async-done(((bf16[16,48,256]{2,1,0:T(8,128)(2,1)}), bf16[16,48,256]{2,1,0:T(8,128)(2,1)S(1)}, u32[]{:S(2)}, u32[]{:S(2)}) %all-to-all-start.9) | async-done | bytes 393248 | tf_op jit(solution)/shard_map/all_to_all | solution.py:363
  142.2 2.2 %apply.7 = (bf16[2,1,2,1280,256]{4,3,2,1,0:T(8,128)(2,1)}, f32[8,128]{1,0:T(8,128)}) custom-call(bf16[16,48,256]{2,1,0:T(8,128)(2,1)S(1)} %all-to-all-done.9.gathered_ref, bf16[1280,256]{1,0:T(8,128)(2,1)S(1)} %get-tuple-element.84.query_ref, f32[8,128]{1,0:T(8,128)S(1)} %get-tuple-element.88.wait_ref, ...), custom_call_target="tpu_custom_call", output_to_operand_aliasing={{0}: (3, {})} | custom-call | flops 503316480 | bytes 1310720 | tf_op jit(solution)/shard_map/apply/pallas_call | solution.py:333
  (26 shorter events, 13.4 us)
Async XLA Ops:
  2.2 16.9 %all-to-all-start.1 = ((bf16[16,48,256]{2,1,0:T(8,128)(2,1)}), bf16[16,48,256]{2,1,0:T(8,128)(2,1)S(1)}, u32[]{:S(2)}, u32[]{:S(2)}) async-start(bf16[16,48,256]{2,1,0:T(8,128)(2,1)} %get-tuple-element.50), calls=%async_computation.1 | async-start | bytes 786432 | tf_op jit(solution)/shard_map/all_to_all | solution.py:363
  9.3 9.8 %copy-start.4 = (f32[2,1,2,1280]{3,2,1,0:T(2,128)S(1)}, f32[2,1,2,1280]{3,2,1,0:T(2,128)}, u32[]{:S(2)}) copy-start(f32[2,1,2,1280]{3,2,1,0:T(2,128)} %rate_ref.7) | copy-start | bytes 61444
  21.4 14.0 %all-to-all-start.2 = ((bf16[16,64,256]{2,1,0:T(8,128)(2,1)}), bf16[16,64,256]{2,1,0:T(8,128)(2,1)S(1)}, u32[]{:S(2)}, u32[]{:S(2)}) async-start(bf16[16,64,256]{2,1,0:T(8,128)(2,1)} %get-tuple-element.54), calls=%async_computation.2 | async-start | bytes 1048576 | tf_op jit(solution)/shard_map/all_to_all | solution.py:363
  25.2 10.3 %copy-start = (f32[1,3,256,16]{2,3,1,0:T(8,128)S(1)}, f32[1,3,256,16]{2,3,1,0:T(8,128)}, u32[]{:S(2)}) copy-start(f32[1,3,256,16]{2,3,1,0:T(8,128)} %param.14) | copy-start | bytes 147460
  25.2 10.3 %copy-start.1 = (f32[1,3,256,16]{2,3,1,0:T(8,128)S(1)}, f32[1,3,256,16]{2,3,1,0:T(8,128)}, u32[]{:S(2)}) copy-start(f32[1,3,256,16]{2,3,1,0:T(8,128)} %param.15) | copy-start | bytes 147460
  50.3 12.9 %all-to-all-start.4 = ((bf16[16,48,256]{2,1,0:T(8,128)(2,1)}), bf16[16,48,256]{2,1,0:T(8,128)(2,1)S(1)}, u32[]{:S(2)}, u32[]{:S(2)}) async-start(bf16[16,48,256]{2,1,0:T(8,128)(2,1)} %get-tuple-element.60), calls=%async_computation.4 | async-start | bytes 786432 | tf_op jit(solution)/shard_map/all_to_all | solution.py:363
  54.1 15.5 %copy-start.2 = (f32[3,256,16]{1,2,0:T(8,128)S(1)}, f32[3,256,16]{1,2,0:T(8,128)}, u32[]{:S(2)}) copy-start(f32[3,256,16]{1,2,0:T(8,128)} %param.16) | copy-start | bytes 147460
  54.1 15.5 %copy-start.3 = (f32[3,256,16]{1,2,0:T(8,128)S(1)}, f32[3,256,16]{1,2,0:T(8,128)}, u32[]{:S(2)}) copy-start(f32[3,256,16]{1,2,0:T(8,128)} %param.17) | copy-start | bytes 147460
  64.0 5.6 %collective-permute-start = (bf16[96,256]{1,0:T(8,128)(2,1)}, bf16[96,256]{1,0:T(8,128)(2,1)S(1)}, u32[]{:S(2)}, u32[]{:S(2)}) collective-permute-start(bf16[96,256]{1,0:T(8,128)(2,1)} %update.5), channel_id=1, source_target_pairs={{0,16},{16,32},{32,48},{48,64},{64,80},{80,96},{96,112},{112,128},... | collective-permute-start | bytes 147464 | tf_op jit(solution)/shard_map/ppermute | solution.py:368
  86.6 13.3 %all-to-all-start.6 = ((bf16[16,48,256]{2,1,0:T(8,128)(2,1)}), bf16[16,48,256]{2,1,0:T(8,128)(2,1)S(1)}, u32[]{:S(2)}, u32[]{:S(2)}) async-start(bf16[16,48,256]{2,1,0:T(8,128)(2,1)} %get-tuple-element.69), calls=%async_computation.6 | async-start | bytes 786432 | tf_op jit(solution)/shard_map/all_to_all | solution.py:363
  115.1 12.9 %all-to-all-start.8 = ((bf16[16,48,256]{2,1,0:T(8,128)(2,1)}), bf16[16,48,256]{2,1,0:T(8,128)(2,1)S(1)}, u32[]{:S(2)}, u32[]{:S(2)}) async-start(bf16[16,48,256]{2,1,0:T(8,128)(2,1)} %get-tuple-element.77), calls=%async_computation.8 | async-start | bytes 786432 | tf_op jit(solution)/shard_map/all_to_all | solution.py:363
  118.8 15.0 %collective-permute-start.1 = (bf16[16,48,256]{2,1,0:T(8,128)(2,1)S(1)}, bf16[16,48,256]{2,1,0:T(8,128)(2,1)S(1)}, u32[]{:S(2)}, u32[]{:S(2)}) collective-permute-start(bf16[16,48,256]{2,1,0:T(8,128)(2,1)S(1)} %get-tuple-element.85), channel_id=1, source_target_pairs={{16,0},{32,16},{48,32},{64,48},{80,64},{96,80},{112,96},{128,112},... | collective-permute-start | bytes 1179656 | tf_op jit(solution)/shard_map/ppermute | solution.py:373
  128.9 13.3 %all-to-all-start.9 = ((bf16[16,48,256]{2,1,0:T(8,128)(2,1)}), bf16[16,48,256]{2,1,0:T(8,128)(2,1)S(1)}, u32[]{:S(2)}, u32[]{:S(2)}) async-start(bf16[16,48,256]{2,1,0:T(8,128)(2,1)} %get-tuple-element.83), calls=%async_computation.9 | async-start | bytes 786432 | tf_op jit(solution)/shard_map/all_to_all | solution.py:363

commit v5 on v4

--- a/solution.py
+++ b/solution.py
@@ -89,44 +89,45 @@
     )(in_hbm(weights))
 
 
+def copies_kernel(state_ref, message_ref):
+    rows = message_ref.shape[1]
+    message_ref[...] = jnp.broadcast_to(state_ref[:rows, :][None], message_ref.shape)
+
+
 def stage_kernel(places, *refs):
     count = len(places)
     token_ref, sems = refs[-2:]
     copies = started(refs[1 : 1 + count], refs[-2 - count : -2], places, sems)
     token_ref[...] = jnp.zeros_like(token_ref)
-    handed = refs[1 + count : -2 - count]
-    for source, target in zip(handed[: len(handed) // 2], handed[len(handed) // 2 :]):
-        target[...] = source[...]
     for copy in copies:
         copy.wait()
 
 
-def stage(token, place, arrays, handed=()):
+def stage(token, place, arrays):
     count = len(arrays)
     return pl.pallas_call(
         functools.partial(stage_kernel, [place] * count),
-        in_specs=[VMEM] + [HBM] * count + [VMEM] * len(handed),
-        out_specs=[VMEM] * (len(handed) + count + 1),
-        out_shape=[in_vmem(*array.shape, dtype=array.dtype) for array in handed]
-        + [rows_in_vmem(array) for array in arrays]
-        + [TOKEN],
+        in_specs=[VMEM] + [HBM] * count,
+        out_specs=[VMEM] * (count + 1),
+        out_shape=[rows_in_vmem(array) for array in arrays] + [TOKEN],
         scratch_shapes=[pltpu.SemaphoreType.DMA((count,))],
         compiler_params=params(),
         cost_estimate=pl.CostEstimate(
             flops=0, bytes_accessed=count * arrays[0].size, transcendentals=0
         ),
         name="stage",
-    )(token, *(in_hbm(array) for array in arrays), *handed)
-
-
-def grads_kernel(
-    place, tile, gathered_ref, rate_ref, key_rows, value_rows, message_ref, token_ref, left_ref, back_ref, held_ref, sems
-):
+    )(token, *(in_hbm(array) for array in arrays))
+
+
+def grads_kernel(place, tile, ahead, gathered_ref, rate_ref, key_rows, value_rows, *refs):
+    later = len(ahead)
+    message_ref = refs[later]
+    left_ref, back_ref, sems = refs[-3:]
+    copies = started(refs[:later], refs[later + 1 : 2 * later + 1], ahead, sems)
     parties, rows, width = message_ref.shape
     share = width // parties
     count = key_rows.shape[0]
     section, block = place
-    token_ref[...] = jnp.zeros_like(token_ref)
     left_ref[...] = matrix(gathered_ref, 1, share).astype(f32).T.astype(bf16)
     gate, up = matrix(gathered_ref, 0, share), matrix(gathered_ref, 2, share)
     for start in range(0, count, tile):
@@ -142,18 +143,16 @@
         back_ref[0, :, span] = (back * pre_up * slope).astype(bf16)
         back_ref[1, :, span] = (active * pre_up * rate).astype(bf16)
         back_ref[2, :, span] = (back * active).astype(bf16)
-    copies = []
-
-    def send(index, tiles):
-        part = pl.ds(index * share, share)
-        held_ref[:, index * share : (index + 1) * share, :] = tiles
-        copies.append(
-            pltpu.make_async_copy(
-                held_ref.at[:, part, :], message_ref.at[:, part, :], sems.at[index]
-            )
+    keys, values = key_rows[...], value_rows[...]
+    gradients = (
+        dot(back_ref[0], keys, NN),
+        -dot(back_ref[1], values, NN).T,
+        dot(back_ref[2], keys, NN),
+    )
+    for index, gradient in enumerate(gradients):
+        message_ref[:, index * share : (index + 1) * share, :] = gradient.astype(bf16).reshape(
+            parties, share, width
         )
-        copies[-1].start()
-
     if rows > 3 * share:
         row = lax.broadcasted_iota(jnp.int32, (share, width), 0)
         extra = jnp.zeros((share, width), f32)
@@ -165,41 +164,38 @@
             high = square.astype(bf16).astype(f32)
             extra = jnp.where(row == 2 * index, high, extra)
             extra = jnp.where(row == 2 * index + 1, square - high, extra)
-        send(3, jnp.broadcast_to(extra.astype(bf16)[None], (parties, share, width)))
-    keys, values = key_rows[...], value_rows[...]
-    shape = (parties, share, width)
-    send(1, -dot(back_ref[1], values, NN).T.astype(bf16).reshape(shape))
-    send(0, dot(back_ref[0], keys, NN).astype(bf16).reshape(shape))
-    send(2, dot(back_ref[2], keys, NN).astype(bf16).reshape(shape))
+        message_ref[:, 3 * share :, :] = jnp.broadcast_to(
+            extra.astype(bf16)[None], (parties, share, width)
+        )
     for copy in copies:
         copy.wait()
 
 
-def grads(gathered, rates, keys, values, place):
+def grads(gathered, rates, keys, values, place, ahead):
     parties, _, width = gathered.shape
     share = width // parties
     count = keys.shape[0]
     rows = (4 if place == (0, 0) else 3) * share
     return pl.pallas_call(
-        functools.partial(grads_kernel, place, 256),
-        in_specs=[VMEM] * 4,
-        out_specs=[HBM, VMEM],
-        out_shape=[jax.ShapeDtypeStruct((parties, rows, width), bf16), TOKEN],
+        functools.partial(grads_kernel, place, 256, [where for _, where in ahead]),
+        in_specs=[VMEM] * 4 + [HBM] * len(ahead),
+        out_specs=[VMEM] * (1 + len(ahead)),
+        out_shape=[in_vmem(parties, rows, width, dtype=bf16)]
+        + [rows_in_vmem(array) for array, _ in ahead],
         scratch_shapes=[
             pltpu.VMEM((width, width), bf16),
             pltpu.VMEM((3, width, count), bf16),
-            pltpu.VMEM((parties, rows, width), bf16),
-            pltpu.SemaphoreType.DMA((4,)),
+            pltpu.SemaphoreType.DMA((len(ahead),)),
         ],
         compiler_params=params(),
         cost_estimate=pl.CostEstimate(
             flops=12 * count * width * width, bytes_accessed=4 * count * width, transcendentals=0
         ),
         name="grads",
-    )(gathered, rates, keys, values)
-
-
-def update_kernel(index, *refs):
+    )(gathered, rates, keys, values, *(in_hbm(array) for array, _ in ahead))
+
+
+def update_kernel(index, waits, *refs):
     arrived_ref, weights_ref, moment_ref = refs[:3]
     refs = refs[3:]
     rows = weights_ref.shape[0]
@@ -219,11 +215,12 @@
     )
     weights = stepped * rescale
     rounded = weights.astype(bf16)
-    message_ref = refs[1]
+    refs = refs[waits:]
+    message_ref = refs[0]
     if len(message_ref.shape) == 3:
         message_ref[...] = jnp.broadcast_to(rounded[None], message_ref.shape)
-        refs[2][...] = weights
-        refs[3][...] = moment
+        refs[1][...] = weights
+        refs[2][...] = moment
     else:
         message_ref[:rows, :] = rounded
         message_ref[rows:, :] = moment.astype(bf16)
@@ -235,8 +232,10 @@
     if index > 0:
         given.append(squares)
         in_specs.append(VMEM)
-    given.append(token)
-    in_specs.append(VMEM)
+    waits = token is not None
+    if waits:
+        given.append(token)
+        in_specs.append(VMEM)
     if leaving:
         out_shape = [in_vmem(2 * rows, width, dtype=bf16)]
     else:
@@ -245,7 +244,7 @@
     if index == 0:
         out_shape.append(in_vmem(arrived.shape[1] - rows, width))
     return pl.pallas_call(
-        functools.partial(update_kernel, index),
+        functools.partial(update_kernel, index, waits),
         in_specs=in_specs,
         out_specs=[VMEM] * len(out_shape),
         out_shape=out_shape,
@@ -282,29 +281,23 @@
     )(first, passed, fresh_weights, fresh_moment)
 
 
-def apply_kernel(place, ahead, staged, aliased, parts, chosen, gathered_ref, query_ref, wait_ref, *refs):
-    count = len(ahead)
+def apply_kernel(place, staged, waits, chosen, parts, gathered_ref, query_ref, *refs):
+    refs = refs[waits:]
     if chosen:
-        other_ref, flag_ref = refs[:2]
-        refs = refs[2:]
-
-        gathered_ref = jnp.where(flag_ref[0] == 1, other_ref[...], gathered_ref[...])
-
-    sources, refs = refs[:count], refs[count + aliased :]
-    out_ref, token_ref, targets = refs[0], refs[1], refs[2 : 2 + count]
-    query_rows, held_ref, sems, ahead_sems = refs[2 + count :]
+        gathered_ref = jnp.where(refs[1][0] == 1, refs[0][...], gathered_ref[...])
+    out_ref, token_ref, query_rows, held_ref, sems = refs[-5:]
     token_ref[...] = jnp.zeros_like(token_ref)
     length, width = query_rows.shape
     share = width // gathered_ref.shape[0]
-    if not staged:
-        (first,) = started([query_ref], [query_rows], [place], sems.at[pl.ds(parts, 1)])
-    copies = started(sources, targets, ahead, ahead_sems)
-    if not staged:
-        first.wait()
-    rows_ref = query_ref if staged else query_rows
+    if staged:
+        query_rows = query_ref
+    else:
+        (copy,) = started([query_ref], [query_rows], [place], sems)
+        copy.wait()
     size = length // parts
+    copies = []
     for part in range(parts):
-        queries = rows_ref[part * size : (part + 1) * size, :]
+        queries = query_rows[part * size : (part + 1) * size, :]
         pre_gate = dot(queries, matrix(gathered_ref, 0, share), NT)
         pre_up = dot(queries, matrix(gathered_ref, 2, share), NT)
         hidden = (pre_gate * sigmoid(pre_gate) * pre_up).astype(bf16)
@@ -313,43 +306,40 @@
         ).astype(bf16)
         span = pl.ds(part * size, size)
         copies.append(
-            pltpu.make_async_copy(held_ref.at[span, :], out_ref.at[*place].at[span, :], sems.at[part])
+            pltpu.make_async_copy(
+                held_ref.at[span, :], out_ref.at[*place].at[span, :], sems.at[1 + part]
+            )
         )
         copies[-1].start()
     for copy in copies:
         copy.wait()
 
 
-def apply_fast(gathered, queries, place, results, shape, token, ahead=(), parts=1, instead=()):
+def apply_fast(gathered, queries, place, results, shape, token=None, parts=1, instead=()):
     count, width = shape[3:]
     staged = len(queries.shape) == 2
-    given = [gathered, queries if staged else in_hbm(queries), token]
-    given += [*instead, *(in_hbm(array) for array, _ in ahead)]
-    in_specs = [VMEM, VMEM if staged else HBM, VMEM]
-    in_specs += [VMEM, SMEM][: len(instead)] + [HBM] * len(ahead)
+    waits = token is not None
+    given = [gathered, queries if staged else in_hbm(queries)]
+    in_specs = [VMEM, VMEM if staged else HBM]
+    if waits:
+        given.append(token)
+        in_specs.append(VMEM)
+    if instead:
+        given += instead
+        in_specs += [VMEM, SMEM]
     if results is not None:
         given.append(results)
         in_specs.append(HBM)
     return pl.pallas_call(
-        functools.partial(
-            apply_kernel,
-            place,
-            [where for _, where in ahead],
-            staged,
-            int(results is not None),
-            parts,
-            bool(instead),
-        ),
+        functools.partial(apply_kernel, place, staged, waits, bool(instead), parts),
         in_specs=in_specs,
-        out_specs=[HBM] + [VMEM] * (1 + len(ahead)),
-        out_shape=[jax.ShapeDtypeStruct(shape, bf16), TOKEN]
-        + [rows_in_vmem(array) for array, _ in ahead],
+        out_specs=[HBM, VMEM],
+        out_shape=[jax.ShapeDtypeStruct(shape, bf16), TOKEN],
         input_output_aliases={} if results is None else {len(given) - 1: 0},
         scratch_shapes=[
             pltpu.VMEM((count, width), bf16),
             pltpu.VMEM((count, width), bf16),
-            pltpu.SemaphoreType.DMA((parts + 1,)),
-            pltpu.SemaphoreType.DMA((max(len(ahead), 1),)),
+            pltpu.SemaphoreType.DMA((1 + parts,)),
         ],
         compiler_params=params(),
         cost_estimate=pl.CostEstimate(
@@ -371,6 +361,19 @@
 def handed_back(array):
     length = lax.axis_size("seg")
     return lax.ppermute(array, "seg", [(i + 1, i) for i in range(length - 1)])
+
+
+def gathered_by_last(is_last, state, rows, parties):
+    width = state.shape[1]
+    message = pl.pallas_call(
+        copies_kernel,
+        in_specs=[VMEM],
+        out_specs=VMEM,
+        out_shape=in_vmem(parties, rows, width, dtype=bf16),
+        compiler_params=params(),
+        name="copies",
+    )(state)
+    return lax.cond(is_last, exchanged, lambda tiles: tiles, message)
 
 
 def columns_first(state):
@@ -397,52 +400,37 @@
     message, token = spread(weights, parties)
     *staged, _ = stage(token, places[0], (key_vectors, values))
     gathered = exchanged(message)
-    results = squares = left = owed = None
+    results = squares = owed = None
+    pending = []
     for index, place in enumerate(places):
         last = index == len(places) - 1
         leaving = not last and place[2] == blocks - 1
-        message, token = grads(gathered, token_rates, *staged, (place[0], place[2]))
-        arrived = exchanged(message)
         if last:
             ahead = ((queries, place),)
         else:
             ahead = ((key_vectors, places[index + 1]), (values, places[index + 1]))
-        if index == 0:
-            *staged, token = stage(token, places[1], (key_vectors, values))
-        elif left is not None:
-            handed, *staged, token = stage(
-                token, places[index + 1], (key_vectors, values), (gathered,)
-            )
-            back = handed_back(handed)
-            own = lax.cond(
-                is_last,
-                lambda mine: exchanged(jnp.broadcast_to(mine[None], (parties, *mine.shape))),
-                lambda mine: jnp.zeros((parties, *mine.shape), bf16),
-                left[:rows],
-            )
-            owed, left = (back, places[index - 1], own), None
-        else:
-            results, token, *staged = apply_fast(
-                gathered, queries, places[index - 1], results, shape, token, ahead
-            )
+        message, *staged = grads(
+            gathered, token_rates, *staged, (place[0], place[2]), ahead
+        )
+        arrived = exchanged(message)
+        token = None
+        if pending:
+            results, token = apply_fast(*pending.pop(), results, shape)
         message, *state = update(index, arrived, weights, moment, squares, token, leaving)
         if leaving:
-            left = message
+            own = gathered_by_last(is_last, message, rows, parties)
             weights, moment, message = enter(
                 first, passed_on(message), fresh_weights, fresh_moment, parties
             )
+            gathered = exchanged(message)
+            owed = (handed_back(gathered), queries, place)
         else:
             weights, moment, squares = (*state, squares)[:3]
-        gathered = exchanged(message)
-    results, token = apply_fast(
-        owed[0],
-        queries,
-        owed[1],
-        results,
-        shape,
-        weights,
-        instead=(owed[2], is_last.astype(jnp.int32).reshape(1)),
-    )
+            gathered = exchanged(message)
+            pending.append((gathered, queries, place))
+    pending.pop()
+    flag = is_last.astype(jnp.int32).reshape(1)
+    results, token = apply_fast(*owed, results, shape, weights, instead=(own, flag))
     results, _ = apply_fast(gathered, staged[0], places[-1], results, shape, token, parts=2)
     return (results, rows_first(weights, share)[None], rows_first(moment, share)[None])
 

time: 146 us -> 143 us (0.979)
  blocking collectives: 39.8 us -> 66.3 us
  waiting for transfers between devices: 45 us -> 27.6 us
  starting transfers between devices: 29.3 us -> 22.1 us
  Pallas kernels: 28.1 us -> 23.2 us
    all_to_all x3 -> x5, blocking collectives: 39.8 us -> 66.3 us  [exchanged(): return lax.all_to_all(tiles, TOK, split_axis=0, concat_axis=0, tiled=True)]
    all_to_all x6 -> x4, waiting for transfers between devices: 41.3 us -> 24.2 us  [exchanged(): return lax.all_to_all(tiles, TOK, split_axis=0, concat_axis=0, tiled=True)]
    all_to_all x6 -> x4, starting transfers between devices: 25.5 us -> 18.2 us  [exchanged(): return lax.all_to_all(tiles, TOK, split_axis=0, concat_axis=0, tiled=True)]
    pallas_call x3 -> x1, Pallas kernels: 4.53 us -> 1.9 us  [stage(): pl.pallas_call(functools.partial(stage_kernel, [place] * count), in_specs...]
    pallas_call x12 -> x13, Pallas kernels: 21.9 us -> 19.6 us  [the longest x4 10.5 us: apply_fast(): pl.pallas_call(functools.partial(apply_kernel, place, staged, waits, bool...]
  transfers between devices with their start and end apart: 8 -> 6, of which waited for: 7 -> 5; matrix products, arithmetic and copies ran while one was open for 1% -> 1% of each run, Pallas kernels for 10% -> 8%
where the time goes in v5:
time: 143 us; the launch traced here: 141 us
  blocking collectives  66.3 us (46%)
  waiting for transfers between devices  27.6 us (19%)
  Pallas kernels  23.2 us (16%)
  starting transfers between devices  22.1 us (15%)
    all_to_all x5, blocking collectives, exchanged(): return lax.all_to_all(tiles, TOK, split_axis=0, concat_axis=0, tiled=True)  66.3 us
    all_to_all x4, waiting for transfers between devices, exchanged(): return lax.all_to_all(tiles, TOK, split_axis=0, concat_axis=0, tiled=True)  24.2 us
    all_to_all x4, starting transfers between devices, exchanged(): return lax.all_to_all(tiles, TOK, split_axis=0, concat_axis=0, tiled=True)  18.2 us
    pallas_call x4, Pallas kernels, apply_fast(): pl.pallas_call(functools.partial(apply_kernel, place, staged, waits, bool...  10.5 us
    pallas_call x4, Pallas kernels, grads(): pl.pallas_call(functools.partial(grads_kernel, place, 256, [where for _,...  7.65 us
    ppermute x1, waiting for transfers between devices, passed_on(): return lax.ppermute(array, 'seg', [(i, i + 1) for i in range(length - 1)])  3.42 us
  transfers between devices with their start and end apart: 6, of which 5 were waited for; matrix products, arithmetic and copies ran while one was open for 1% of the time, Pallas kernels for 8%

profile of v5, /device:TPU:96, one launch (start us, length us, event | category | flops | bytes accessed | tf_op | source)
XLA Modules:
  0.0 141.2 jit_solution(15363471898628337950)
XLA Ops:
  0.6 1.6 %spread.1 = (bf16[16,48,256]{2,1,0:T(8,128)(2,1)}, f32[8,128]{1,0:T(8,128)S(1)}) custom-call(f32[48,256]{1,0:T(8,128)} %bitcast.30), custom_call_target="tpu_custom_call" | custom-call | tf_op jit(solution)/shard_map/spread/pallas_call | solution.py:81
  2.2 7.0 %all-to-all-start.1 = ((bf16[16,48,256]{2,1,0:T(8,128)(2,1)}), bf16[16,48,256]{2,1,0:T(8,128)(2,1)S(1)}, u32[]{:S(2)}, u32[]{:S(2)}) async-start(bf16[16,48,256]{2,1,0:T(8,128)(2,1)} %get-tuple-element.43), calls=%async_computation.1 | async-start | bytes 786432 | tf_op jit(solution)/shard_map/all_to_all | solution.py:353
  9.3 1.9 %stage.1 = (bf16[1280,256]{1,0:T(8,128)(2,1)S(1)}, bf16[1280,256]{1,0:T(8,128)(2,1)S(1)}, f32[8,128]{1,0:T(8,128)}) custom-call(f32[8,128]{1,0:T(8,128)S(1)} %get-tuple-element.44.refs_0_, bf16[2,1,2,1280,256]{4,3,2,1,0:T(8,128)(2,1)} %refs_0_.6, bf16[2,1,2,1280,256]{4,3,2,1,0:T(8,128)(2,1)} %refs_1_.7), custom_call_target="tpu_custom_call" | custom-call | bytes 2621440 | tf_op jit(solution)/shard_map/stage/pallas_call | solution.py:108
  11.2 7.9 %all-to-all-done.1.gathered_ref = bf16[16,48,256]{2,1,0:T(8,128)(2,1)S(1)} async-done(((bf16[16,48,256]{2,1,0:T(8,128)(2,1)}), bf16[16,48,256]{2,1,0:T(8,128)(2,1)S(1)}, u32[]{:S(2)}, u32[]{:S(2)}) %all-to-all-start.1) | async-done | bytes 393248 | tf_op jit(solution)/shard_map/all_to_all | solution.py:353
  20.6 13.8 %all_to_all.50.refs_0_ = bf16[16,64,256]{2,1,0:T(8,128)(2,1)S(1)} all-to-all(bf16[16,64,256]{2,1,0:T(8,128)(2,1)S(1)} %get-tuple-element.47), channel_id=1, replica_groups=mesh['seg'=16,'tok_0'=4,'tok_1'=4] {'tok_0','tok_1'}, dimensions={0} | all-to-all | bytes 1048576 | tf_op jit(solution)/shard_map/all_to_all | solution.py:353
  34.6 12.4 %all_to_all.51.gathered_ref = bf16[16,48,256]{2,1,0:T(8,128)(2,1)S(1)} all-to-all(bf16[16,48,256]{2,1,0:T(8,128)(2,1)S(1)} %get-tuple-element.48), channel_id=1, replica_groups=mesh['seg'=16,'tok_0'=4,'tok_1'=4] {'tok_0','tok_1'}, dimensions={0} | all-to-all | bytes 786432 | tf_op jit(solution)/shard_map/all_to_all | solution.py:353
  47.0 2.3 %grads.5 = (bf16[16,48,256]{2,1,0:T(8,128)(2,1)}, bf16[1280,256]{1,0:T(8,128)(2,1)S(1)}, bf16[1280,256]{1,0:T(8,128)(2,1)S(1)}) custom-call(bf16[16,48,256]{2,1,0:T(8,128)(2,1)S(1)} %all_to_all.51.gathered_ref, f32[2,1,2,1280]{3,2,1,0:T(2,128)S(1)} %copy-done, bf16[1280,256]{1,0:T(8,128)(2,1)S(1)} %get-tuple-element.49.key_rows, ...), custom_call_target="tpu_custom_call" | custom-call | flops 1006632960 | bytes 1310720 | tf_op jit(solution)/shard_map/grads/pallas_call | solution.py:179
  49.3 3.7 %all-to-all-start.4 = ((bf16[16,48,256]{2,1,0:T(8,128)(2,1)}), bf16[16,48,256]{2,1,0:T(8,128)(2,1)S(1)}, u32[]{:S(2)}, u32[]{:S(2)}) async-start(bf16[16,48,256]{2,1,0:T(8,128)(2,1)} %get-tuple-element.51), calls=%async_computation.4 | async-start | bytes 786432 | tf_op jit(solution)/shard_map/all_to_all | solution.py:353
  53.1 2.8 %apply.4 = (bf16[2,1,2,1280,256]{4,3,2,1,0:T(8,128)(2,1)}, f32[8,128]{1,0:T(8,128)S(1)}) custom-call(bf16[16,48,256]{2,1,0:T(8,128)(2,1)S(1)} %all_to_all.51.gathered_ref, bf16[2,1,2,1280,256]{4,3,2,1,0:T(8,128)(2,1)} %query_ref.5), custom_call_target="tpu_custom_call" | custom-call | flops 503316480 | bytes 1310720 | tf_op jit(solution)/shard_map/apply/pallas_call | solution.py:333
  55.9 6.3 %all-to-all-done.4.refs_0_ = bf16[16,48,256]{2,1,0:T(8,128)(2,1)S(1)} async-done(((bf16[16,48,256]{2,1,0:T(8,128)(2,1)}), bf16[16,48,256]{2,1,0:T(8,128)(2,1)S(1)}, u32[]{:S(2)}, u32[]{:S(2)}) %all-to-all-start.4) | async-done | bytes 393248 | tf_op jit(solution)/shard_map/all_to_all | solution.py:353
  62.4 1.9 %collective-permute-start = (bf16[96,256]{1,0:T(8,128)(2,1)S(1)}, bf16[96,256]{1,0:T(8,128)(2,1)S(1)}, u32[]{:S(2)}, u32[]{:S(2)}) collective-permute-start(bf16[96,256]{1,0:T(8,128)(2,1)S(1)} %update.5.state_ref), channel_id=1, source_target_pairs={{0,16},{16,32},{32,48},{48,64},{64,80},{80,96},{96,112},{112,128},... | collective-permute-start | bytes 147464 | tf_op jit(solution)/shard_map/ppermute | solution.py:358
  64.4 3.4 %collective-permute-done.passed_ref = bf16[96,256]{1,0:T(8,128)(2,1)S(1)} collective-permute-done((bf16[96,256]{1,0:T(8,128)(2,1)S(1)}, bf16[96,256]{1,0:T(8,128)(2,1)S(1)}, u32[]{:S(2)}, u32[]{:S(2)}) %collective-permute-start) | collective-permute-done | bytes 49184 | tf_op jit(solution)/shard_map/ppermute | solution.py:358
  67.8 14.6 %all_to_all.52.gathered_ref = bf16[16,48,256]{2,1,0:T(8,128)(2,1)S(1)} all-to-all(bf16[16,48,256]{2,1,0:T(8,128)(2,1)S(1)} %get-tuple-element.56), channel_id=1, replica_groups=mesh['seg'=16,'tok_0'=4,'tok_1'=4] {'tok_0','tok_1'}, dimensions={0} | all-to-all | bytes 786432 | tf_op jit(solution)/shard_map/all_to_all | solution.py:353
  83.9 12.9 %all_to_all.53.refs_0_ = bf16[16,48,256]{2,1,0:T(8,128)(2,1)S(1)} all-to-all(bf16[16,48,256]{2,1,0:T(8,128)(2,1)S(1)} %get-tuple-element.59), channel_id=1, replica_groups=mesh['seg'=16,'tok_0'=4,'tok_1'=4] {'tok_0','tok_1'}, dimensions={0} | all-to-all | bytes 786432 | tf_op jit(solution)/shard_map/all_to_all | solution.py:353
  96.9 12.6 %all_to_all.54.gathered_ref = bf16[16,48,256]{2,1,0:T(8,128)(2,1)S(1)} all-to-all(bf16[16,48,256]{2,1,0:T(8,128)(2,1)S(1)} %get-tuple-element.62), channel_id=1, replica_groups=mesh['seg'=16,'tok_0'=4,'tok_1'=4] {'tok_0','tok_1'}, dimensions={0} | all-to-all | bytes 786432 | tf_op jit(solution)/shard_map/all_to_all | solution.py:353
  109.6 2.3 %grads.7 = (bf16[16,48,256]{2,1,0:T(8,128)(2,1)}, bf16[1280,256]{1,0:T(8,128)(2,1)S(1)}) custom-call(bf16[16,48,256]{2,1,0:T(8,128)(2,1)S(1)} %all_to_all.54.gathered_ref, f32[2,1,2,1280]{3,2,1,0:T(2,128)S(1)} %copy-done, bf16[1280,256]{1,0:T(8,128)(2,1)S(1)} %get-tuple-element.63.key_rows, bf16[1280,256]{1,0:T(8,128)(2,1)S(1)} %get-tuple-element.64.value_rows, ...), custom_call_target="tpu_custom_call" | custom-call | flops 1006632960 | bytes 1310720 | tf_op jit(solution)/shard_map/grads/pallas_call | solution.py:179
  111.9 3.7 %all-to-all-start.8 = ((bf16[16,48,256]{2,1,0:T(8,128)(2,1)}), bf16[16,48,256]{2,1,0:T(8,128)(2,1)S(1)}, u32[]{:S(2)}, u32[]{:S(2)}) async-start(bf16[16,48,256]{2,1,0:T(8,128)(2,1)} %get-tuple-element.65), calls=%async_computation.8 | async-start | bytes 786432 | tf_op jit(solution)/shard_map/all_to_all | solution.py:353
  115.6 1.9 %collective-permute-start.1 = (bf16[16,48,256]{2,1,0:T(8,128)(2,1)S(1)}, bf16[16,48,256]{2,1,0:T(8,128)(2,1)S(1)}, u32[]{:S(2)}, u32[]{:S(2)}) collective-permute-start(bf16[16,48,256]{2,1,0:T(8,128)(2,1)S(1)} %all_to_all.52.gathered_ref), channel_id=1, source_target_pairs={{16,0},{32,16},{48,32},{64,48},{80,64},{96,80},{112,96},{128,112},... | collective-permute-start | bytes 1179656 | tf_op jit(solution)/shard_map/ppermute | solution.py:363
  117.6 2.8 %apply.5 = (bf16[2,1,2,1280,256]{4,3,2,1,0:T(8,128)(2,1)}, f32[8,128]{1,0:T(8,128)S(1)}) custom-call(bf16[16,48,256]{2,1,0:T(8,128)(2,1)S(1)} %all_to_all.54.gathered_ref, bf16[2,1,2,1280,256]{4,3,2,1,0:T(8,128)(2,1)} %query_ref.5, bf16[2,1,2,1280,256]{4,3,2,1,0:T(8,128)(2,1)} %get-tuple-element.68.refs_0_), custom_call_target="tpu_custom_call", output_to_operand_aliasing={{0}: (2, {})} | custom-call | flops 503316480 | bytes 1310720 | tf_op jit(solution)/shard_map/apply/pallas_call | solution.py:333
  120.4 4.4 %all-to-all-done.8.refs_0_ = bf16[16,48,256]{2,1,0:T(8,128)(2,1)S(1)} async-done(((bf16[16,48,256]{2,1,0:T(8,128)(2,1)}), bf16[16,48,256]{2,1,0:T(8,128)(2,1)S(1)}, u32[]{:S(2)}, u32[]{:S(2)}) %all-to-all-start.8) | async-done | bytes 393248 | tf_op jit(solution)/shard_map/all_to_all | solution.py:353
  125.7 3.7 %all-to-all-start.9 = ((bf16[16,48,256]{2,1,0:T(8,128)(2,1)}), bf16[16,48,256]{2,1,0:T(8,128)(2,1)S(1)}, u32[]{:S(2)}, u32[]{:S(2)}) async-start(bf16[16,48,256]{2,1,0:T(8,128)(2,1)} %get-tuple-element.70), calls=%async_computation.9 | async-start | bytes 786432 | tf_op jit(solution)/shard_map/all_to_all | solution.py:353
  130.7 2.8 %apply.6 = (bf16[2,1,2,1280,256]{4,3,2,1,0:T(8,128)(2,1)}, f32[8,128]{1,0:T(8,128)S(1)}) custom-call(bf16[16,48,256]{2,1,0:T(8,128)(2,1)S(1)} %collective-permute-done.1.gathered_ref, bf16[2,1,2,1280,256]{4,3,2,1,0:T(8,128)(2,1)} %query_ref.5, f32[48,256]{1,0:T(8,128)S(1)} %get-tuple-element.72.refs_0_, ...), custom_call_target="tpu_custom_call", output_to_operand_aliasing={{0}: (5, {})} | custom-call | flops 503316480 | bytes 1310720 | tf_op jit(solution)/shard_map/apply/pallas_call | solution.py:333
  133.4 5.6 %all-to-all-done.9.gathered_ref = bf16[16,48,256]{2,1,0:T(8,128)(2,1)S(1)} async-done(((bf16[16,48,256]{2,1,0:T(8,128)(2,1)}), bf16[16,48,256]{2,1,0:T(8,128)(2,1)S(1)}, u32[]{:S(2)}, u32[]{:S(2)}) %all-to-all-start.9) | async-done | bytes 393248 | tf_op jit(solution)/shard_map/all_to_all | solution.py:353
  139.0 2.2 %apply.7 = (bf16[2,1,2,1280,256]{4,3,2,1,0:T(8,128)(2,1)}, f32[8,128]{1,0:T(8,128)}) custom-call(bf16[16,48,256]{2,1,0:T(8,128)(2,1)S(1)} %all-to-all-done.9.gathered_ref, bf16[1280,256]{1,0:T(8,128)(2,1)S(1)} %get-tuple-element.71.query_ref, f32[8,128]{1,0:T(8,128)S(1)} %get-tuple-element.74.refs_0_, ...), custom_call_target="tpu_custom_call", output_to_operand_aliasing={{0}: (3, {})} | custom-call | flops 503316480 | bytes 1310720 | tf_op jit(solution)/shard_map/apply/pallas_call | solution.py:333
  (22 shorter events, 5.8 us)
Async XLA Ops:
  2.2 16.9 %all-to-all-start.1 = ((bf16[16,48,256]{2,1,0:T(8,128)(2,1)}), bf16[16,48,256]{2,1,0:T(8,128)(2,1)S(1)}, u32[]{:S(2)}, u32[]{:S(2)}) async-start(bf16[16,48,256]{2,1,0:T(8,128)(2,1)} %get-tuple-element.43), calls=%async_computation.1 | async-start | bytes 786432 | tf_op jit(solution)/shard_map/all_to_all | solution.py:353
  9.3 9.8 %copy-start = (f32[2,1,2,1280]{3,2,1,0:T(2,128)S(1)}, f32[2,1,2,1280]{3,2,1,0:T(2,128)}, u32[]{:S(2)}) copy-start(f32[2,1,2,1280]{3,2,1,0:T(2,128)} %rate_ref.7) | copy-start | bytes 61444
  19.1 15.3 %copy-start.1 = (f32[1,3,256,16]{2,3,1,0:T(8,128)S(1)}, f32[1,3,256,16]{2,3,1,0:T(8,128)}, u32[]{:S(2)}) copy-start(f32[1,3,256,16]{2,3,1,0:T(8,128)} %param.14) | copy-start | bytes 147460
  19.1 15.3 %copy-start.2 = (f32[1,3,256,16]{2,3,1,0:T(8,128)S(1)}, f32[1,3,256,16]{2,3,1,0:T(8,128)}, u32[]{:S(2)}) copy-start(f32[1,3,256,16]{2,3,1,0:T(8,128)} %param.15) | copy-start | bytes 147460
  49.3 12.9 %all-to-all-start.4 = ((bf16[16,48,256]{2,1,0:T(8,128)(2,1)}), bf16[16,48,256]{2,1,0:T(8,128)(2,1)S(1)}, u32[]{:S(2)}, u32[]{:S(2)}) async-start(bf16[16,48,256]{2,1,0:T(8,128)(2,1)} %get-tuple-element.51), calls=%async_computation.4 | async-start | bytes 786432 | tf_op jit(solution)/shard_map/all_to_all | solution.py:353
  53.1 14.7 %copy-start.3 = (f32[3,256,16]{1,2,0:T(8,128)S(1)}, f32[3,256,16]{1,2,0:T(8,128)}, u32[]{:S(2)}) copy-start(f32[3,256,16]{1,2,0:T(8,128)} %param.16) | copy-start | bytes 147460
  53.1 14.7 %copy-start.4 = (f32[3,256,16]{1,2,0:T(8,128)S(1)}, f32[3,256,16]{1,2,0:T(8,128)}, u32[]{:S(2)}) copy-start(f32[3,256,16]{1,2,0:T(8,128)} %param.17) | copy-start | bytes 147460
  62.4 5.4 %collective-permute-start = (bf16[96,256]{1,0:T(8,128)(2,1)S(1)}, bf16[96,256]{1,0:T(8,128)(2,1)S(1)}, u32[]{:S(2)}, u32[]{:S(2)}) collective-permute-start(bf16[96,256]{1,0:T(8,128)(2,1)S(1)} %update.5.state_ref), channel_id=1, source_target_pairs={{0,16},{16,32},{32,48},{48,64},{64,80},{80,96},{96,112},{112,128},... | collective-permute-start | bytes 147464 | tf_op jit(solution)/shard_map/ppermute | solution.py:358
  111.9 12.9 %all-to-all-start.8 = ((bf16[16,48,256]{2,1,0:T(8,128)(2,1)}), bf16[16,48,256]{2,1,0:T(8,128)(2,1)S(1)}, u32[]{:S(2)}, u32[]{:S(2)}) async-start(bf16[16,48,256]{2,1,0:T(8,128)(2,1)} %get-tuple-element.65), calls=%async_computation.8 | async-start | bytes 786432 | tf_op jit(solution)/shard_map/all_to_all | solution.py:353
  115.6 15.0 %collective-permute-start.1 = (bf16[16,48,256]{2,1,0:T(8,128)(2,1)S(1)}, bf16[16,48,256]{2,1,0:T(8,128)(2,1)S(1)}, u32[]{:S(2)}, u32[]{:S(2)}) collective-permute-start(bf16[16,48,256]{2,1,0:T(8,128)(2,1)S(1)} %all_to_all.52.gathered_ref), channel_id=1, source_target_pairs={{16,0},{32,16},{48,32},{64,48},{80,64},{96,80},{112,96},{128,112},... | collective-permute-start | bytes 1179656 | tf_op jit(solution)/shard_map/ppermute | solution.py:363
  125.7 13.3 %all-to-all-start.9 = ((bf16[16,48,256]{2,1,0:T(8,128)(2,1)}), bf16[16,48,256]{2,1,0:T(8,128)(2,1)S(1)}, u32[]{:S(2)}, u32[]{:S(2)}) async-start(bf16[16,48,256]{2,1,0:T(8,128)(2,1)} %get-tuple-element.70), calls=%async_computation.9 | async-start | bytes 786432 | tf_op jit(solution)/shard_map/all_to_all | solution.py:353

commit v6 on v5

--- a/solution.py
+++ b/solution.py
@@ -254,7 +254,14 @@
 
 
 def enter_kernel(
-    first_ref, passed_ref, fresh_weights_ref, fresh_moment_ref, weights_ref, moment_ref, message_ref
+    first_ref,
+    passed_ref,
+    fresh_weights_ref,
+    fresh_moment_ref,
+    wait_ref,
+    weights_ref,
+    moment_ref,
+    message_ref,
 ):
     rows = weights_ref.shape[0]
     first = first_ref[0] == 1
@@ -265,11 +272,11 @@
     message_ref[...] = jnp.broadcast_to(weights.astype(bf16)[None], message_ref.shape)
 
 
-def enter(first, passed, fresh_weights, fresh_moment, parties):
+def enter(first, passed, fresh_weights, fresh_moment, token, parties):
     rows, width = fresh_weights.shape
     return pl.pallas_call(
         enter_kernel,
-        in_specs=[SMEM] + [VMEM] * 3,
+        in_specs=[SMEM] + [VMEM] * 4,
         out_specs=[VMEM] * 3,
         out_shape=[
             in_vmem(rows, width),
@@ -278,7 +285,7 @@
         ],
         compiler_params=params(),
         name="enter",
-    )(first, passed, fresh_weights, fresh_moment)
+    )(first, passed, fresh_weights, fresh_moment, token)
 
 
 def apply_kernel(place, staged, waits, chosen, parts, gathered_ref, query_ref, *refs):
@@ -414,13 +421,15 @@
         )
         arrived = exchanged(message)
         token = None
-        if pending:
+        if pending and not leaving:
             results, token = apply_fast(*pending.pop(), results, shape)
         message, *state = update(index, arrived, weights, moment, squares, token, leaving)
         if leaving:
+            passed = passed_on(message)
+            results, token = apply_fast(*pending.pop(), results, shape, message)
             own = gathered_by_last(is_last, message, rows, parties)
             weights, moment, message = enter(
-                first, passed_on(message), fresh_weights, fresh_moment, parties
+                first, passed, fresh_weights, fresh_moment, token, parties
             )
             gathered = exchanged(message)
             owed = (handed_back(gathered), queries, place)

time: 143 us -> 143 us (level)
  blocking collectives: 66.3 us -> 80.3 us
  waiting for transfers between devices: 27.6 us -> 18.5 us
  starting transfers between devices: 22.1 us -> 18.5 us
    all_to_all x5 -> x6, blocking collectives: 66.3 us -> 80.3 us  [exchanged(): return lax.all_to_all(tiles, TOK, split_axis=0, concat_axis=0, tiled=True)]
    all_to_all x4 -> x3, waiting for transfers between devices: 24.2 us -> 17.9 us  [exchanged(): return lax.all_to_all(tiles, TOK, split_axis=0, concat_axis=0, tiled=True)]
    all_to_all x4 -> x3, starting transfers between devices: 18.2 us -> 14.5 us  [exchanged(): return lax.all_to_all(tiles, TOK, split_axis=0, concat_axis=0, tiled=True)]
    ppermute x1, waiting for transfers between devices: 3.42 us -> 0.64 us  [passed_on(): return lax.ppermute(array, 'seg', [(i, i + 1) for i in range(length - 1)])]
  transfers between devices with their start and end apart: 6 -> 5, of which waited for: 5 -> 4; matrix products, arithmetic and copies ran while one was open for 1% -> 1% of each run, Pallas kernels for 8% -> 8%
where the time goes in v6:
time: 143 us; the launch traced here: 142 us
  blocking collectives  80.3 us (56%)
  Pallas kernels  22.3 us (16%)
  starting transfers between devices  18.5 us (13%)
  waiting for transfers between devices  18.5 us (13%)
    all_to_all x6, blocking collectives, exchanged(): return lax.all_to_all(tiles, TOK, split_axis=0, concat_axis=0, tiled=True)  80.3 us
    all_to_all x3, waiting for transfers between devices, exchanged(): return lax.all_to_all(tiles, TOK, split_axis=0, concat_axis=0, tiled=True)  17.9 us
    all_to_all x3, starting transfers between devices, exchanged(): return lax.all_to_all(tiles, TOK, split_axis=0, concat_axis=0, tiled=True)  14.5 us
    pallas_call x4, Pallas kernels, apply_fast(): pl.pallas_call(functools.partial(apply_kernel, place, staged, waits, bool...  10.5 us
    pallas_call x4, Pallas kernels, grads(): pl.pallas_call(functools.partial(grads_kernel, place, 256, [where for _,...  6.89 us
  transfers between devices with their start and end apart: 5, of which 4 were waited for; matrix products, arithmetic and copies ran while one was open for 1% of the time, Pallas kernels for 8%

profile of v6, /device:TPU:96, one launch (start us, length us, event | category | flops | bytes accessed | tf_op | source)
XLA Modules:
  0.0 141.7 jit_solution(4532617222267504685)
XLA Ops:
  0.6 1.6 %spread.1 = (bf16[16,48,256]{2,1,0:T(8,128)(2,1)}, f32[8,128]{1,0:T(8,128)S(1)}) custom-call(f32[48,256]{1,0:T(8,128)} %bitcast.30), custom_call_target="tpu_custom_call" | custom-call | tf_op jit(solution)/shard_map/spread/pallas_call | solution.py:81
  2.2 7.0 %all-to-all-start.1 = ((bf16[16,48,256]{2,1,0:T(8,128)(2,1)}), bf16[16,48,256]{2,1,0:T(8,128)(2,1)S(1)}, u32[]{:S(2)}, u32[]{:S(2)}) async-start(bf16[16,48,256]{2,1,0:T(8,128)(2,1)} %get-tuple-element.43), calls=%async_computation.1 | async-start | bytes 786432 | tf_op jit(solution)/shard_map/all_to_all | solution.py:360
  9.3 1.9 %stage.1 = (bf16[1280,256]{1,0:T(8,128)(2,1)S(1)}, bf16[1280,256]{1,0:T(8,128)(2,1)S(1)}, f32[8,128]{1,0:T(8,128)}) custom-call(f32[8,128]{1,0:T(8,128)S(1)} %get-tuple-element.44.refs_0_, bf16[2,1,2,1280,256]{4,3,2,1,0:T(8,128)(2,1)} %refs_0_.6, bf16[2,1,2,1280,256]{4,3,2,1,0:T(8,128)(2,1)} %refs_1_.7), custom_call_target="tpu_custom_call" | custom-call | bytes 2621440 | tf_op jit(solution)/shard_map/stage/pallas_call | solution.py:108
  11.2 7.9 %all-to-all-done.1.gathered_ref = bf16[16,48,256]{2,1,0:T(8,128)(2,1)S(1)} async-done(((bf16[16,48,256]{2,1,0:T(8,128)(2,1)}), bf16[16,48,256]{2,1,0:T(8,128)(2,1)S(1)}, u32[]{:S(2)}, u32[]{:S(2)}) %all-to-all-start.1) | async-done | bytes 393248 | tf_op jit(solution)/shard_map/all_to_all | solution.py:360
  19.1 1.5 %grads.4 = (bf16[16,64,256]{2,1,0:T(8,128)(2,1)S(1)}, bf16[1280,256]{1,0:T(8,128)(2,1)S(1)}, bf16[1280,256]{1,0:T(8,128)(2,1)S(1)}) custom-call(bf16[16,48,256]{2,1,0:T(8,128)(2,1)S(1)} %all-to-all-done.1.gathered_ref, f32[2,1,2,1280]{3,2,1,0:T(2,128)S(1)} %copy-done, bf16[1280,256]{1,0:T(8,128)(2,1)S(1)} %get-tuple-element.45.key_rows, ...), custom_call_target="tpu_custom_call" | custom-call | flops 1006632960 | bytes 1310720 | tf_op jit(solution)/shard_map/grads/pallas_call | solution.py:179
  20.6 13.8 %all_to_all.50.refs_0_ = bf16[16,64,256]{2,1,0:T(8,128)(2,1)S(1)} all-to-all(bf16[16,64,256]{2,1,0:T(8,128)(2,1)S(1)} %get-tuple-element.47), channel_id=1, replica_groups=mesh['seg'=16,'tok_0'=4,'tok_1'=4] {'tok_0','tok_1'}, dimensions={0} | all-to-all | bytes 1048576 | tf_op jit(solution)/shard_map/all_to_all | solution.py:360
  34.6 12.4 %all_to_all.51.gathered_ref = bf16[16,48,256]{2,1,0:T(8,128)(2,1)S(1)} all-to-all(bf16[16,48,256]{2,1,0:T(8,128)(2,1)S(1)} %get-tuple-element.48), channel_id=1, replica_groups=mesh['seg'=16,'tok_0'=4,'tok_1'=4] {'tok_0','tok_1'}, dimensions={0} | all-to-all | bytes 786432 | tf_op jit(solution)/shard_map/all_to_all | solution.py:360
  47.0 1.6 %grads.5 = (bf16[16,48,256]{2,1,0:T(8,128)(2,1)S(1)}, bf16[1280,256]{1,0:T(8,128)(2,1)S(1)}, bf16[1280,256]{1,0:T(8,128)(2,1)S(1)}) custom-call(bf16[16,48,256]{2,1,0:T(8,128)(2,1)S(1)} %all_to_all.51.gathered_ref, f32[2,1,2,1280]{3,2,1,0:T(2,128)S(1)} %copy-done, bf16[1280,256]{1,0:T(8,128)(2,1)S(1)} %get-tuple-element.49.key_rows, ...), custom_call_target="tpu_custom_call" | custom-call | flops 1006632960 | bytes 1310720 | tf_op jit(solution)/shard_map/grads/pallas_call | solution.py:179
  48.6 12.6 %all_to_all.52.refs_0_ = bf16[16,48,256]{2,1,0:T(8,128)(2,1)S(1)} all-to-all(bf16[16,48,256]{2,1,0:T(8,128)(2,1)S(1)} %get-tuple-element.51), channel_id=1, replica_groups=mesh['seg'=16,'tok_0'=4,'tok_1'=4] {'tok_0','tok_1'}, dimensions={0} | all-to-all | bytes 786432 | tf_op jit(solution)/shard_map/all_to_all | solution.py:360
  61.4 2.1 %collective-permute-start = (bf16[96,256]{1,0:T(8,128)(2,1)S(1)}, bf16[96,256]{1,0:T(8,128)(2,1)S(1)}, u32[]{:S(2)}, u32[]{:S(2)}) collective-permute-start(bf16[96,256]{1,0:T(8,128)(2,1)S(1)} %update.5.refs_0_.state_ref), channel_id=1, source_target_pairs={{0,16},{16,32},{32,48},{48,64},{64,80},{80,96},{96,112},{112,128},... | collective-permute-start | bytes 147464 | tf_op jit(solution)/shard_map/ppermute | solution.py:365
  63.5 2.8 %apply.4 = (bf16[2,1,2,1280,256]{4,3,2,1,0:T(8,128)(2,1)}, f32[8,128]{1,0:T(8,128)S(1)}) custom-call(bf16[16,48,256]{2,1,0:T(8,128)(2,1)S(1)} %all_to_all.51.gathered_ref, bf16[2,1,2,1280,256]{4,3,2,1,0:T(8,128)(2,1)} %query_ref.5, bf16[96,256]{1,0:T(8,128)(2,1)S(1)} %update.5.refs_0_.state_ref), custom_call_target="tpu_custom_call" | custom-call | flops 503316480 | bytes 1310720 | tf_op jit(solution)/shard_map/apply/pallas_call | solution.py:340
  67.0 12.9 %all_to_all.53.gathered_ref = bf16[16,48,256]{2,1,0:T(8,128)(2,1)S(1)} all-to-all(bf16[16,48,256]{2,1,0:T(8,128)(2,1)S(1)} %get-tuple-element.56), channel_id=1, replica_groups=mesh['seg'=16,'tok_0'=4,'tok_1'=4] {'tok_0','tok_1'}, dimensions={0} | all-to-all | bytes 786432 | tf_op jit(solution)/shard_map/all_to_all | solution.py:360
  79.9 1.5 %grads.6 = (bf16[16,48,256]{2,1,0:T(8,128)(2,1)S(1)}, bf16[1280,256]{1,0:T(8,128)(2,1)S(1)}, bf16[1280,256]{1,0:T(8,128)(2,1)S(1)}) custom-call(bf16[16,48,256]{2,1,0:T(8,128)(2,1)S(1)} %all_to_all.53.gathered_ref, f32[2,1,2,1280]{3,2,1,0:T(2,128)S(1)} %copy-done, bf16[1280,256]{1,0:T(8,128)(2,1)S(1)} %get-tuple-element.57.key_rows, ...), custom_call_target="tpu_custom_call" | custom-call | flops 1006632960 | bytes 1310720 | tf_op jit(solution)/shard_map/grads/pallas_call | solution.py:179
  81.4 15.4 %all_to_all.54.refs_0_ = bf16[16,48,256]{2,1,0:T(8,128)(2,1)S(1)} all-to-all(bf16[16,48,256]{2,1,0:T(8,128)(2,1)S(1)} %get-tuple-element.59), channel_id=1, replica_groups=mesh['seg'=16,'tok_0'=4,'tok_1'=4] {'tok_0','tok_1'}, dimensions={0} | all-to-all | bytes 786432 | tf_op jit(solution)/shard_map/all_to_all | solution.py:360
  97.0 13.1 %all_to_all.55.gathered_ref = bf16[16,48,256]{2,1,0:T(8,128)(2,1)S(1)} all-to-all(bf16[16,48,256]{2,1,0:T(8,128)(2,1)S(1)} %get-tuple-element.62), channel_id=1, replica_groups=mesh['seg'=16,'tok_0'=4,'tok_1'=4] {'tok_0','tok_1'}, dimensions={0} | all-to-all | bytes 786432 | tf_op jit(solution)/shard_map/all_to_all | solution.py:360
  110.1 2.3 %grads.7 = (bf16[16,48,256]{2,1,0:T(8,128)(2,1)}, bf16[1280,256]{1,0:T(8,128)(2,1)S(1)}) custom-call(bf16[16,48,256]{2,1,0:T(8,128)(2,1)S(1)} %all_to_all.55.gathered_ref, f32[2,1,2,1280]{3,2,1,0:T(2,128)S(1)} %copy-done, bf16[1280,256]{1,0:T(8,128)(2,1)S(1)} %get-tuple-element.63.key_rows, bf16[1280,256]{1,0:T(8,128)(2,1)S(1)} %get-tuple-element.64.value_rows, ...), custom_call_target="tpu_custom_call" | custom-call | flops 1006632960 | bytes 1310720 | tf_op jit(solution)/shard_map/grads/pallas_call | solution.py:179
  112.5 3.7 %all-to-all-start.8 = ((bf16[16,48,256]{2,1,0:T(8,128)(2,1)}), bf16[16,48,256]{2,1,0:T(8,128)(2,1)S(1)}, u32[]{:S(2)}, u32[]{:S(2)}) async-start(bf16[16,48,256]{2,1,0:T(8,128)(2,1)} %get-tuple-element.65), calls=%async_computation.8 | async-start | bytes 786432 | tf_op jit(solution)/shard_map/all_to_all | solution.py:360
  116.2 1.9 %collective-permute-start.1 = (bf16[16,48,256]{2,1,0:T(8,128)(2,1)S(1)}, bf16[16,48,256]{2,1,0:T(8,128)(2,1)S(1)}, u32[]{:S(2)}, u32[]{:S(2)}) collective-permute-start(bf16[16,48,256]{2,1,0:T(8,128)(2,1)S(1)} %all_to_all.53.gathered_ref), channel_id=1, source_target_pairs={{16,0},{32,16},{48,32},{64,48},{80,64},{96,80},{112,96},{128,112},... | collective-permute-start | bytes 1179656 | tf_op jit(solution)/shard_map/ppermute | solution.py:370
  118.1 2.8 %apply.5 = (bf16[2,1,2,1280,256]{4,3,2,1,0:T(8,128)(2,1)}, f32[8,128]{1,0:T(8,128)S(1)}) custom-call(bf16[16,48,256]{2,1,0:T(8,128)(2,1)S(1)} %all_to_all.55.gathered_ref, bf16[2,1,2,1280,256]{4,3,2,1,0:T(8,128)(2,1)} %query_ref.5, bf16[2,1,2,1280,256]{4,3,2,1,0:T(8,128)(2,1)} %get-tuple-element.68.refs_0_), custom_call_target="tpu_custom_call", output_to_operand_aliasing={{0}: (2, {})} | custom-call | flops 503316480 | bytes 1310720 | tf_op jit(solution)/shard_map/apply/pallas_call | solution.py:340
  120.9 4.4 %all-to-all-done.8.refs_0_ = bf16[16,48,256]{2,1,0:T(8,128)(2,1)S(1)} async-done(((bf16[16,48,256]{2,1,0:T(8,128)(2,1)}), bf16[16,48,256]{2,1,0:T(8,128)(2,1)S(1)}, u32[]{:S(2)}, u32[]{:S(2)}) %all-to-all-start.8) | async-done | bytes 393248 | tf_op jit(solution)/shard_map/all_to_all | solution.py:360
  126.3 3.7 %all-to-all-start.9 = ((bf16[16,48,256]{2,1,0:T(8,128)(2,1)}), bf16[16,48,256]{2,1,0:T(8,128)(2,1)S(1)}, u32[]{:S(2)}, u32[]{:S(2)}) async-start(bf16[16,48,256]{2,1,0:T(8,128)(2,1)} %get-tuple-element.70), calls=%async_computation.9 | async-start | bytes 786432 | tf_op jit(solution)/shard_map/all_to_all | solution.py:360
  131.2 2.8 %apply.6 = (bf16[2,1,2,1280,256]{4,3,2,1,0:T(8,128)(2,1)}, f32[8,128]{1,0:T(8,128)S(1)}) custom-call(bf16[16,48,256]{2,1,0:T(8,128)(2,1)S(1)} %collective-permute-done.1.gathered_ref, bf16[2,1,2,1280,256]{4,3,2,1,0:T(8,128)(2,1)} %query_ref.5, f32[48,256]{1,0:T(8,128)S(1)} %get-tuple-element.72.refs_0_, ...), custom_call_target="tpu_custom_call", output_to_operand_aliasing={{0}: (5, {})} | custom-call | flops 503316480 | bytes 1310720 | tf_op jit(solution)/shard_map/apply/pallas_call | solution.py:340
  134.0 5.6 %all-to-all-done.9.gathered_ref = bf16[16,48,256]{2,1,0:T(8,128)(2,1)S(1)} async-done(((bf16[16,48,256]{2,1,0:T(8,128)(2,1)}), bf16[16,48,256]{2,1,0:T(8,128)(2,1)S(1)}, u32[]{:S(2)}, u32[]{:S(2)}) %all-to-all-start.9) | async-done | bytes 393248 | tf_op jit(solution)/shard_map/all_to_all | solution.py:360
  139.5 2.2 %apply.7 = (bf16[2,1,2,1280,256]{4,3,2,1,0:T(8,128)(2,1)}, f32[8,128]{1,0:T(8,128)}) custom-call(bf16[16,48,256]{2,1,0:T(8,128)(2,1)S(1)} %all-to-all-done.9.gathered_ref, bf16[1280,256]{1,0:T(8,128)(2,1)S(1)} %get-tuple-element.71.query_ref, f32[8,128]{1,0:T(8,128)S(1)} %get-tuple-element.74.refs_0_, ...), custom_call_target="tpu_custom_call", output_to_operand_aliasing={{0}: (3, {})} | custom-call | flops 503316480 | bytes 1310720 | tf_op jit(solution)/shard_map/apply/pallas_call | solution.py:340
  (21 shorter events, 3.4 us)
Async XLA Ops:
  2.2 16.9 %all-to-all-start.1 = ((bf16[16,48,256]{2,1,0:T(8,128)(2,1)}), bf16[16,48,256]{2,1,0:T(8,128)(2,1)S(1)}, u32[]{:S(2)}, u32[]{:S(2)}) async-start(bf16[16,48,256]{2,1,0:T(8,128)(2,1)} %get-tuple-element.43), calls=%async_computation.1 | async-start | bytes 786432 | tf_op jit(solution)/shard_map/all_to_all | solution.py:360
  9.3 9.8 %copy-start = (f32[2,1,2,1280]{3,2,1,0:T(2,128)S(1)}, f32[2,1,2,1280]{3,2,1,0:T(2,128)}, u32[]{:S(2)}) copy-start(f32[2,1,2,1280]{3,2,1,0:T(2,128)} %rate_ref.7) | copy-start | bytes 61444
  19.1 15.3 %copy-start.1 = (f32[1,3,256,16]{2,3,1,0:T(8,128)S(1)}, f32[1,3,256,16]{2,3,1,0:T(8,128)}, u32[]{:S(2)}) copy-start(f32[1,3,256,16]{2,3,1,0:T(8,128)} %param.14) | copy-start | bytes 147460
  19.1 15.3 %copy-start.2 = (f32[1,3,256,16]{2,3,1,0:T(8,128)S(1)}, f32[1,3,256,16]{2,3,1,0:T(8,128)}, u32[]{:S(2)}) copy-start(f32[1,3,256,16]{2,3,1,0:T(8,128)} %param.15) | copy-start | bytes 147460
  61.4 5.6 %copy-start.3 = (f32[3,256,16]{1,2,0:T(8,128)S(1)}, f32[3,256,16]{1,2,0:T(8,128)}, u32[]{:S(2)}) copy-start(f32[3,256,16]{1,2,0:T(8,128)} %param.16) | copy-start | bytes 147460
  61.4 5.6 %copy-start.4 = (f32[3,256,16]{1,2,0:T(8,128)S(1)}, f32[3,256,16]{1,2,0:T(8,128)}, u32[]{:S(2)}) copy-start(f32[3,256,16]{1,2,0:T(8,128)} %param.17) | copy-start | bytes 147460
  61.4 5.5 %collective-permute-start = (bf16[96,256]{1,0:T(8,128)(2,1)S(1)}, bf16[96,256]{1,0:T(8,128)(2,1)S(1)}, u32[]{:S(2)}, u32[]{:S(2)}) collective-permute-start(bf16[96,256]{1,0:T(8,128)(2,1)S(1)} %update.5.refs_0_.state_ref), channel_id=1, source_target_pairs={{0,16},{16,32},{32,48},{48,64},{64,80},{80,96},{96,112},{112,128},... | collective-permute-start | bytes 147464 | tf_op jit(solution)/shard_map/ppermute | solution.py:365
  112.5 12.9 %all-to-all-start.8 = ((bf16[16,48,256]{2,1,0:T(8,128)(2,1)}), bf16[16,48,256]{2,1,0:T(8,128)(2,1)S(1)}, u32[]{:S(2)}, u32[]{:S(2)}) async-start(bf16[16,48,256]{2,1,0:T(8,128)(2,1)} %get-tuple-element.65), calls=%async_computation.8 | async-start | bytes 786432 | tf_op jit(solution)/shard_map/all_to_all | solution.py:360
  116.2 15.0 %collective-permute-start.1 = (bf16[16,48,256]{2,1,0:T(8,128)(2,1)S(1)}, bf16[16,48,256]{2,1,0:T(8,128)(2,1)S(1)}, u32[]{:S(2)}, u32[]{:S(2)}) collective-permute-start(bf16[16,48,256]{2,1,0:T(8,128)(2,1)S(1)} %all_to_all.53.gathered_ref), channel_id=1, source_target_pairs={{16,0},{32,16},{48,32},{64,48},{80,64},{96,80},{112,96},{128,112},... | collective-permute-start | bytes 1179656 | tf_op jit(solution)/shard_map/ppermute | solution.py:370
  126.3 13.3 %all-to-all-start.9 = ((bf16[16,48,256]{2,1,0:T(8,128)(2,1)}), bf16[16,48,256]{2,1,0:T(8,128)(2,1)S(1)}, u32[]{:S(2)}, u32[]{:S(2)}) async-start(bf16[16,48,256]{2,1,0:T(8,128)(2,1)} %get-tuple-element.70), calls=%async_computation.9 | async-start | bytes 786432 | tf_op jit(solution)/shard_map/all_to_all | solution.py:360

commit v7 on v6

--- a/solution.py
+++ b/solution.py
@@ -97,17 +97,17 @@
 def stage_kernel(places, *refs):
     count = len(places)
     token_ref, sems = refs[-2:]
-    copies = started(refs[1 : 1 + count], refs[-2 - count : -2], places, sems)
+    copies = started(refs[2 : 2 + count], refs[-2 - count : -2], places, sems)
     token_ref[...] = jnp.zeros_like(token_ref)
     for copy in copies:
         copy.wait()
 
 
-def stage(token, place, arrays):
+def stage(token, who, place, arrays):
     count = len(arrays)
     return pl.pallas_call(
         functools.partial(stage_kernel, [place] * count),
-        in_specs=[VMEM] + [HBM] * count,
+        in_specs=[VMEM, SMEM] + [HBM] * count,
         out_specs=[VMEM] * (count + 1),
         out_shape=[rows_in_vmem(array) for array in arrays] + [TOKEN],
         scratch_shapes=[pltpu.SemaphoreType.DMA((count,))],
@@ -116,7 +116,7 @@
             flops=0, bytes_accessed=count * arrays[0].size, transcendentals=0
         ),
         name="stage",
-    )(token, *(in_hbm(array) for array in arrays))
+    )(token, who, *(in_hbm(array) for array in arrays))
 
 
 def grads_kernel(place, tile, ahead, gathered_ref, rate_ref, key_rows, value_rows, *refs):
@@ -264,7 +264,7 @@
     message_ref,
 ):
     rows = weights_ref.shape[0]
-    first = first_ref[0] == 1
+    first = first_ref[0] == 0
     passed = passed_ref[...].astype(f32)
     weights = jnp.where(first, fresh_weights_ref[...], passed[:rows])
     weights_ref[...] = weights
@@ -288,28 +288,21 @@
     )(first, passed, fresh_weights, fresh_moment, token)
 
 
-def apply_kernel(place, staged, waits, chosen, parts, gathered_ref, query_ref, *refs):
-    refs = refs[waits:]
-    if chosen:
-        gathered_ref = jnp.where(refs[1][0] == 1, refs[0][...], gathered_ref[...])
-    out_ref, token_ref, query_rows, held_ref, sems = refs[-5:]
-    token_ref[...] = jnp.zeros_like(token_ref)
+def apply_rows(place, parts, gathered, query_ref, query_rows, out_ref, held_ref, sems):
     length, width = query_rows.shape
-    share = width // gathered_ref.shape[0]
-    if staged:
-        query_rows = query_ref
-    else:
+    share = width // gathered.shape[0]
+    if query_ref is not query_rows:
         (copy,) = started([query_ref], [query_rows], [place], sems)
         copy.wait()
     size = length // parts
     copies = []
     for part in range(parts):
         queries = query_rows[part * size : (part + 1) * size, :]
-        pre_gate = dot(queries, matrix(gathered_ref, 0, share), NT)
-        pre_up = dot(queries, matrix(gathered_ref, 2, share), NT)
+        pre_gate = dot(queries, matrix(gathered, 0, share), NT)
+        pre_up = dot(queries, matrix(gathered, 2, share), NT)
         hidden = (pre_gate * sigmoid(pre_gate) * pre_up).astype(bf16)
         held_ref[part * size : (part + 1) * size, :] = dot(
-            hidden, matrix(gathered_ref, 1, share), NT
+            hidden, matrix(gathered, 1, share), NT
         ).astype(bf16)
         span = pl.ds(part * size, size)
         copies.append(
@@ -322,26 +315,58 @@
         copy.wait()
 
 
-def apply_fast(gathered, queries, place, results, shape, token=None, parts=1, instead=()):
+def apply_kernel(place, staged, waits, extra, when, aliased, hands, parts, gathered_ref, query_ref, *refs):
+    wait_ref, refs = (refs[0], refs[1:]) if waits else (None, refs)
+    extra_refs, refs = refs[: len(extra)], refs[len(extra) + aliased :]
+    out_ref, query_rows, held_ref, sems = refs[0], *refs[-3:]
+    if hands:
+        refs[1][...] = wait_ref[...] if waits else jnp.zeros_like(refs[1])
+    rows_ref = query_ref if staged else query_rows
+    if extra == ("instead", "who"):
+        gathered_ref = jnp.where(when(extra_refs[1][0]), extra_refs[0][...], gathered_ref[...])
+    if extra == ("who",):
+
+        @pl.when(when(extra_refs[0][0]))
+        def _():
+            apply_rows(place, parts, gathered_ref, query_ref, rows_ref, out_ref, held_ref, sems)
+
+    else:
+        apply_rows(place, parts, gathered_ref, query_ref, rows_ref, out_ref, held_ref, sems)
+
+
+def apply_fast(
+    gathered, queries, place, results, shape, token=None, parts=1, instead=None, who=None, when=None, hands=True
+):
     count, width = shape[3:]
     staged = len(queries.shape) == 2
     waits = token is not None
     given = [gathered, queries if staged else in_hbm(queries)]
     in_specs = [VMEM, VMEM if staged else HBM]
+    extra = ()
     if waits:
         given.append(token)
         in_specs.append(VMEM)
-    if instead:
-        given += instead
-        in_specs += [VMEM, SMEM]
+    if instead is not None:
+        given.append(instead)
+        in_specs.append(VMEM)
+        extra += ("instead",)
+    if who is not None:
+        given.append(who)
+        in_specs.append(SMEM)
+        extra += ("who",)
     if results is not None:
         given.append(results)
         in_specs.append(HBM)
-    return pl.pallas_call(
-        functools.partial(apply_kernel, place, staged, waits, bool(instead), parts),
+    out_shape = [jax.ShapeDtypeStruct(shape, bf16)]
+    if hands:
+        out_shape.append(in_vmem(*token.shape, dtype=token.dtype) if waits else TOKEN)
+    results, *handed = pl.pallas_call(
+        functools.partial(
+            apply_kernel, place, staged, waits, extra, when, int(results is not None), hands, parts
+        ),
         in_specs=in_specs,
-        out_specs=[HBM, VMEM],
-        out_shape=[jax.ShapeDtypeStruct(shape, bf16), TOKEN],
+        out_specs=[HBM] + [VMEM] * hands,
+        out_shape=out_shape,
         input_output_aliases={} if results is None else {len(given) - 1: 0},
         scratch_shapes=[
             pltpu.VMEM((count, width), bf16),
@@ -354,6 +379,7 @@
         ),
         name="apply",
     )(*given)
+    return (results, *handed)
 
 
 def exchanged(tiles):
@@ -398,14 +424,25 @@
     parties = lax.axis_size(TOK)
     share = fast_weights.shape[3]
     place_in_chain = lax.axis_index("seg")
-    first = (place_in_chain == 0).astype(jnp.int32).reshape(1)
-    is_last = place_in_chain == lax.axis_size("seg") - 1
+    who = place_in_chain.reshape(1)
+    length = lax.axis_size("seg")
+    is_last = place_in_chain == length - 1
+
+    def early(segment):
+        return (segment % 2 == 1) & (segment != length - 1)
+
+    def late(segment):
+        return (segment % 2 == 0) | (segment == length - 1)
+
+    def at_end(segment):
+        return segment == length - 1
+
     weights, moment = columns_first(fast_weights[0]), columns_first(momenta[0])
     fresh_weights, fresh_moment = columns_first(fresh_weights), columns_first(fresh_momenta)
     rows, shape = weights.shape[0], queries.shape
     places = [(section, 0, block) for section in range(sections) for block in range(blocks)]
     message, token = spread(weights, parties)
-    *staged, _ = stage(token, places[0], (key_vectors, values))
+    *staged, _ = stage(token, who, places[0], (key_vectors, values))
     gathered = exchanged(message)
     results = squares = owed = None
     pending = []
@@ -425,11 +462,13 @@
             results, token = apply_fast(*pending.pop(), results, shape)
         message, *state = update(index, arrived, weights, moment, squares, token, leaving)
         if leaving:
+            here = pending.pop()
+            results, message = apply_fast(*here, results, shape, message, who=who, when=early)
             passed = passed_on(message)
-            results, token = apply_fast(*pending.pop(), results, shape, message)
+            results, token = apply_fast(*here, results, shape, message, who=who, when=late)
             own = gathered_by_last(is_last, message, rows, parties)
             weights, moment, message = enter(
-                first, passed, fresh_weights, fresh_moment, token, parties
+                who, passed, fresh_weights, fresh_moment, token, parties
             )
             gathered = exchanged(message)
             owed = (handed_back(gathered), queries, place)
@@ -438,9 +477,10 @@
             gathered = exchanged(message)
             pending.append((gathered, queries, place))
     pending.pop()
-    flag = is_last.astype(jnp.int32).reshape(1)
-    results, token = apply_fast(*owed, results, shape, weights, instead=(own, flag))
-    results, _ = apply_fast(gathered, staged[0], places[-1], results, shape, token, parts=2)
+    results, token = apply_fast(*owed, results, shape, weights, instead=own, who=who, when=at_end)
+    (results,) = apply_fast(
+        gathered, staged[0], places[-1], results, shape, token, parts=2, hands=False
+    )
     return (results, rows_first(weights, share)[None], rows_first(moment, share)[None])
 
 

time: 143 us -> 141 us (0.986)
    pallas_call x4 -> x5, Pallas kernels: 10.5 us -> 9.93 us  [apply_fast(): pl.pallas_call(functools.partial(apply_kernel, place, staged, waits, extr...]
where the time goes in v7:
time: 141 us; the launch traced here: 140 us
  blocking collectives  78.9 us (56%)
  Pallas kernels  21.8 us (15%)
  waiting for transfers between devices  18.5 us (13%)
  starting transfers between devices  18.3 us (13%)
    all_to_all x6, blocking collectives, exchanged(): return lax.all_to_all(tiles, TOK, split_axis=0, concat_axis=0, tiled=True)  78.9 us
    all_to_all x3, waiting for transfers between devices, exchanged(): return lax.all_to_all(tiles, TOK, split_axis=0, concat_axis=0, tiled=True)  17.9 us
    all_to_all x3, starting transfers between devices, exchanged(): return lax.all_to_all(tiles, TOK, split_axis=0, concat_axis=0, tiled=True)  14.5 us
    pallas_call x5, Pallas kernels, apply_fast(): pl.pallas_call(functools.partial(apply_kernel, place, staged, waits, extr...  9.93 us
    pallas_call x4, Pallas kernels, grads(): pl.pallas_call(functools.partial(grads_kernel, place, 256, [where for _,...  6.87 us
  transfers between devices with their start and end apart: 5, of which 4 were waited for; matrix products, arithmetic and copies ran while one was open for 1% of the time, Pallas kernels for 8%

profile of v7, /device:TPU:96, one launch (start us, length us, event | category | flops | bytes accessed | tf_op | source)
XLA Modules:
  0.0 139.6 jit_solution(16708879370723592375)
XLA Ops:
  0.6 1.6 %spread.1 = (bf16[16,48,256]{2,1,0:T(8,128)(2,1)}, f32[8,128]{1,0:T(8,128)S(1)}) custom-call(f32[48,256]{1,0:T(8,128)} %bitcast.29), custom_call_target="tpu_custom_call" | custom-call | tf_op jit(solution)/shard_map/spread/pallas_call | solution.py:81
  2.2 7.0 %all-to-all-start.1 = ((bf16[16,48,256]{2,1,0:T(8,128)(2,1)}), bf16[16,48,256]{2,1,0:T(8,128)(2,1)S(1)}, u32[]{:S(2)}, u32[]{:S(2)}) async-start(bf16[16,48,256]{2,1,0:T(8,128)(2,1)} %get-tuple-element.44), calls=%async_computation.1 | async-start | bytes 786432 | tf_op jit(solution)/shard_map/all_to_all | solution.py:386
  9.3 1.9 %stage.1 = (bf16[1280,256]{1,0:T(8,128)(2,1)S(1)}, bf16[1280,256]{1,0:T(8,128)(2,1)S(1)}, f32[8,128]{1,0:T(8,128)}) custom-call(f32[8,128]{1,0:T(8,128)S(1)} %get-tuple-element.45.refs_0_, s32[1]{0:T(128)} %bitcast.refs_1_.first_ref.refs_2_, bf16[2,1,2,1280,256]{4,3,2,1,0:T(8,128)(2,1)} %refs_0_.6, bf16[2,1,2,1280,256]{4,3,2,1,0:T(8,128)(2,1)} %refs_1_.5), custom_call_target="tpu_custom_call" | custom-call | bytes 2621440 | tf_op jit(solution)/shard_map/stage/pallas_call | solution.py:108
  11.2 7.9 %all-to-all-done.1.gathered_ref = bf16[16,48,256]{2,1,0:T(8,128)(2,1)S(1)} async-done(((bf16[16,48,256]{2,1,0:T(8,128)(2,1)}), bf16[16,48,256]{2,1,0:T(8,128)(2,1)S(1)}, u32[]{:S(2)}, u32[]{:S(2)}) %all-to-all-start.1) | async-done | bytes 393248 | tf_op jit(solution)/shard_map/all_to_all | solution.py:386
  19.1 1.5 %grads.4 = (bf16[16,64,256]{2,1,0:T(8,128)(2,1)S(1)}, bf16[1280,256]{1,0:T(8,128)(2,1)S(1)}, bf16[1280,256]{1,0:T(8,128)(2,1)S(1)}) custom-call(bf16[16,48,256]{2,1,0:T(8,128)(2,1)S(1)} %all-to-all-done.1.gathered_ref, f32[2,1,2,1280]{3,2,1,0:T(2,128)S(1)} %copy-done, bf16[1280,256]{1,0:T(8,128)(2,1)S(1)} %get-tuple-element.46.key_rows, ...), custom_call_target="tpu_custom_call" | custom-call | flops 1006632960 | bytes 1310720 | tf_op jit(solution)/shard_map/grads/pallas_call | solution.py:179
  20.6 13.8 %all_to_all.50.refs_0_ = bf16[16,64,256]{2,1,0:T(8,128)(2,1)S(1)} all-to-all(bf16[16,64,256]{2,1,0:T(8,128)(2,1)S(1)} %get-tuple-element.48), channel_id=1, replica_groups=mesh['seg'=16,'tok_0'=4,'tok_1'=4] {'tok_0','tok_1'}, dimensions={0} | all-to-all | bytes 1048576 | tf_op jit(solution)/shard_map/all_to_all | solution.py:386
  34.6 12.4 %all_to_all.51.gathered_ref = bf16[16,48,256]{2,1,0:T(8,128)(2,1)S(1)} all-to-all(bf16[16,48,256]{2,1,0:T(8,128)(2,1)S(1)} %get-tuple-element.49), channel_id=1, replica_groups=mesh['seg'=16,'tok_0'=4,'tok_1'=4] {'tok_0','tok_1'}, dimensions={0} | all-to-all | bytes 786432 | tf_op jit(solution)/shard_map/all_to_all | solution.py:386
  47.0 1.6 %grads.5 = (bf16[16,48,256]{2,1,0:T(8,128)(2,1)S(1)}, bf16[1280,256]{1,0:T(8,128)(2,1)S(1)}, bf16[1280,256]{1,0:T(8,128)(2,1)S(1)}) custom-call(bf16[16,48,256]{2,1,0:T(8,128)(2,1)S(1)} %all_to_all.51.gathered_ref, f32[2,1,2,1280]{3,2,1,0:T(2,128)S(1)} %copy-done, bf16[1280,256]{1,0:T(8,128)(2,1)S(1)} %get-tuple-element.50.key_rows, ...), custom_call_target="tpu_custom_call" | custom-call | flops 1006632960 | bytes 1310720 | tf_op jit(solution)/shard_map/grads/pallas_call | solution.py:179
  48.6 12.6 %all_to_all.52.refs_0_ = bf16[16,48,256]{2,1,0:T(8,128)(2,1)S(1)} all-to-all(bf16[16,48,256]{2,1,0:T(8,128)(2,1)S(1)} %get-tuple-element.52), channel_id=1, replica_groups=mesh['seg'=16,'tok_0'=4,'tok_1'=4] {'tok_0','tok_1'}, dimensions={0} | all-to-all | bytes 786432 | tf_op jit(solution)/shard_map/all_to_all | solution.py:386
  61.4 1.9 %collective-permute-start = (bf16[96,256]{1,0:T(8,128)(2,1)S(1)}, bf16[96,256]{1,0:T(8,128)(2,1)S(1)}, u32[]{:S(2)}, u32[]{:S(2)}) collective-permute-start(bf16[96,256]{1,0:T(8,128)(2,1)S(1)} %get-tuple-element.56.refs_0_.state_ref), channel_id=1, source_target_pairs={{0,16},{16,32},{32,48},{48,64},{64,80},{80,96},{96,112},{112,128},... | collective-permute-start | bytes 147464 | tf_op jit(solution)/shard_map/ppermute | solution.py:391
  63.4 2.8 %apply.6 = (bf16[2,1,2,1280,256]{4,3,2,1,0:T(8,128)(2,1)}, bf16[96,256]{1,0:T(8,128)(2,1)S(1)}) custom-call(bf16[16,48,256]{2,1,0:T(8,128)(2,1)S(1)} %all_to_all.51.gathered_ref, bf16[2,1,2,1280,256]{4,3,2,1,0:T(8,128)(2,1)} %query_ref.7, bf16[96,256]{1,0:T(8,128)(2,1)S(1)} %get-tuple-element.56.refs_0_.state_ref, ...), custom_call_target="tpu_custom_call", output_to_operand_aliasing={{0}: (4, {})} | custom-call | flops 503316480 | bytes 1310720 | tf_op jit(solution)/shard_map/apply/pallas_call | solution.py:363
  66.9 14.6 %all_to_all.53.gathered_ref = bf16[16,48,256]{2,1,0:T(8,128)(2,1)S(1)} all-to-all(bf16[16,48,256]{2,1,0:T(8,128)(2,1)S(1)} %get-tuple-element.59), channel_id=1, replica_groups=mesh['seg'=16,'tok_0'=4,'tok_1'=4] {'tok_0','tok_1'}, dimensions={0} | all-to-all | bytes 786432 | tf_op jit(solution)/shard_map/all_to_all | solution.py:386
  81.4 1.5 %grads.6 = (bf16[16,48,256]{2,1,0:T(8,128)(2,1)S(1)}, bf16[1280,256]{1,0:T(8,128)(2,1)S(1)}, bf16[1280,256]{1,0:T(8,128)(2,1)S(1)}) custom-call(bf16[16,48,256]{2,1,0:T(8,128)(2,1)S(1)} %all_to_all.53.gathered_ref, f32[2,1,2,1280]{3,2,1,0:T(2,128)S(1)} %copy-done, bf16[1280,256]{1,0:T(8,128)(2,1)S(1)} %get-tuple-element.60.key_rows, ...), custom_call_target="tpu_custom_call" | custom-call | flops 1006632960 | bytes 1310720 | tf_op jit(solution)/shard_map/grads/pallas_call | solution.py:179
  82.9 12.9 %all_to_all.54.refs_0_ = bf16[16,48,256]{2,1,0:T(8,128)(2,1)S(1)} all-to-all(bf16[16,48,256]{2,1,0:T(8,128)(2,1)S(1)} %get-tuple-element.62), channel_id=1, replica_groups=mesh['seg'=16,'tok_0'=4,'tok_1'=4] {'tok_0','tok_1'}, dimensions={0} | all-to-all | bytes 786432 | tf_op jit(solution)/shard_map/all_to_all | solution.py:386
  96.0 12.6 %all_to_all.55.gathered_ref = bf16[16,48,256]{2,1,0:T(8,128)(2,1)S(1)} all-to-all(bf16[16,48,256]{2,1,0:T(8,128)(2,1)S(1)} %get-tuple-element.65), channel_id=1, replica_groups=mesh['seg'=16,'tok_0'=4,'tok_1'=4] {'tok_0','tok_1'}, dimensions={0} | all-to-all | bytes 786432 | tf_op jit(solution)/shard_map/all_to_all | solution.py:386
  108.6 2.3 %grads.7 = (bf16[16,48,256]{2,1,0:T(8,128)(2,1)}, bf16[1280,256]{1,0:T(8,128)(2,1)S(1)}) custom-call(bf16[16,48,256]{2,1,0:T(8,128)(2,1)S(1)} %all_to_all.55.gathered_ref, f32[2,1,2,1280]{3,2,1,0:T(2,128)S(1)} %copy-done, bf16[1280,256]{1,0:T(8,128)(2,1)S(1)} %get-tuple-element.66.key_rows, bf16[1280,256]{1,0:T(8,128)(2,1)S(1)} %get-tuple-element.67.value_rows, ...), custom_call_target="tpu_custom_call" | custom-call | flops 1006632960 | bytes 1310720 | tf_op jit(solution)/shard_map/grads/pallas_call | solution.py:179
  110.9 3.7 %all-to-all-start.8 = ((bf16[16,48,256]{2,1,0:T(8,128)(2,1)}), bf16[16,48,256]{2,1,0:T(8,128)(2,1)S(1)}, u32[]{:S(2)}, u32[]{:S(2)}) async-start(bf16[16,48,256]{2,1,0:T(8,128)(2,1)} %get-tuple-element.68), calls=%async_computation.8 | async-start | bytes 786432 | tf_op jit(solution)/shard_map/all_to_all | solution.py:386
  114.7 1.9 %collective-permute-start.1 = (bf16[16,48,256]{2,1,0:T(8,128)(2,1)S(1)}, bf16[16,48,256]{2,1,0:T(8,128)(2,1)S(1)}, u32[]{:S(2)}, u32[]{:S(2)}) collective-permute-start(bf16[16,48,256]{2,1,0:T(8,128)(2,1)S(1)} %all_to_all.53.gathered_ref), channel_id=1, source_target_pairs={{16,0},{32,16},{48,32},{64,48},{80,64},{96,80},{112,96},{128,112},... | collective-permute-start | bytes 1179656 | tf_op jit(solution)/shard_map/ppermute | solution.py:396
  116.6 2.8 %apply.7 = (bf16[2,1,2,1280,256]{4,3,2,1,0:T(8,128)(2,1)}, f32[8,128]{1,0:T(8,128)S(1)}) custom-call(bf16[16,48,256]{2,1,0:T(8,128)(2,1)S(1)} %all_to_all.55.gathered_ref, bf16[2,1,2,1280,256]{4,3,2,1,0:T(8,128)(2,1)} %query_ref.7, bf16[2,1,2,1280,256]{4,3,2,1,0:T(8,128)(2,1)} %get-tuple-element.71.refs_0_), custom_call_target="tpu_custom_call", output_to_operand_aliasing={{0}: (2, {})} | custom-call | flops 503316480 | bytes 1310720 | tf_op jit(solution)/shard_map/apply/pallas_call | solution.py:363
  119.4 4.4 %all-to-all-done.8.refs_0_ = bf16[16,48,256]{2,1,0:T(8,128)(2,1)S(1)} async-done(((bf16[16,48,256]{2,1,0:T(8,128)(2,1)}), bf16[16,48,256]{2,1,0:T(8,128)(2,1)S(1)}, u32[]{:S(2)}, u32[]{:S(2)}) %all-to-all-start.8) | async-done | bytes 393248 | tf_op jit(solution)/shard_map/all_to_all | solution.py:386
  124.7 3.7 %all-to-all-start.9 = ((bf16[16,48,256]{2,1,0:T(8,128)(2,1)}), bf16[16,48,256]{2,1,0:T(8,128)(2,1)S(1)}, u32[]{:S(2)}, u32[]{:S(2)}) async-start(bf16[16,48,256]{2,1,0:T(8,128)(2,1)} %get-tuple-element.73), calls=%async_computation.9 | async-start | bytes 786432 | tf_op jit(solution)/shard_map/all_to_all | solution.py:386
  129.7 2.8 %apply.8 = (bf16[2,1,2,1280,256]{4,3,2,1,0:T(8,128)(2,1)}, f32[48,256]{1,0:T(8,128)S(1)}) custom-call(bf16[16,48,256]{2,1,0:T(8,128)(2,1)S(1)} %collective-permute-done.1.gathered_ref, bf16[2,1,2,1280,256]{4,3,2,1,0:T(8,128)(2,1)} %query_ref.7, f32[48,256]{1,0:T(8,128)S(1)} %get-tuple-element.75.refs_0_, ...), custom_call_target="tpu_custom_call", output_to_operand_aliasing={{0}: (5, {})} | custom-call | flops 503316480 | bytes 1310720 | tf_op jit(solution)/shard_map/apply/pallas_call | solution.py:363
  132.5 5.6 %all-to-all-done.9.gathered_ref = bf16[16,48,256]{2,1,0:T(8,128)(2,1)S(1)} async-done(((bf16[16,48,256]{2,1,0:T(8,128)(2,1)}), bf16[16,48,256]{2,1,0:T(8,128)(2,1)S(1)}, u32[]{:S(2)}, u32[]{:S(2)}) %all-to-all-start.9) | async-done | bytes 393248 | tf_op jit(solution)/shard_map/all_to_all | solution.py:386
  138.0 1.6 %apply.9 = bf16[2,1,2,1280,256]{4,3,2,1,0:T(8,128)(2,1)} custom-call(bf16[16,48,256]{2,1,0:T(8,128)(2,1)S(1)} %all-to-all-done.9.gathered_ref, bf16[1280,256]{1,0:T(8,128)(2,1)S(1)} %get-tuple-element.74.query_ref, f32[48,256]{1,0:T(8,128)S(1)} %get-tuple-element.77.refs_0_, ...), custom_call_target="tpu_custom_call", output_to_operand_aliasing={{}: (3, {})} | custom-call | flops 503316480 | bytes 1310720 | tf_op jit(solution)/shard_map/apply/pallas_call | solution.py:363
  (22 shorter events, 3.4 us)
Async XLA Ops:
  2.2 16.9 %all-to-all-start.1 = ((bf16[16,48,256]{2,1,0:T(8,128)(2,1)}), bf16[16,48,256]{2,1,0:T(8,128)(2,1)S(1)}, u32[]{:S(2)}, u32[]{:S(2)}) async-start(bf16[16,48,256]{2,1,0:T(8,128)(2,1)} %get-tuple-element.44), calls=%async_computation.1 | async-start | bytes 786432 | tf_op jit(solution)/shard_map/all_to_all | solution.py:386
  9.3 9.8 %copy-start = (f32[2,1,2,1280]{3,2,1,0:T(2,128)S(1)}, f32[2,1,2,1280]{3,2,1,0:T(2,128)}, u32[]{:S(2)}) copy-start(f32[2,1,2,1280]{3,2,1,0:T(2,128)} %rate_ref.7) | copy-start | bytes 61444
  19.1 15.3 %copy-start.1 = (f32[1,3,256,16]{2,3,1,0:T(8,128)S(1)}, f32[1,3,256,16]{2,3,1,0:T(8,128)}, u32[]{:S(2)}) copy-start(f32[1,3,256,16]{2,3,1,0:T(8,128)} %param.14) | copy-start | bytes 147460
  19.1 15.3 %copy-start.2 = (f32[1,3,256,16]{2,3,1,0:T(8,128)S(1)}, f32[1,3,256,16]{2,3,1,0:T(8,128)}, u32[]{:S(2)}) copy-start(f32[1,3,256,16]{2,3,1,0:T(8,128)} %param.15) | copy-start | bytes 147460
  61.4 5.4 %collective-permute-start = (bf16[96,256]{1,0:T(8,128)(2,1)S(1)}, bf16[96,256]{1,0:T(8,128)(2,1)S(1)}, u32[]{:S(2)}, u32[]{:S(2)}) collective-permute-start(bf16[96,256]{1,0:T(8,128)(2,1)S(1)} %get-tuple-element.56.refs_0_.state_ref), channel_id=1, source_target_pairs={{0,16},{16,32},{32,48},{48,64},{64,80},{80,96},{96,112},{112,128},... | collective-permute-start | bytes 147464 | tf_op jit(solution)/shard_map/ppermute | solution.py:391
  63.4 3.4 %copy-start.3 = (f32[3,256,16]{1,2,0:T(8,128)S(1)}, f32[3,256,16]{1,2,0:T(8,128)}, u32[]{:S(2)}) copy-start(f32[3,256,16]{1,2,0:T(8,128)} %param.16) | copy-start | bytes 147460
  63.4 3.4 %copy-start.4 = (f32[3,256,16]{1,2,0:T(8,128)S(1)}, f32[3,256,16]{1,2,0:T(8,128)}, u32[]{:S(2)}) copy-start(f32[3,256,16]{1,2,0:T(8,128)} %param.17) | copy-start | bytes 147460
  110.9 12.9 %all-to-all-start.8 = ((bf16[16,48,256]{2,1,0:T(8,128)(2,1)}), bf16[16,48,256]{2,1,0:T(8,128)(2,1)S(1)}, u32[]{:S(2)}, u32[]{:S(2)}) async-start(bf16[16,48,256]{2,1,0:T(8,128)(2,1)} %get-tuple-element.68), calls=%async_computation.8 | async-start | bytes 786432 | tf_op jit(solution)/shard_map/all_to_all | solution.py:386
  114.7 15.0 %collective-permute-start.1 = (bf16[16,48,256]{2,1,0:T(8,128)(2,1)S(1)}, bf16[16,48,256]{2,1,0:T(8,128)(2,1)S(1)}, u32[]{:S(2)}, u32[]{:S(2)}) collective-permute-start(bf16[16,48,256]{2,1,0:T(8,128)(2,1)S(1)} %all_to_all.53.gathered_ref), channel_id=1, source_target_pairs={{16,0},{32,16},{48,32},{64,48},{80,64},{96,80},{112,96},{128,112},... | collective-permute-start | bytes 1179656 | tf_op jit(solution)/shard_map/ppermute | solution.py:396
  124.7 13.3 %all-to-all-start.9 = ((bf16[16,48,256]{2,1,0:T(8,128)(2,1)}), bf16[16,48,256]{2,1,0:T(8,128)(2,1)S(1)}, u32[]{:S(2)}, u32[]{:S(2)}) async-start(bf16[16,48,256]{2,1,0:T(8,128)(2,1)} %get-tuple-element.73), calls=%async_computation.9 | async-start | bytes 786432 | tf_op jit(solution)/shard_map/all_to_all | solution.py:386

commit v8 on v7

--- a/solution.py
+++ b/solution.py
@@ -124,7 +124,8 @@
     message_ref = refs[later]
     left_ref, back_ref, sems = refs[-3:]
     copies = started(refs[:later], refs[later + 1 : 2 * later + 1], ahead, sems)
-    parties, rows, width = message_ref.shape
+    parties, rows, lanes = message_ref.shape
+    width = gathered_ref.shape[2]
     share = width // parties
     count = key_rows.shape[0]
     section, block = place
@@ -150,12 +151,16 @@
         dot(back_ref[2], keys, NN),
     )
     for index, gradient in enumerate(gradients):
-        message_ref[:, index * share : (index + 1) * share, :] = gradient.astype(bf16).reshape(
-            parties, share, width
-        )
-    if rows > 3 * share:
-        row = lax.broadcasted_iota(jnp.int32, (share, width), 0)
-        extra = jnp.zeros((share, width), f32)
+        tiles = gradient.astype(bf16).reshape(parties, share, width)
+        for half in range(width // lanes):
+            start = (3 * half + index) * share
+            message_ref[:, start : start + share, :] = tiles[
+                :, :, half * lanes : (half + 1) * lanes
+            ]
+    used = 3 * share * (width // lanes)
+    if rows > used:
+        row = lax.broadcasted_iota(jnp.int32, (share, lanes), 0)
+        extra = jnp.zeros((share, lanes), f32)
         blocks = rate_ref.shape[2]
         for index in range(rate_ref.shape[0] * blocks):
             each = index % blocks
@@ -164,8 +169,8 @@
             high = square.astype(bf16).astype(f32)
             extra = jnp.where(row == 2 * index, high, extra)
             extra = jnp.where(row == 2 * index + 1, square - high, extra)
-        message_ref[:, 3 * share :, :] = jnp.broadcast_to(
-            extra.astype(bf16)[None], (parties, share, width)
+        message_ref[:, used:, :] = jnp.broadcast_to(
+            extra.astype(bf16)[None], (parties, share, lanes)
         )
     for copy in copies:
         copy.wait()
@@ -175,12 +180,17 @@
     parties, _, width = gathered.shape
     share = width // parties
     count = keys.shape[0]
-    rows = (4 if place == (0, 0) else 3) * share
+    if place == (0, 0):
+        lanes = width // 2
+        rows = 7 * share
+    else:
+        lanes = width
+        rows = 3 * share
     return pl.pallas_call(
         functools.partial(grads_kernel, place, 256, [where for _, where in ahead]),
         in_specs=[VMEM] * 4 + [HBM] * len(ahead),
         out_specs=[VMEM] * (1 + len(ahead)),
-        out_shape=[in_vmem(parties, rows, width, dtype=bf16)]
+        out_shape=[in_vmem(parties, rows, lanes, dtype=bf16)]
         + [rows_in_vmem(array) for array, _ in ahead],
         scratch_shapes=[
             pltpu.VMEM((width, width), bf16),
@@ -199,9 +209,17 @@
     arrived_ref, weights_ref, moment_ref = refs[:3]
     refs = refs[3:]
     rows = weights_ref.shape[0]
-    gradients = jnp.sum(arrived_ref[:, :rows, :].astype(f32), axis=0)
+    halves = weights_ref.shape[1] // arrived_ref.shape[2]
+    gradients = jnp.concatenate(
+        [
+            jnp.sum(arrived_ref[:, half * rows : (half + 1) * rows, :].astype(f32), axis=0)
+            for half in range(halves)
+        ],
+        axis=1,
+    )
     if index == 0:
-        squares = jnp.sum(arrived_ref[:, rows:, :].astype(f32), axis=0)
+        squares = jnp.sum(arrived_ref[:, halves * rows :, :].astype(f32), axis=0)
+        squares = jnp.concatenate([squares] * halves, axis=1)
         refs[-1][...] = squares
     else:
         squares, refs = refs[0][...], refs[1:]
@@ -242,7 +260,7 @@
         out_shape = [in_vmem(arrived.shape[0], rows, width, dtype=bf16)]
         out_shape += [in_vmem(rows, width)] * 2
     if index == 0:
-        out_shape.append(in_vmem(arrived.shape[1] - rows, width))
+        out_shape.append(in_vmem(arrived.shape[1] - rows * width // arrived.shape[2], width))
     return pl.pallas_call(
         functools.partial(update_kernel, index, waits),
         in_specs=in_specs,

time: 141 us -> 142 us (level)
  no operation moved by 1% of the time
where the time goes in v8:
time: 142 us; the launch traced here: 140 us
  blocking collectives  78.3 us (55%)
  Pallas kernels  22.8 us (16%)
  waiting for transfers between devices  18.5 us (13%)
  starting transfers between devices  18.3 us (13%)
    all_to_all x6, blocking collectives, exchanged(): return lax.all_to_all(tiles, TOK, split_axis=0, concat_axis=0, tiled=True)  78.3 us
    all_to_all x3, waiting for transfers between devices, exchanged(): return lax.all_to_all(tiles, TOK, split_axis=0, concat_axis=0, tiled=True)  17.9 us
    all_to_all x3, starting transfers between devices, exchanged(): return lax.all_to_all(tiles, TOK, split_axis=0, concat_axis=0, tiled=True)  14.5 us
    pallas_call x5, Pallas kernels, apply_fast(): pl.pallas_call(functools.partial(apply_kernel, place, staged, waits, extr...  9.93 us
    pallas_call x4, Pallas kernels, grads(): pl.pallas_call(functools.partial(grads_kernel, place, 256, [where for _,...  7.87 us
  transfers between devices with their start and end apart: 5, of which 4 were waited for; matrix products, arithmetic and copies ran while one was open for 1% of the time, Pallas kernels for 8%

profile of v8, /device:TPU:96, one launch (start us, length us, event | category | flops | bytes accessed | tf_op | source)
XLA Modules:
  0.0 140.1 jit_solution(18421273276729727020)
XLA Ops:
  0.6 1.6 %spread.1 = (bf16[16,48,256]{2,1,0:T(8,128)(2,1)}, f32[8,128]{1,0:T(8,128)S(1)}) custom-call(f32[48,256]{1,0:T(8,128)} %bitcast.29), custom_call_target="tpu_custom_call" | custom-call | tf_op jit(solution)/shard_map/spread/pallas_call | solution.py:81
  2.2 7.0 %all-to-all-start.1 = ((bf16[16,48,256]{2,1,0:T(8,128)(2,1)}), bf16[16,48,256]{2,1,0:T(8,128)(2,1)S(1)}, u32[]{:S(2)}, u32[]{:S(2)}) async-start(bf16[16,48,256]{2,1,0:T(8,128)(2,1)} %get-tuple-element.44), calls=%async_computation.1 | async-start | bytes 786432 | tf_op jit(solution)/shard_map/all_to_all | solution.py:404
  9.3 1.9 %stage.1 = (bf16[1280,256]{1,0:T(8,128)(2,1)S(1)}, bf16[1280,256]{1,0:T(8,128)(2,1)S(1)}, f32[8,128]{1,0:T(8,128)}) custom-call(f32[8,128]{1,0:T(8,128)S(1)} %get-tuple-element.45.refs_0_, s32[1]{0:T(128)} %bitcast.refs_1_.first_ref.refs_2_, bf16[2,1,2,1280,256]{4,3,2,1,0:T(8,128)(2,1)} %refs_0_.6, bf16[2,1,2,1280,256]{4,3,2,1,0:T(8,128)(2,1)} %refs_1_.5), custom_call_target="tpu_custom_call" | custom-call | bytes 2621440 | tf_op jit(solution)/shard_map/stage/pallas_call | solution.py:108
  11.2 7.9 %all-to-all-done.1.gathered_ref = bf16[16,48,256]{2,1,0:T(8,128)(2,1)S(1)} async-done(((bf16[16,48,256]{2,1,0:T(8,128)(2,1)}), bf16[16,48,256]{2,1,0:T(8,128)(2,1)S(1)}, u32[]{:S(2)}, u32[]{:S(2)}) %all-to-all-start.1) | async-done | bytes 393248 | tf_op jit(solution)/shard_map/all_to_all | solution.py:404
  19.1 2.5 %grads.4 = (bf16[16,112,128]{2,1,0:T(8,128)(2,1)S(1)}, bf16[1280,256]{1,0:T(8,128)(2,1)S(1)}, bf16[1280,256]{1,0:T(8,128)(2,1)S(1)}) custom-call(bf16[16,48,256]{2,1,0:T(8,128)(2,1)S(1)} %all-to-all-done.1.gathered_ref, f32[2,1,2,1280]{3,2,1,0:T(2,128)S(1)} %copy-done, bf16[1280,256]{1,0:T(8,128)(2,1)S(1)} %get-tuple-element.46.key_rows, ...), custom_call_target="tpu_custom_call" | custom-call | flops 1006632960 | bytes 1310720 | tf_op jit(solution)/shard_map/grads/pallas_call | solution.py:189
  21.6 13.3 %all_to_all.50.refs_0_ = bf16[16,112,128]{2,1,0:T(8,128)(2,1)S(1)} all-to-all(bf16[16,112,128]{2,1,0:T(8,128)(2,1)S(1)} %get-tuple-element.48), channel_id=1, replica_groups=mesh['seg'=16,'tok_0'=4,'tok_1'=4] {'tok_0','tok_1'}, dimensions={0} | all-to-all | bytes 917504 | tf_op jit(solution)/shard_map/all_to_all | solution.py:404
  35.1 12.4 %all_to_all.51.gathered_ref = bf16[16,48,256]{2,1,0:T(8,128)(2,1)S(1)} all-to-all(bf16[16,48,256]{2,1,0:T(8,128)(2,1)S(1)} %get-tuple-element.49), channel_id=1, replica_groups=mesh['seg'=16,'tok_0'=4,'tok_1'=4] {'tok_0','tok_1'}, dimensions={0} | all-to-all | bytes 786432 | tf_op jit(solution)/shard_map/all_to_all | solution.py:404
  47.4 1.6 %grads.5 = (bf16[16,48,256]{2,1,0:T(8,128)(2,1)S(1)}, bf16[1280,256]{1,0:T(8,128)(2,1)S(1)}, bf16[1280,256]{1,0:T(8,128)(2,1)S(1)}) custom-call(bf16[16,48,256]{2,1,0:T(8,128)(2,1)S(1)} %all_to_all.51.gathered_ref, f32[2,1,2,1280]{3,2,1,0:T(2,128)S(1)} %copy-done, bf16[1280,256]{1,0:T(8,128)(2,1)S(1)} %get-tuple-element.50.key_rows, ...), custom_call_target="tpu_custom_call" | custom-call | flops 1006632960 | bytes 1310720 | tf_op jit(solution)/shard_map/grads/pallas_call | solution.py:189
  49.0 12.6 %all_to_all.52.refs_0_ = bf16[16,48,256]{2,1,0:T(8,128)(2,1)S(1)} all-to-all(bf16[16,48,256]{2,1,0:T(8,128)(2,1)S(1)} %get-tuple-element.52), channel_id=1, replica_groups=mesh['seg'=16,'tok_0'=4,'tok_1'=4] {'tok_0','tok_1'}, dimensions={0} | all-to-all | bytes 786432 | tf_op jit(solution)/shard_map/all_to_all | solution.py:404
  61.9 1.9 %collective-permute-start = (bf16[96,256]{1,0:T(8,128)(2,1)S(1)}, bf16[96,256]{1,0:T(8,128)(2,1)S(1)}, u32[]{:S(2)}, u32[]{:S(2)}) collective-permute-start(bf16[96,256]{1,0:T(8,128)(2,1)S(1)} %get-tuple-element.56.refs_0_.state_ref), channel_id=1, source_target_pairs={{0,16},{16,32},{32,48},{48,64},{64,80},{80,96},{96,112},{112,128},... | collective-permute-start | bytes 147464 | tf_op jit(solution)/shard_map/ppermute | solution.py:409
  63.9 2.8 %apply.6 = (bf16[2,1,2,1280,256]{4,3,2,1,0:T(8,128)(2,1)}, bf16[96,256]{1,0:T(8,128)(2,1)S(1)}) custom-call(bf16[16,48,256]{2,1,0:T(8,128)(2,1)S(1)} %all_to_all.51.gathered_ref, bf16[2,1,2,1280,256]{4,3,2,1,0:T(8,128)(2,1)} %query_ref.7, bf16[96,256]{1,0:T(8,128)(2,1)S(1)} %get-tuple-element.56.refs_0_.state_ref, ...), custom_call_target="tpu_custom_call", output_to_operand_aliasing={{0}: (4, {})} | custom-call | flops 503316480 | bytes 1310720 | tf_op jit(solution)/shard_map/apply/pallas_call | solution.py:381
  67.3 14.6 %all_to_all.53.gathered_ref = bf16[16,48,256]{2,1,0:T(8,128)(2,1)S(1)} all-to-all(bf16[16,48,256]{2,1,0:T(8,128)(2,1)S(1)} %get-tuple-element.59), channel_id=1, replica_groups=mesh['seg'=16,'tok_0'=4,'tok_1'=4] {'tok_0','tok_1'}, dimensions={0} | all-to-all | bytes 786432 | tf_op jit(solution)/shard_map/all_to_all | solution.py:404
  81.9 1.5 %grads.6 = (bf16[16,48,256]{2,1,0:T(8,128)(2,1)S(1)}, bf16[1280,256]{1,0:T(8,128)(2,1)S(1)}, bf16[1280,256]{1,0:T(8,128)(2,1)S(1)}) custom-call(bf16[16,48,256]{2,1,0:T(8,128)(2,1)S(1)} %all_to_all.53.gathered_ref, f32[2,1,2,1280]{3,2,1,0:T(2,128)S(1)} %copy-done, bf16[1280,256]{1,0:T(8,128)(2,1)S(1)} %get-tuple-element.60.key_rows, ...), custom_call_target="tpu_custom_call" | custom-call | flops 1006632960 | bytes 1310720 | tf_op jit(solution)/shard_map/grads/pallas_call | solution.py:189
  83.4 12.9 %all_to_all.54.refs_0_ = bf16[16,48,256]{2,1,0:T(8,128)(2,1)S(1)} all-to-all(bf16[16,48,256]{2,1,0:T(8,128)(2,1)S(1)} %get-tuple-element.62), channel_id=1, replica_groups=mesh['seg'=16,'tok_0'=4,'tok_1'=4] {'tok_0','tok_1'}, dimensions={0} | all-to-all | bytes 786432 | tf_op jit(solution)/shard_map/all_to_all | solution.py:404
  96.4 12.6 %all_to_all.55.gathered_ref = bf16[16,48,256]{2,1,0:T(8,128)(2,1)S(1)} all-to-all(bf16[16,48,256]{2,1,0:T(8,128)(2,1)S(1)} %get-tuple-element.65), channel_id=1, replica_groups=mesh['seg'=16,'tok_0'=4,'tok_1'=4] {'tok_0','tok_1'}, dimensions={0} | all-to-all | bytes 786432 | tf_op jit(solution)/shard_map/all_to_all | solution.py:404
  109.1 2.3 %grads.7 = (bf16[16,48,256]{2,1,0:T(8,128)(2,1)}, bf16[1280,256]{1,0:T(8,128)(2,1)S(1)}) custom-call(bf16[16,48,256]{2,1,0:T(8,128)(2,1)S(1)} %all_to_all.55.gathered_ref, f32[2,1,2,1280]{3,2,1,0:T(2,128)S(1)} %copy-done, bf16[1280,256]{1,0:T(8,128)(2,1)S(1)} %get-tuple-element.66.key_rows, bf16[1280,256]{1,0:T(8,128)(2,1)S(1)} %get-tuple-element.67.value_rows, ...), custom_call_target="tpu_custom_call" | custom-call | flops 1006632960 | bytes 1310720 | tf_op jit(solution)/shard_map/grads/pallas_call | solution.py:189
  111.4 3.7 %all-to-all-start.8 = ((bf16[16,48,256]{2,1,0:T(8,128)(2,1)}), bf16[16,48,256]{2,1,0:T(8,128)(2,1)S(1)}, u32[]{:S(2)}, u32[]{:S(2)}) async-start(bf16[16,48,256]{2,1,0:T(8,128)(2,1)} %get-tuple-element.68), calls=%async_computation.8 | async-start | bytes 786432 | tf_op jit(solution)/shard_map/all_to_all | solution.py:404
  115.1 1.9 %collective-permute-start.1 = (bf16[16,48,256]{2,1,0:T(8,128)(2,1)S(1)}, bf16[16,48,256]{2,1,0:T(8,128)(2,1)S(1)}, u32[]{:S(2)}, u32[]{:S(2)}) collective-permute-start(bf16[16,48,256]{2,1,0:T(8,128)(2,1)S(1)} %all_to_all.53.gathered_ref), channel_id=1, source_target_pairs={{16,0},{32,16},{48,32},{64,48},{80,64},{96,80},{112,96},{128,112},... | collective-permute-start | bytes 1179656 | tf_op jit(solution)/shard_map/ppermute | solution.py:414
  117.1 2.8 %apply.7 = (bf16[2,1,2,1280,256]{4,3,2,1,0:T(8,128)(2,1)}, f32[8,128]{1,0:T(8,128)S(1)}) custom-call(bf16[16,48,256]{2,1,0:T(8,128)(2,1)S(1)} %all_to_all.55.gathered_ref, bf16[2,1,2,1280,256]{4,3,2,1,0:T(8,128)(2,1)} %query_ref.7, bf16[2,1,2,1280,256]{4,3,2,1,0:T(8,128)(2,1)} %get-tuple-element.71.refs_0_), custom_call_target="tpu_custom_call", output_to_operand_aliasing={{0}: (2, {})} | custom-call | flops 503316480 | bytes 1310720 | tf_op jit(solution)/shard_map/apply/pallas_call | solution.py:381
  119.8 4.4 %all-to-all-done.8.refs_0_ = bf16[16,48,256]{2,1,0:T(8,128)(2,1)S(1)} async-done(((bf16[16,48,256]{2,1,0:T(8,128)(2,1)}), bf16[16,48,256]{2,1,0:T(8,128)(2,1)S(1)}, u32[]{:S(2)}, u32[]{:S(2)}) %all-to-all-start.8) | async-done | bytes 393248 | tf_op jit(solution)/shard_map/all_to_all | solution.py:404
  125.2 3.7 %all-to-all-start.9 = ((bf16[16,48,256]{2,1,0:T(8,128)(2,1)}), bf16[16,48,256]{2,1,0:T(8,128)(2,1)S(1)}, u32[]{:S(2)}, u32[]{:S(2)}) async-start(bf16[16,48,256]{2,1,0:T(8,128)(2,1)} %get-tuple-element.73), calls=%async_computation.9 | async-start | bytes 786432 | tf_op jit(solution)/shard_map/all_to_all | solution.py:404
  130.2 2.8 %apply.8 = (bf16[2,1,2,1280,256]{4,3,2,1,0:T(8,128)(2,1)}, f32[48,256]{1,0:T(8,128)S(1)}) custom-call(bf16[16,48,256]{2,1,0:T(8,128)(2,1)S(1)} %collective-permute-done.1.gathered_ref, bf16[2,1,2,1280,256]{4,3,2,1,0:T(8,128)(2,1)} %query_ref.7, f32[48,256]{1,0:T(8,128)S(1)} %get-tuple-element.75.refs_0_, ...), custom_call_target="tpu_custom_call", output_to_operand_aliasing={{0}: (5, {})} | custom-call | flops 503316480 | bytes 1310720 | tf_op jit(solution)/shard_map/apply/pallas_call | solution.py:381
  132.9 5.6 %all-to-all-done.9.gathered_ref = bf16[16,48,256]{2,1,0:T(8,128)(2,1)S(1)} async-done(((bf16[16,48,256]{2,1,0:T(8,128)(2,1)}), bf16[16,48,256]{2,1,0:T(8,128)(2,1)S(1)}, u32[]{:S(2)}, u32[]{:S(2)}) %all-to-all-start.9) | async-done | bytes 393248 | tf_op jit(solution)/shard_map/all_to_all | solution.py:404
  138.5 1.6 %apply.9 = bf16[2,1,2,1280,256]{4,3,2,1,0:T(8,128)(2,1)} custom-call(bf16[16,48,256]{2,1,0:T(8,128)(2,1)S(1)} %all-to-all-done.9.gathered_ref, bf16[1280,256]{1,0:T(8,128)(2,1)S(1)} %get-tuple-element.74.query_ref, f32[48,256]{1,0:T(8,128)S(1)} %get-tuple-element.77.refs_0_, ...), custom_call_target="tpu_custom_call", output_to_operand_aliasing={{}: (3, {})} | custom-call | flops 503316480 | bytes 1310720 | tf_op jit(solution)/shard_map/apply/pallas_call | solution.py:381
  (22 shorter events, 3.4 us)
Async XLA Ops:
  2.2 16.9 %all-to-all-start.1 = ((bf16[16,48,256]{2,1,0:T(8,128)(2,1)}), bf16[16,48,256]{2,1,0:T(8,128)(2,1)S(1)}, u32[]{:S(2)}, u32[]{:S(2)}) async-start(bf16[16,48,256]{2,1,0:T(8,128)(2,1)} %get-tuple-element.44), calls=%async_computation.1 | async-start | bytes 786432 | tf_op jit(solution)/shard_map/all_to_all | solution.py:404
  9.3 9.8 %copy-start = (f32[2,1,2,1280]{3,2,1,0:T(2,128)S(1)}, f32[2,1,2,1280]{3,2,1,0:T(2,128)}, u32[]{:S(2)}) copy-start(f32[2,1,2,1280]{3,2,1,0:T(2,128)} %rate_ref.7) | copy-start | bytes 61444
  19.1 15.8 %copy-start.1 = (f32[1,3,256,16]{2,3,1,0:T(8,128)S(1)}, f32[1,3,256,16]{2,3,1,0:T(8,128)}, u32[]{:S(2)}) copy-start(f32[1,3,256,16]{2,3,1,0:T(8,128)} %param.14) | copy-start | bytes 147460
  19.1 15.8 %copy-start.2 = (f32[1,3,256,16]{2,3,1,0:T(8,128)S(1)}, f32[1,3,256,16]{2,3,1,0:T(8,128)}, u32[]{:S(2)}) copy-start(f32[1,3,256,16]{2,3,1,0:T(8,128)} %param.15) | copy-start | bytes 147460
  61.9 5.4 %collective-permute-start = (bf16[96,256]{1,0:T(8,128)(2,1)S(1)}, bf16[96,256]{1,0:T(8,128)(2,1)S(1)}, u32[]{:S(2)}, u32[]{:S(2)}) collective-permute-start(bf16[96,256]{1,0:T(8,128)(2,1)S(1)} %get-tuple-element.56.refs_0_.state_ref), channel_id=1, source_target_pairs={{0,16},{16,32},{32,48},{48,64},{64,80},{80,96},{96,112},{112,128},... | collective-permute-start | bytes 147464 | tf_op jit(solution)/shard_map/ppermute | solution.py:409
  63.9 3.4 %copy-start.3 = (f32[3,256,16]{1,2,0:T(8,128)S(1)}, f32[3,256,16]{1,2,0:T(8,128)}, u32[]{:S(2)}) copy-start(f32[3,256,16]{1,2,0:T(8,128)} %param.16) | copy-start | bytes 147460
  63.9 3.4 %copy-start.4 = (f32[3,256,16]{1,2,0:T(8,128)S(1)}, f32[3,256,16]{1,2,0:T(8,128)}, u32[]{:S(2)}) copy-start(f32[3,256,16]{1,2,0:T(8,128)} %param.17) | copy-start | bytes 147460
  111.4 12.9 %all-to-all-start.8 = ((bf16[16,48,256]{2,1,0:T(8,128)(2,1)}), bf16[16,48,256]{2,1,0:T(8,128)(2,1)S(1)}, u32[]{:S(2)}, u32[]{:S(2)}) async-start(bf16[16,48,256]{2,1,0:T(8,128)(2,1)} %get-tuple-element.68), calls=%async_computation.8 | async-start | bytes 786432 | tf_op jit(solution)/shard_map/all_to_all | solution.py:404
  115.1 15.0 %collective-permute-start.1 = (bf16[16,48,256]{2,1,0:T(8,128)(2,1)S(1)}, bf16[16,48,256]{2,1,0:T(8,128)(2,1)S(1)}, u32[]{:S(2)}, u32[]{:S(2)}) collective-permute-start(bf16[16,48,256]{2,1,0:T(8,128)(2,1)S(1)} %all_to_all.53.gathered_ref), channel_id=1, source_target_pairs={{16,0},{32,16},{48,32},{64,48},{80,64},{96,80},{112,96},{128,112},... | collective-permute-start | bytes 1179656 | tf_op jit(solution)/shard_map/ppermute | solution.py:414
  125.2 13.3 %all-to-all-start.9 = ((bf16[16,48,256]{2,1,0:T(8,128)(2,1)}), bf16[16,48,256]{2,1,0:T(8,128)(2,1)S(1)}, u32[]{:S(2)}, u32[]{:S(2)}) async-start(bf16[16,48,256]{2,1,0:T(8,128)(2,1)} %get-tuple-element.73), calls=%async_computation.9 | async-start | bytes 786432 | tf_op jit(solution)/shard_map/all_to_all | solution.py:404

commit v9 on v8

--- a/solution.py
+++ b/solution.py
@@ -97,30 +97,44 @@
 def stage_kernel(places, *refs):
     count = len(places)
     token_ref, sems = refs[-2:]
-    copies = started(refs[2 : 2 + count], refs[-2 - count : -2], places, sems)
-    token_ref[...] = jnp.zeros_like(token_ref)
+    rate_ref = refs[2]
+    copies = started(refs[3 : 3 + count], refs[-2 - count : -2], places, sems)
+    share, lanes = token_ref.shape
+    row = lax.broadcasted_iota(jnp.int32, (share, lanes), 0)
+    totals = jnp.zeros((share, lanes), f32)
+    blocks = rate_ref.shape[2]
+    for index in range(rate_ref.shape[0] * blocks):
+        each = index % blocks
+        rates = rate_ref[index // blocks, 0, each : each + 1, :]
+        square = jnp.sum(rates * rates, axis=1, keepdims=True)
+        high = square.astype(bf16).astype(f32)
+        totals = jnp.where(row == 2 * index, high, totals)
+        totals = jnp.where(row == 2 * index + 1, square - high, totals)
+    token_ref[...] = totals.astype(bf16)
     for copy in copies:
         copy.wait()
 
 
-def stage(token, who, place, arrays):
+def stage(token, who, rates, place, arrays, share):
     count = len(arrays)
     return pl.pallas_call(
         functools.partial(stage_kernel, [place] * count),
-        in_specs=[VMEM, SMEM] + [HBM] * count,
+        in_specs=[VMEM, SMEM, VMEM] + [HBM] * count,
         out_specs=[VMEM] * (count + 1),
-        out_shape=[rows_in_vmem(array) for array in arrays] + [TOKEN],
+        out_shape=[rows_in_vmem(array) for array in arrays]
+        + [in_vmem(share, arrays[0].shape[4] // 2, dtype=bf16)],
         scratch_shapes=[pltpu.SemaphoreType.DMA((count,))],
         compiler_params=params(),
         cost_estimate=pl.CostEstimate(
             flops=0, bytes_accessed=count * arrays[0].size, transcendentals=0
         ),
         name="stage",
-    )(token, who, *(in_hbm(array) for array in arrays))
-
-
-def grads_kernel(place, tile, ahead, gathered_ref, rate_ref, key_rows, value_rows, *refs):
+    )(token, who, rates, *(in_hbm(array) for array in arrays))
+
+
+def grads_kernel(place, tile, ahead, first, gathered_ref, rate_ref, key_rows, value_rows, *refs):
     later = len(ahead)
+    totals_ref, refs = (refs[later], refs[:later] + refs[later + 1 :]) if first else (None, refs)
     message_ref = refs[later]
     left_ref, back_ref, sems = refs[-3:]
     copies = started(refs[:later], refs[later + 1 : 2 * later + 1], ahead, sems)
@@ -159,36 +173,26 @@
             ]
     used = 3 * share * (width // lanes)
     if rows > used:
-        row = lax.broadcasted_iota(jnp.int32, (share, lanes), 0)
-        extra = jnp.zeros((share, lanes), f32)
-        blocks = rate_ref.shape[2]
-        for index in range(rate_ref.shape[0] * blocks):
-            each = index % blocks
-            rates = rate_ref[index // blocks, 0, each : each + 1, :]
-            square = jnp.sum(rates * rates, axis=1, keepdims=True)
-            high = square.astype(bf16).astype(f32)
-            extra = jnp.where(row == 2 * index, high, extra)
-            extra = jnp.where(row == 2 * index + 1, square - high, extra)
         message_ref[:, used:, :] = jnp.broadcast_to(
-            extra.astype(bf16)[None], (parties, share, lanes)
+            totals_ref[...][None], (parties, share, lanes)
         )
     for copy in copies:
         copy.wait()
 
 
-def grads(gathered, rates, keys, values, place, ahead):
+def grads(gathered, rates, keys, values, place, ahead, totals=None):
     parties, _, width = gathered.shape
     share = width // parties
     count = keys.shape[0]
-    if place == (0, 0):
+    if totals is not None:
         lanes = width // 2
         rows = 7 * share
     else:
         lanes = width
         rows = 3 * share
     return pl.pallas_call(
-        functools.partial(grads_kernel, place, 256, [where for _, where in ahead]),
-        in_specs=[VMEM] * 4 + [HBM] * len(ahead),
+        functools.partial(grads_kernel, place, 256, [where for _, where in ahead], totals is not None),
+        in_specs=[VMEM] * 4 + [HBM] * len(ahead) + [VMEM] * (totals is not None),
         out_specs=[VMEM] * (1 + len(ahead)),
         out_shape=[in_vmem(parties, rows, lanes, dtype=bf16)]
         + [rows_in_vmem(array) for array, _ in ahead],
@@ -202,7 +206,7 @@
             flops=12 * count * width * width, bytes_accessed=4 * count * width, transcendentals=0
         ),
         name="grads",
-    )(gathered, rates, keys, values, *(in_hbm(array) for array, _ in ahead))
+    )(gathered, rates, keys, values, *(in_hbm(array) for array, _ in ahead), *(() if totals is None else (totals,)))
 
 
 def update_kernel(index, waits, *refs):
@@ -460,7 +464,7 @@
     rows, shape = weights.shape[0], queries.shape
     places = [(section, 0, block) for section in range(sections) for block in range(blocks)]
     message, token = spread(weights, parties)
-    *staged, _ = stage(token, who, places[0], (key_vectors, values))
+    *staged, totals = stage(token, who, token_rates, places[0], (key_vectors, values), share)
     gathered = exchanged(message)
     results = squares = owed = None
     pending = []
@@ -472,7 +476,12 @@
         else:
             ahead = ((key_vectors, places[index + 1]), (values, places[index + 1]))
         message, *staged = grads(
-            gathered, token_rates, *staged, (place[0], place[2]), ahead
+            gathered,
+            token_rates,
+            *staged,
+            (place[0], place[2]),
+            ahead,
+            totals if index == 0 else None,
         )
         arrived = exchanged(message)
         token = None

time: 142 us -> 141 us (level)
  Pallas kernels: 22.8 us -> 21.3 us
where the time goes in v9:
time: 141 us; the launch traced here: 139 us
  blocking collectives  78.3 us (56%)
  Pallas kernels  21.3 us (15%)
  starting transfers between devices  18.3 us (13%)
  waiting for transfers between devices  18.3 us (13%)
  local copies, waits for them, and re-layouts  1.99 us (1%)
    all_to_all x6, blocking collectives, exchanged(): return lax.all_to_all(tiles, TOK, split_axis=0, concat_axis=0, tiled=True)  78.3 us
    all_to_all x3, waiting for transfers between devices, exchanged(): return lax.all_to_all(tiles, TOK, split_axis=0, concat_axis=0, tiled=True)  17.7 us
    all_to_all x3, starting transfers between devices, exchanged(): return lax.all_to_all(tiles, TOK, split_axis=0, concat_axis=0, tiled=True)  14.5 us
    pallas_call x5, Pallas kernels, apply_fast(): pl.pallas_call(functools.partial(apply_kernel, place, staged, waits, extr...  9.94 us
    pallas_call x4, Pallas kernels, grads(): pl.pallas_call(functools.partial(grads_kernel, place, 256, [where for _,...  6.92 us
  transfers between devices with their start and end apart: 5, of which 4 were waited for; matrix products, arithmetic and copies ran while one was open for 1% of the time, Pallas kernels for 8%

profile of v9, /device:TPU:96, one launch (start us, length us, event | category | flops | bytes accessed | tf_op | source)
XLA Modules:
  0.0 139.1 jit_solution(12421357226849179183)
XLA Ops:
  0.6 1.6 %spread.1 = (bf16[16,48,256]{2,1,0:T(8,128)(2,1)}, f32[8,128]{1,0:T(8,128)S(1)}) custom-call(f32[48,256]{1,0:T(8,128)} %bitcast.29), custom_call_target="tpu_custom_call" | custom-call | tf_op jit(solution)/shard_map/spread/pallas_call | solution.py:81
  2.2 7.0 %all-to-all-start.1 = ((bf16[16,48,256]{2,1,0:T(8,128)(2,1)}), bf16[16,48,256]{2,1,0:T(8,128)(2,1)S(1)}, u32[]{:S(2)}, u32[]{:S(2)}) async-start(bf16[16,48,256]{2,1,0:T(8,128)(2,1)} %get-tuple-element.45), calls=%async_computation.1 | async-start | bytes 786432 | tf_op jit(solution)/shard_map/all_to_all | solution.py:408
  10.0 1.3 stage.1
  11.3 7.8 %all-to-all-done.1.gathered_ref = bf16[16,48,256]{2,1,0:T(8,128)(2,1)S(1)} async-done(((bf16[16,48,256]{2,1,0:T(8,128)(2,1)}), bf16[16,48,256]{2,1,0:T(8,128)(2,1)S(1)}, u32[]{:S(2)}, u32[]{:S(2)}) %all-to-all-start.1) | async-done | bytes 393248 | tf_op jit(solution)/shard_map/all_to_all | solution.py:408
  19.1 1.5 %grads.4 = (bf16[16,112,128]{2,1,0:T(8,128)(2,1)S(1)}, bf16[1280,256]{1,0:T(8,128)(2,1)S(1)}, bf16[1280,256]{1,0:T(8,128)(2,1)S(1)}) custom-call(bf16[16,48,256]{2,1,0:T(8,128)(2,1)S(1)} %all-to-all-done.1.gathered_ref, f32[2,1,2,1280]{3,2,1,0:T(2,128)S(1)} %copy-done.1, bf16[1280,256]{1,0:T(8,128)(2,1)S(1)} %get-tuple-element.47.key_rows, ...), custom_call_target="tpu_custom_call" | custom-call | flops 1006632960 | bytes 1310720 | tf_op jit(solution)/shard_map/grads/pallas_call | solution.py:193
  20.6 13.3 %all_to_all.50.refs_0_ = bf16[16,112,128]{2,1,0:T(8,128)(2,1)S(1)} all-to-all(bf16[16,112,128]{2,1,0:T(8,128)(2,1)S(1)} %get-tuple-element.50), channel_id=1, replica_groups=mesh['seg'=16,'tok_0'=4,'tok_1'=4] {'tok_0','tok_1'}, dimensions={0} | all-to-all | bytes 917504 | tf_op jit(solution)/shard_map/all_to_all | solution.py:408
  34.1 12.4 %all_to_all.51.gathered_ref = bf16[16,48,256]{2,1,0:T(8,128)(2,1)S(1)} all-to-all(bf16[16,48,256]{2,1,0:T(8,128)(2,1)S(1)} %get-tuple-element.51), channel_id=1, replica_groups=mesh['seg'=16,'tok_0'=4,'tok_1'=4] {'tok_0','tok_1'}, dimensions={0} | all-to-all | bytes 786432 | tf_op jit(solution)/shard_map/all_to_all | solution.py:408
  46.4 1.6 %grads.5 = (bf16[16,48,256]{2,1,0:T(8,128)(2,1)S(1)}, bf16[1280,256]{1,0:T(8,128)(2,1)S(1)}, bf16[1280,256]{1,0:T(8,128)(2,1)S(1)}) custom-call(bf16[16,48,256]{2,1,0:T(8,128)(2,1)S(1)} %all_to_all.51.gathered_ref, f32[2,1,2,1280]{3,2,1,0:T(2,128)S(1)} %copy-done.1, bf16[1280,256]{1,0:T(8,128)(2,1)S(1)} %get-tuple-element.52.key_rows, ...), custom_call_target="tpu_custom_call" | custom-call | flops 1006632960 | bytes 1310720 | tf_op jit(solution)/shard_map/grads/pallas_call | solution.py:193
  48.1 12.6 %all_to_all.52.refs_0_ = bf16[16,48,256]{2,1,0:T(8,128)(2,1)S(1)} all-to-all(bf16[16,48,256]{2,1,0:T(8,128)(2,1)S(1)} %get-tuple-element.54), channel_id=1, replica_groups=mesh['seg'=16,'tok_0'=4,'tok_1'=4] {'tok_0','tok_1'}, dimensions={0} | all-to-all | bytes 786432 | tf_op jit(solution)/shard_map/all_to_all | solution.py:408
  60.9 1.9 %collective-permute-start = (bf16[96,256]{1,0:T(8,128)(2,1)S(1)}, bf16[96,256]{1,0:T(8,128)(2,1)S(1)}, u32[]{:S(2)}, u32[]{:S(2)}) collective-permute-start(bf16[96,256]{1,0:T(8,128)(2,1)S(1)} %get-tuple-element.58.refs_0_.state_ref), channel_id=1, source_target_pairs={{0,16},{16,32},{32,48},{48,64},{64,80},{80,96},{96,112},{112,128},... | collective-permute-start | bytes 147464 | tf_op jit(solution)/shard_map/ppermute | solution.py:413
  62.9 2.8 %apply.6 = (bf16[2,1,2,1280,256]{4,3,2,1,0:T(8,128)(2,1)}, bf16[96,256]{1,0:T(8,128)(2,1)S(1)}) custom-call(bf16[16,48,256]{2,1,0:T(8,128)(2,1)S(1)} %all_to_all.51.gathered_ref, bf16[2,1,2,1280,256]{4,3,2,1,0:T(8,128)(2,1)} %query_ref.7, bf16[96,256]{1,0:T(8,128)(2,1)S(1)} %get-tuple-element.58.refs_0_.state_ref, ...), custom_call_target="tpu_custom_call", output_to_operand_aliasing={{0}: (4, {})} | custom-call | flops 503316480 | bytes 1310720 | tf_op jit(solution)/shard_map/apply/pallas_call | solution.py:385
  66.4 14.6 %all_to_all.53.gathered_ref = bf16[16,48,256]{2,1,0:T(8,128)(2,1)S(1)} all-to-all(bf16[16,48,256]{2,1,0:T(8,128)(2,1)S(1)} %get-tuple-element.61), channel_id=1, replica_groups=mesh['seg'=16,'tok_0'=4,'tok_1'=4] {'tok_0','tok_1'}, dimensions={0} | all-to-all | bytes 786432 | tf_op jit(solution)/shard_map/all_to_all | solution.py:408
  80.9 1.5 %grads.6 = (bf16[16,48,256]{2,1,0:T(8,128)(2,1)S(1)}, bf16[1280,256]{1,0:T(8,128)(2,1)S(1)}, bf16[1280,256]{1,0:T(8,128)(2,1)S(1)}) custom-call(bf16[16,48,256]{2,1,0:T(8,128)(2,1)S(1)} %all_to_all.53.gathered_ref, f32[2,1,2,1280]{3,2,1,0:T(2,128)S(1)} %copy-done.1, bf16[1280,256]{1,0:T(8,128)(2,1)S(1)} %get-tuple-element.62.key_rows, ...), custom_call_target="tpu_custom_call" | custom-call | flops 1006632960 | bytes 1310720 | tf_op jit(solution)/shard_map/grads/pallas_call | solution.py:193
  82.4 12.9 %all_to_all.54.refs_0_ = bf16[16,48,256]{2,1,0:T(8,128)(2,1)S(1)} all-to-all(bf16[16,48,256]{2,1,0:T(8,128)(2,1)S(1)} %get-tuple-element.64), channel_id=1, replica_groups=mesh['seg'=16,'tok_0'=4,'tok_1'=4] {'tok_0','tok_1'}, dimensions={0} | all-to-all | bytes 786432 | tf_op jit(solution)/shard_map/all_to_all | solution.py:408
  95.5 12.6 %all_to_all.55.gathered_ref = bf16[16,48,256]{2,1,0:T(8,128)(2,1)S(1)} all-to-all(bf16[16,48,256]{2,1,0:T(8,128)(2,1)S(1)} %get-tuple-element.67), channel_id=1, replica_groups=mesh['seg'=16,'tok_0'=4,'tok_1'=4] {'tok_0','tok_1'}, dimensions={0} | all-to-all | bytes 786432 | tf_op jit(solution)/shard_map/all_to_all | solution.py:408
  108.1 2.3 %grads.7 = (bf16[16,48,256]{2,1,0:T(8,128)(2,1)}, bf16[1280,256]{1,0:T(8,128)(2,1)S(1)}) custom-call(bf16[16,48,256]{2,1,0:T(8,128)(2,1)S(1)} %all_to_all.55.gathered_ref, f32[2,1,2,1280]{3,2,1,0:T(2,128)S(1)} %copy-done.1, bf16[1280,256]{1,0:T(8,128)(2,1)S(1)} %get-tuple-element.68.key_rows, bf16[1280,256]{1,0:T(8,128)(2,1)S(1)} %get-tuple-element.69.value_rows, ...), custom_call_target="tpu_custom_call" | custom-call | flops 1006632960 | bytes 1310720 | tf_op jit(solution)/shard_map/grads/pallas_call | solution.py:193
  110.4 3.7 %all-to-all-start.8 = ((bf16[16,48,256]{2,1,0:T(8,128)(2,1)}), bf16[16,48,256]{2,1,0:T(8,128)(2,1)S(1)}, u32[]{:S(2)}, u32[]{:S(2)}) async-start(bf16[16,48,256]{2,1,0:T(8,128)(2,1)} %get-tuple-element.70), calls=%async_computation.8 | async-start | bytes 786432 | tf_op jit(solution)/shard_map/all_to_all | solution.py:408
  114.2 1.9 %collective-permute-start.1 = (bf16[16,48,256]{2,1,0:T(8,128)(2,1)S(1)}, bf16[16,48,256]{2,1,0:T(8,128)(2,1)S(1)}, u32[]{:S(2)}, u32[]{:S(2)}) collective-permute-start(bf16[16,48,256]{2,1,0:T(8,128)(2,1)S(1)} %all_to_all.53.gathered_ref), channel_id=1, source_target_pairs={{16,0},{32,16},{48,32},{64,48},{80,64},{96,80},{112,96},{128,112},... | collective-permute-start | bytes 1179656 | tf_op jit(solution)/shard_map/ppermute | solution.py:418
  116.1 2.8 %apply.7 = (bf16[2,1,2,1280,256]{4,3,2,1,0:T(8,128)(2,1)}, f32[8,128]{1,0:T(8,128)S(1)}) custom-call(bf16[16,48,256]{2,1,0:T(8,128)(2,1)S(1)} %all_to_all.55.gathered_ref, bf16[2,1,2,1280,256]{4,3,2,1,0:T(8,128)(2,1)} %query_ref.7, bf16[2,1,2,1280,256]{4,3,2,1,0:T(8,128)(2,1)} %get-tuple-element.73.refs_0_), custom_call_target="tpu_custom_call", output_to_operand_aliasing={{0}: (2, {})} | custom-call | flops 503316480 | bytes 1310720 | tf_op jit(solution)/shard_map/apply/pallas_call | solution.py:385
  118.9 4.4 %all-to-all-done.8.refs_0_ = bf16[16,48,256]{2,1,0:T(8,128)(2,1)S(1)} async-done(((bf16[16,48,256]{2,1,0:T(8,128)(2,1)}), bf16[16,48,256]{2,1,0:T(8,128)(2,1)S(1)}, u32[]{:S(2)}, u32[]{:S(2)}) %all-to-all-start.8) | async-done | bytes 393248 | tf_op jit(solution)/shard_map/all_to_all | solution.py:408
  124.2 3.7 %all-to-all-start.9 = ((bf16[16,48,256]{2,1,0:T(8,128)(2,1)}), bf16[16,48,256]{2,1,0:T(8,128)(2,1)S(1)}, u32[]{:S(2)}, u32[]{:S(2)}) async-start(bf16[16,48,256]{2,1,0:T(8,128)(2,1)} %get-tuple-element.75), calls=%async_computation.9 | async-start | bytes 786432 | tf_op jit(solution)/shard_map/all_to_all | solution.py:408
  129.2 2.8 %apply.8 = (bf16[2,1,2,1280,256]{4,3,2,1,0:T(8,128)(2,1)}, f32[48,256]{1,0:T(8,128)S(1)}) custom-call(bf16[16,48,256]{2,1,0:T(8,128)(2,1)S(1)} %collective-permute-done.1.gathered_ref, bf16[2,1,2,1280,256]{4,3,2,1,0:T(8,128)(2,1)} %query_ref.7, f32[48,256]{1,0:T(8,128)S(1)} %get-tuple-element.77.refs_0_, ...), custom_call_target="tpu_custom_call", output_to_operand_aliasing={{0}: (5, {})} | custom-call | flops 503316480 | bytes 1310720 | tf_op jit(solution)/shard_map/apply/pallas_call | solution.py:385
  132.0 5.6 %all-to-all-done.9.gathered_ref = bf16[16,48,256]{2,1,0:T(8,128)(2,1)S(1)} async-done(((bf16[16,48,256]{2,1,0:T(8,128)(2,1)}), bf16[16,48,256]{2,1,0:T(8,128)(2,1)S(1)}, u32[]{:S(2)}, u32[]{:S(2)}) %all-to-all-start.9) | async-done | bytes 393248 | tf_op jit(solution)/shard_map/all_to_all | solution.py:408
  137.5 1.6 %apply.9 = bf16[2,1,2,1280,256]{4,3,2,1,0:T(8,128)(2,1)} custom-call(bf16[16,48,256]{2,1,0:T(8,128)(2,1)S(1)} %all-to-all-done.9.gathered_ref, bf16[1280,256]{1,0:T(8,128)(2,1)S(1)} %get-tuple-element.76.query_ref, f32[48,256]{1,0:T(8,128)S(1)} %get-tuple-element.79.refs_0_, ...), custom_call_target="tpu_custom_call", output_to_operand_aliasing={{}: (3, {})} | custom-call | flops 503316480 | bytes 1310720 | tf_op jit(solution)/shard_map/apply/pallas_call | solution.py:385
  (24 shorter events, 4.2 us)
Async XLA Ops:
  2.2 16.9 %all-to-all-start.1 = ((bf16[16,48,256]{2,1,0:T(8,128)(2,1)}), bf16[16,48,256]{2,1,0:T(8,128)(2,1)S(1)}, u32[]{:S(2)}, u32[]{:S(2)}) async-start(bf16[16,48,256]{2,1,0:T(8,128)(2,1)} %get-tuple-element.45), calls=%async_computation.1 | async-start | bytes 786432 | tf_op jit(solution)/shard_map/all_to_all | solution.py:408
  9.3 0.7 copy-start
  10.0 9.1 %copy-start.1 = (f32[2,1,2,1280]{3,2,1,0:T(2,128)S(1)}, f32[2,1,2,1280]{3,2,1,0:T(2,128)}, u32[]{:S(2)}) copy-start(f32[2,1,2,1280]{3,2,1,0:T(2,128)} %rate_ref.7) | copy-start | bytes 61444
  19.1 14.8 %copy-start.2 = (f32[1,3,256,16]{2,3,1,0:T(8,128)S(1)}, f32[1,3,256,16]{2,3,1,0:T(8,128)}, u32[]{:S(2)}) copy-start(f32[1,3,256,16]{2,3,1,0:T(8,128)} %param.14) | copy-start | bytes 147460
  19.1 14.8 %copy-start.3 = (f32[1,3,256,16]{2,3,1,0:T(8,128)S(1)}, f32[1,3,256,16]{2,3,1,0:T(8,128)}, u32[]{:S(2)}) copy-start(f32[1,3,256,16]{2,3,1,0:T(8,128)} %param.15) | copy-start | bytes 147460
  60.9 5.4 %collective-permute-start = (bf16[96,256]{1,0:T(8,128)(2,1)S(1)}, bf16[96,256]{1,0:T(8,128)(2,1)S(1)}, u32[]{:S(2)}, u32[]{:S(2)}) collective-permute-start(bf16[96,256]{1,0:T(8,128)(2,1)S(1)} %get-tuple-element.58.refs_0_.state_ref), channel_id=1, source_target_pairs={{0,16},{16,32},{32,48},{48,64},{64,80},{80,96},{96,112},{112,128},... | collective-permute-start | bytes 147464 | tf_op jit(solution)/shard_map/ppermute | solution.py:413
  62.9 3.4 %copy-start.4 = (f32[3,256,16]{1,2,0:T(8,128)S(1)}, f32[3,256,16]{1,2,0:T(8,128)}, u32[]{:S(2)}) copy-start(f32[3,256,16]{1,2,0:T(8,128)} %param.16) | copy-start | bytes 147460
  62.9 3.4 %copy-start.5 = (f32[3,256,16]{1,2,0:T(8,128)S(1)}, f32[3,256,16]{1,2,0:T(8,128)}, u32[]{:S(2)}) copy-start(f32[3,256,16]{1,2,0:T(8,128)} %param.17) | copy-start | bytes 147460
  110.4 12.9 %all-to-all-start.8 = ((bf16[16,48,256]{2,1,0:T(8,128)(2,1)}), bf16[16,48,256]{2,1,0:T(8,128)(2,1)S(1)}, u32[]{:S(2)}, u32[]{:S(2)}) async-start(bf16[16,48,256]{2,1,0:T(8,128)(2,1)} %get-tuple-element.70), calls=%async_computation.8 | async-start | bytes 786432 | tf_op jit(solution)/shard_map/all_to_all | solution.py:408
  114.2 15.0 %collective-permute-start.1 = (bf16[16,48,256]{2,1,0:T(8,128)(2,1)S(1)}, bf16[16,48,256]{2,1,0:T(8,128)(2,1)S(1)}, u32[]{:S(2)}, u32[]{:S(2)}) collective-permute-start(bf16[16,48,256]{2,1,0:T(8,128)(2,1)S(1)} %all_to_all.53.gathered_ref), channel_id=1, source_target_pairs={{16,0},{32,16},{48,32},{64,48},{80,64},{96,80},{112,96},{128,112},... | collective-permute-start | bytes 1179656 | tf_op jit(solution)/shard_map/ppermute | solution.py:418
  124.2 13.3 %all-to-all-start.9 = ((bf16[16,48,256]{2,1,0:T(8,128)(2,1)}), bf16[16,48,256]{2,1,0:T(8,128)(2,1)S(1)}, u32[]{:S(2)}, u32[]{:S(2)}) async-start(bf16[16,48,256]{2,1,0:T(8,128)(2,1)} %get-tuple-element.75), calls=%async_computation.9 | async-start | bytes 786432 | tf_op jit(solution)/shard_map/all_to_all | solution.py:408

commit v10 on v9

--- a/solution.py
+++ b/solution.py
@@ -486,7 +486,8 @@
         arrived = exchanged(message)
         token = None
         if pending and not leaving:
-            results, token = apply_fast(*pending.pop(), results, shape)
+            results, token = apply_fast(*pending.pop(), results, shape, owed[0])
+            owed = (handed_back(token), *owed[1:])
         message, *state = update(index, arrived, weights, moment, squares, token, leaving)
         if leaving:
             here = pending.pop()
@@ -498,7 +499,7 @@
                 who, passed, fresh_weights, fresh_moment, token, parties
             )
             gathered = exchanged(message)
-            owed = (handed_back(gathered), queries, place)
+            owed = (gathered, queries, place)
         else:
             weights, moment, squares = (*state, squares)[:3]
             gathered = exchanged(message)

time: 141 us -> 141 us (level)
  no operation moved by 1% of the time
where the time goes in v10:
time: 141 us; the launch traced here: 139 us
  blocking collectives  78.3 us (56%)
  Pallas kernels  21.3 us (15%)
  starting transfers between devices  18.3 us (13%)
  waiting for transfers between devices  18.3 us (13%)
  local copies, waits for them, and re-layouts  1.99 us (1%)
    all_to_all x6, blocking collectives, exchanged(): return lax.all_to_all(tiles, TOK, split_axis=0, concat_axis=0, tiled=True)  78.3 us
    all_to_all x3, waiting for transfers between devices, exchanged(): return lax.all_to_all(tiles, TOK, split_axis=0, concat_axis=0, tiled=True)  17.7 us
    all_to_all x3, starting transfers between devices, exchanged(): return lax.all_to_all(tiles, TOK, split_axis=0, concat_axis=0, tiled=True)  14.5 us
    pallas_call x5, Pallas kernels, apply_fast(): pl.pallas_call(functools.partial(apply_kernel, place, staged, waits, extr...  9.93 us
    pallas_call x4, Pallas kernels, grads(): pl.pallas_call(functools.partial(grads_kernel, place, 256, [where for _,...  6.92 us
  transfers between devices with their start and end apart: 5, of which 4 were waited for; matrix products, arithmetic and copies ran while one was open for 1% of the time, Pallas kernels for 8%

profile of v10, /device:TPU:96, one launch (start us, length us, event | category | flops | bytes accessed | tf_op | source)
XLA Modules:
  0.0 139.1 jit_solution(1558448092752196039)
XLA Ops:
  0.6 1.6 %spread.1 = (bf16[16,48,256]{2,1,0:T(8,128)(2,1)}, f32[8,128]{1,0:T(8,128)S(1)}) custom-call(f32[48,256]{1,0:T(8,128)} %bitcast.29), custom_call_target="tpu_custom_call" | custom-call | tf_op jit(solution)/shard_map/spread/pallas_call | solution.py:81
  2.2 7.0 %all-to-all-start.1 = ((bf16[16,48,256]{2,1,0:T(8,128)(2,1)}), bf16[16,48,256]{2,1,0:T(8,128)(2,1)S(1)}, u32[]{:S(2)}, u32[]{:S(2)}) async-start(bf16[16,48,256]{2,1,0:T(8,128)(2,1)} %get-tuple-element.45), calls=%async_computation.1 | async-start | bytes 786432 | tf_op jit(solution)/shard_map/all_to_all | solution.py:408
  10.0 1.3 stage.1
  11.3 7.8 %all-to-all-done.1.gathered_ref = bf16[16,48,256]{2,1,0:T(8,128)(2,1)S(1)} async-done(((bf16[16,48,256]{2,1,0:T(8,128)(2,1)}), bf16[16,48,256]{2,1,0:T(8,128)(2,1)S(1)}, u32[]{:S(2)}, u32[]{:S(2)}) %all-to-all-start.1) | async-done | bytes 393248 | tf_op jit(solution)/shard_map/all_to_all | solution.py:408
  19.1 1.5 %grads.4 = (bf16[16,112,128]{2,1,0:T(8,128)(2,1)S(1)}, bf16[1280,256]{1,0:T(8,128)(2,1)S(1)}, bf16[1280,256]{1,0:T(8,128)(2,1)S(1)}) custom-call(bf16[16,48,256]{2,1,0:T(8,128)(2,1)S(1)} %all-to-all-done.1.gathered_ref, f32[2,1,2,1280]{3,2,1,0:T(2,128)S(1)} %copy-done.1, bf16[1280,256]{1,0:T(8,128)(2,1)S(1)} %get-tuple-element.47.key_rows, ...), custom_call_target="tpu_custom_call" | custom-call | flops 1006632960 | bytes 1310720 | tf_op jit(solution)/shard_map/grads/pallas_call | solution.py:193
  20.6 13.3 %all_to_all.50.refs_0_ = bf16[16,112,128]{2,1,0:T(8,128)(2,1)S(1)} all-to-all(bf16[16,112,128]{2,1,0:T(8,128)(2,1)S(1)} %get-tuple-element.50), channel_id=1, replica_groups=mesh['seg'=16,'tok_0'=4,'tok_1'=4] {'tok_0','tok_1'}, dimensions={0} | all-to-all | bytes 917504 | tf_op jit(solution)/shard_map/all_to_all | solution.py:408
  34.1 12.4 %all_to_all.51.gathered_ref = bf16[16,48,256]{2,1,0:T(8,128)(2,1)S(1)} all-to-all(bf16[16,48,256]{2,1,0:T(8,128)(2,1)S(1)} %get-tuple-element.51), channel_id=1, replica_groups=mesh['seg'=16,'tok_0'=4,'tok_1'=4] {'tok_0','tok_1'}, dimensions={0} | all-to-all | bytes 786432 | tf_op jit(solution)/shard_map/all_to_all | solution.py:408
  46.4 1.6 %grads.5 = (bf16[16,48,256]{2,1,0:T(8,128)(2,1)S(1)}, bf16[1280,256]{1,0:T(8,128)(2,1)S(1)}, bf16[1280,256]{1,0:T(8,128)(2,1)S(1)}) custom-call(bf16[16,48,256]{2,1,0:T(8,128)(2,1)S(1)} %all_to_all.51.gathered_ref, f32[2,1,2,1280]{3,2,1,0:T(2,128)S(1)} %copy-done.1, bf16[1280,256]{1,0:T(8,128)(2,1)S(1)} %get-tuple-element.52.key_rows, ...), custom_call_target="tpu_custom_call" | custom-call | flops 1006632960 | bytes 1310720 | tf_op jit(solution)/shard_map/grads/pallas_call | solution.py:193
  48.1 12.6 %all_to_all.52.refs_0_ = bf16[16,48,256]{2,1,0:T(8,128)(2,1)S(1)} all-to-all(bf16[16,48,256]{2,1,0:T(8,128)(2,1)S(1)} %get-tuple-element.54), channel_id=1, replica_groups=mesh['seg'=16,'tok_0'=4,'tok_1'=4] {'tok_0','tok_1'}, dimensions={0} | all-to-all | bytes 786432 | tf_op jit(solution)/shard_map/all_to_all | solution.py:408
  60.9 1.9 %collective-permute-start = (bf16[96,256]{1,0:T(8,128)(2,1)S(1)}, bf16[96,256]{1,0:T(8,128)(2,1)S(1)}, u32[]{:S(2)}, u32[]{:S(2)}) collective-permute-start(bf16[96,256]{1,0:T(8,128)(2,1)S(1)} %get-tuple-element.58.refs_0_.state_ref), channel_id=1, source_target_pairs={{0,16},{16,32},{32,48},{48,64},{64,80},{80,96},{96,112},{112,128},... | collective-permute-start | bytes 147464 | tf_op jit(solution)/shard_map/ppermute | solution.py:413
  62.9 2.8 %apply.6 = (bf16[2,1,2,1280,256]{4,3,2,1,0:T(8,128)(2,1)}, bf16[96,256]{1,0:T(8,128)(2,1)S(1)}) custom-call(bf16[16,48,256]{2,1,0:T(8,128)(2,1)S(1)} %all_to_all.51.gathered_ref, bf16[2,1,2,1280,256]{4,3,2,1,0:T(8,128)(2,1)} %query_ref.7, bf16[96,256]{1,0:T(8,128)(2,1)S(1)} %get-tuple-element.58.refs_0_.state_ref, ...), custom_call_target="tpu_custom_call", output_to_operand_aliasing={{0}: (4, {})} | custom-call | flops 503316480 | bytes 1310720 | tf_op jit(solution)/shard_map/apply/pallas_call | solution.py:385
  66.4 14.6 %all_to_all.53.gathered_ref.refs_0_ = bf16[16,48,256]{2,1,0:T(8,128)(2,1)S(1)} all-to-all(bf16[16,48,256]{2,1,0:T(8,128)(2,1)S(1)} %get-tuple-element.61), channel_id=1, replica_groups=mesh['seg'=16,'tok_0'=4,'tok_1'=4] {'tok_0','tok_1'}, dimensions={0} | all-to-all | bytes 786432 | tf_op jit(solution)/shard_map/all_to_all | solution.py:408
  80.9 1.5 %grads.6 = (bf16[16,48,256]{2,1,0:T(8,128)(2,1)S(1)}, bf16[1280,256]{1,0:T(8,128)(2,1)S(1)}, bf16[1280,256]{1,0:T(8,128)(2,1)S(1)}) custom-call(bf16[16,48,256]{2,1,0:T(8,128)(2,1)S(1)} %all_to_all.53.gathered_ref.refs_0_, f32[2,1,2,1280]{3,2,1,0:T(2,128)S(1)} %copy-done.1, bf16[1280,256]{1,0:T(8,128)(2,1)S(1)} %get-tuple-element.62.key_rows, ...), custom_call_target="tpu_custom_call" | custom-call | flops 1006632960 | bytes 1310720 | tf_op jit(solution)/shard_map/grads/pallas_call | solution.py:193
  82.4 12.9 %all_to_all.54.refs_0_ = bf16[16,48,256]{2,1,0:T(8,128)(2,1)S(1)} all-to-all(bf16[16,48,256]{2,1,0:T(8,128)(2,1)S(1)} %get-tuple-element.64), channel_id=1, replica_groups=mesh['seg'=16,'tok_0'=4,'tok_1'=4] {'tok_0','tok_1'}, dimensions={0} | all-to-all | bytes 786432 | tf_op jit(solution)/shard_map/all_to_all | solution.py:408
  95.5 12.6 %all_to_all.55.gathered_ref = bf16[16,48,256]{2,1,0:T(8,128)(2,1)S(1)} all-to-all(bf16[16,48,256]{2,1,0:T(8,128)(2,1)S(1)} %get-tuple-element.67), channel_id=1, replica_groups=mesh['seg'=16,'tok_0'=4,'tok_1'=4] {'tok_0','tok_1'}, dimensions={0} | all-to-all | bytes 786432 | tf_op jit(solution)/shard_map/all_to_all | solution.py:408
  108.1 2.3 %grads.7 = (bf16[16,48,256]{2,1,0:T(8,128)(2,1)}, bf16[1280,256]{1,0:T(8,128)(2,1)S(1)}) custom-call(bf16[16,48,256]{2,1,0:T(8,128)(2,1)S(1)} %all_to_all.55.gathered_ref, f32[2,1,2,1280]{3,2,1,0:T(2,128)S(1)} %copy-done.1, bf16[1280,256]{1,0:T(8,128)(2,1)S(1)} %get-tuple-element.68.key_rows, bf16[1280,256]{1,0:T(8,128)(2,1)S(1)} %get-tuple-element.69.value_rows, ...), custom_call_target="tpu_custom_call" | custom-call | flops 1006632960 | bytes 1310720 | tf_op jit(solution)/shard_map/grads/pallas_call | solution.py:193
  110.4 3.7 %all-to-all-start.8 = ((bf16[16,48,256]{2,1,0:T(8,128)(2,1)}), bf16[16,48,256]{2,1,0:T(8,128)(2,1)S(1)}, u32[]{:S(2)}, u32[]{:S(2)}) async-start(bf16[16,48,256]{2,1,0:T(8,128)(2,1)} %get-tuple-element.70), calls=%async_computation.8 | async-start | bytes 786432 | tf_op jit(solution)/shard_map/all_to_all | solution.py:408
  114.2 2.8 %apply.7 = (bf16[2,1,2,1280,256]{4,3,2,1,0:T(8,128)(2,1)}, bf16[16,48,256]{2,1,0:T(8,128)(2,1)S(1)}) custom-call(bf16[16,48,256]{2,1,0:T(8,128)(2,1)S(1)} %all_to_all.55.gathered_ref, bf16[2,1,2,1280,256]{4,3,2,1,0:T(8,128)(2,1)} %query_ref.7, bf16[16,48,256]{2,1,0:T(8,128)(2,1)S(1)} %all_to_all.53.gathered_ref.refs_0_, ...), custom_call_target="tpu_custom_call", output_to_operand_aliasing={{0}: (3, {})} | custom-call | flops 503316480 | bytes 1310720 | tf_op jit(solution)/shard_map/apply/pallas_call | solution.py:385
  117.0 1.9 %collective-permute-start.1 = (bf16[16,48,256]{2,1,0:T(8,128)(2,1)S(1)}, bf16[16,48,256]{2,1,0:T(8,128)(2,1)S(1)}, u32[]{:S(2)}, u32[]{:S(2)}) collective-permute-start(bf16[16,48,256]{2,1,0:T(8,128)(2,1)S(1)} %get-tuple-element.74.refs_4_), channel_id=1, source_target_pairs={{16,0},{32,16},{48,32},{64,48},{80,64},{96,80},{112,96},{128,112},... | collective-permute-start | bytes 1179656 | tf_op jit(solution)/shard_map/ppermute | solution.py:418
  118.9 4.4 %all-to-all-done.8.refs_0_ = bf16[16,48,256]{2,1,0:T(8,128)(2,1)S(1)} async-done(((bf16[16,48,256]{2,1,0:T(8,128)(2,1)}), bf16[16,48,256]{2,1,0:T(8,128)(2,1)S(1)}, u32[]{:S(2)}, u32[]{:S(2)}) %all-to-all-start.8) | async-done | bytes 393248 | tf_op jit(solution)/shard_map/all_to_all | solution.py:408
  124.2 3.7 %all-to-all-start.9 = ((bf16[16,48,256]{2,1,0:T(8,128)(2,1)}), bf16[16,48,256]{2,1,0:T(8,128)(2,1)S(1)}, u32[]{:S(2)}, u32[]{:S(2)}) async-start(bf16[16,48,256]{2,1,0:T(8,128)(2,1)} %get-tuple-element.75), calls=%async_computation.9 | async-start | bytes 786432 | tf_op jit(solution)/shard_map/all_to_all | solution.py:408
  129.2 2.8 %apply.8 = (bf16[2,1,2,1280,256]{4,3,2,1,0:T(8,128)(2,1)}, f32[48,256]{1,0:T(8,128)S(1)}) custom-call(bf16[16,48,256]{2,1,0:T(8,128)(2,1)S(1)} %collective-permute-done.1.gathered_ref, bf16[2,1,2,1280,256]{4,3,2,1,0:T(8,128)(2,1)} %query_ref.7, f32[48,256]{1,0:T(8,128)S(1)} %get-tuple-element.77.refs_0_, ...), custom_call_target="tpu_custom_call", output_to_operand_aliasing={{0}: (5, {})} | custom-call | flops 503316480 | bytes 1310720 | tf_op jit(solution)/shard_map/apply/pallas_call | solution.py:385
  132.0 5.6 %all-to-all-done.9.gathered_ref = bf16[16,48,256]{2,1,0:T(8,128)(2,1)S(1)} async-done(((bf16[16,48,256]{2,1,0:T(8,128)(2,1)}), bf16[16,48,256]{2,1,0:T(8,128)(2,1)S(1)}, u32[]{:S(2)}, u32[]{:S(2)}) %all-to-all-start.9) | async-done | bytes 393248 | tf_op jit(solution)/shard_map/all_to_all | solution.py:408
  137.5 1.6 %apply.9 = bf16[2,1,2,1280,256]{4,3,2,1,0:T(8,128)(2,1)} custom-call(bf16[16,48,256]{2,1,0:T(8,128)(2,1)S(1)} %all-to-all-done.9.gathered_ref, bf16[1280,256]{1,0:T(8,128)(2,1)S(1)} %get-tuple-element.76.query_ref, f32[48,256]{1,0:T(8,128)S(1)} %get-tuple-element.79.refs_0_, ...), custom_call_target="tpu_custom_call", output_to_operand_aliasing={{}: (3, {})} | custom-call | flops 503316480 | bytes 1310720 | tf_op jit(solution)/shard_map/apply/pallas_call | solution.py:385
  (24 shorter events, 4.1 us)
Async XLA Ops:
  2.2 16.9 %all-to-all-start.1 = ((bf16[16,48,256]{2,1,0:T(8,128)(2,1)}), bf16[16,48,256]{2,1,0:T(8,128)(2,1)S(1)}, u32[]{:S(2)}, u32[]{:S(2)}) async-start(bf16[16,48,256]{2,1,0:T(8,128)(2,1)} %get-tuple-element.45), calls=%async_computation.1 | async-start | bytes 786432 | tf_op jit(solution)/shard_map/all_to_all | solution.py:408
  9.3 0.7 copy-start
  10.0 9.1 %copy-start.1 = (f32[2,1,2,1280]{3,2,1,0:T(2,128)S(1)}, f32[2,1,2,1280]{3,2,1,0:T(2,128)}, u32[]{:S(2)}) copy-start(f32[2,1,2,1280]{3,2,1,0:T(2,128)} %rate_ref.7) | copy-start | bytes 61444
  19.1 14.8 %copy-start.2 = (f32[1,3,256,16]{2,3,1,0:T(8,128)S(1)}, f32[1,3,256,16]{2,3,1,0:T(8,128)}, u32[]{:S(2)}) copy-start(f32[1,3,256,16]{2,3,1,0:T(8,128)} %param.14) | copy-start | bytes 147460
  19.1 14.8 %copy-start.3 = (f32[1,3,256,16]{2,3,1,0:T(8,128)S(1)}, f32[1,3,256,16]{2,3,1,0:T(8,128)}, u32[]{:S(2)}) copy-start(f32[1,3,256,16]{2,3,1,0:T(8,128)} %param.15) | copy-start | bytes 147460
  60.9 5.4 %collective-permute-start = (bf16[96,256]{1,0:T(8,128)(2,1)S(1)}, bf16[96,256]{1,0:T(8,128)(2,1)S(1)}, u32[]{:S(2)}, u32[]{:S(2)}) collective-permute-start(bf16[96,256]{1,0:T(8,128)(2,1)S(1)} %get-tuple-element.58.refs_0_.state_ref), channel_id=1, source_target_pairs={{0,16},{16,32},{32,48},{48,64},{64,80},{80,96},{96,112},{112,128},... | collective-permute-start | bytes 147464 | tf_op jit(solution)/shard_map/ppermute | solution.py:413
  62.9 3.4 %copy-start.4 = (f32[3,256,16]{1,2,0:T(8,128)S(1)}, f32[3,256,16]{1,2,0:T(8,128)}, u32[]{:S(2)}) copy-start(f32[3,256,16]{1,2,0:T(8,128)} %param.16) | copy-start | bytes 147460
  62.9 3.4 %copy-start.5 = (f32[3,256,16]{1,2,0:T(8,128)S(1)}, f32[3,256,16]{1,2,0:T(8,128)}, u32[]{:S(2)}) copy-start(f32[3,256,16]{1,2,0:T(8,128)} %param.17) | copy-start | bytes 147460
  110.4 12.9 %all-to-all-start.8 = ((bf16[16,48,256]{2,1,0:T(8,128)(2,1)}), bf16[16,48,256]{2,1,0:T(8,128)(2,1)S(1)}, u32[]{:S(2)}, u32[]{:S(2)}) async-start(bf16[16,48,256]{2,1,0:T(8,128)(2,1)} %get-tuple-element.70), calls=%async_computation.8 | async-start | bytes 786432 | tf_op jit(solution)/shard_map/all_to_all | solution.py:408
  117.0 12.2 %collective-permute-start.1 = (bf16[16,48,256]{2,1,0:T(8,128)(2,1)S(1)}, bf16[16,48,256]{2,1,0:T(8,128)(2,1)S(1)}, u32[]{:S(2)}, u32[]{:S(2)}) collective-permute-start(bf16[16,48,256]{2,1,0:T(8,128)(2,1)S(1)} %get-tuple-element.74.refs_4_), channel_id=1, source_target_pairs={{16,0},{32,16},{48,32},{64,48},{80,64},{96,80},{112,96},{128,112},... | collective-permute-start | bytes 1179656 | tf_op jit(solution)/shard_map/ppermute | solution.py:418
  124.2 13.3 %all-to-all-start.9 = ((bf16[16,48,256]{2,1,0:T(8,128)(2,1)}), bf16[16,48,256]{2,1,0:T(8,128)(2,1)S(1)}, u32[]{:S(2)}, u32[]{:S(2)}) async-start(bf16[16,48,256]{2,1,0:T(8,128)(2,1)} %get-tuple-element.75), calls=%async_computation.9 | async-start | bytes 786432 | tf_op jit(solution)/shard_map/all_to_all | solution.py:408

commit v11 on v10

--- a/solution.py
+++ b/solution.py
@@ -316,17 +316,19 @@
     if query_ref is not query_rows:
         (copy,) = started([query_ref], [query_rows], [place], sems)
         copy.wait()
-    size = length // parts
+    block = 256
+    first = length if parts == 1 else -(-length // (parts * block)) * block
     copies = []
-    for part in range(parts):
-        queries = query_rows[part * size : (part + 1) * size, :]
+    for part, start in enumerate(range(0, length, first)):
+        size = min(first, length - start)
+        queries = query_rows[start : start + size, :]
         pre_gate = dot(queries, matrix(gathered, 0, share), NT)
         pre_up = dot(queries, matrix(gathered, 2, share), NT)
         hidden = (pre_gate * sigmoid(pre_gate) * pre_up).astype(bf16)
-        held_ref[part * size : (part + 1) * size, :] = dot(
+        held_ref[start : start + size, :] = dot(
             hidden, matrix(gathered, 1, share), NT
         ).astype(bf16)
-        span = pl.ds(part * size, size)
+        span = pl.ds(start, size)
         copies.append(
             pltpu.make_async_copy(
                 held_ref.at[span, :], out_ref.at[*place].at[span, :], sems.at[1 + part]

time: 141 us -> 141 us (level)
  no operation moved by 1% of the time
where the time goes in v11:
time: 141 us; the launch traced here: 139 us
  blocking collectives  78.3 us (56%)
  Pallas kernels  21.2 us (15%)
  starting transfers between devices  18.3 us (13%)
  waiting for transfers between devices  18.3 us (13%)
  local copies, waits for them, and re-layouts  1.99 us (1%)
    all_to_all x6, blocking collectives, exchanged(): return lax.all_to_all(tiles, TOK, split_axis=0, concat_axis=0, tiled=True)  78.3 us
    all_to_all x3, waiting for transfers between devices, exchanged(): return lax.all_to_all(tiles, TOK, split_axis=0, concat_axis=0, tiled=True)  17.7 us
    all_to_all x3, starting transfers between devices, exchanged(): return lax.all_to_all(tiles, TOK, split_axis=0, concat_axis=0, tiled=True)  14.5 us
    pallas_call x5, Pallas kernels, apply_fast(): pl.pallas_call(functools.partial(apply_kernel, place, staged, waits, extr...  9.87 us
    pallas_call x4, Pallas kernels, grads(): pl.pallas_call(functools.partial(grads_kernel, place, 256, [where for _,...  6.92 us
  transfers between devices with their start and end apart: 5, of which 4 were waited for; matrix products, arithmetic and copies ran while one was open for 1% of the time, Pallas kernels for 8%

profile of v11, /device:TPU:96, one launch (start us, length us, event | category | flops | bytes accessed | tf_op | source)
XLA Modules:
  0.0 139.1 jit_solution(1743598034468132767)
XLA Ops:
  0.6 1.6 %spread.1 = (bf16[16,48,256]{2,1,0:T(8,128)(2,1)}, f32[8,128]{1,0:T(8,128)S(1)}) custom-call(f32[48,256]{1,0:T(8,128)} %bitcast.29), custom_call_target="tpu_custom_call" | custom-call | tf_op jit(solution)/shard_map/spread/pallas_call | solution.py:81
  2.2 7.0 %all-to-all-start.1 = ((bf16[16,48,256]{2,1,0:T(8,128)(2,1)}), bf16[16,48,256]{2,1,0:T(8,128)(2,1)S(1)}, u32[]{:S(2)}, u32[]{:S(2)}) async-start(bf16[16,48,256]{2,1,0:T(8,128)(2,1)} %get-tuple-element.45), calls=%async_computation.1 | async-start | bytes 786432 | tf_op jit(solution)/shard_map/all_to_all | solution.py:410
  10.0 1.3 stage.1
  11.3 7.8 %all-to-all-done.1.gathered_ref = bf16[16,48,256]{2,1,0:T(8,128)(2,1)S(1)} async-done(((bf16[16,48,256]{2,1,0:T(8,128)(2,1)}), bf16[16,48,256]{2,1,0:T(8,128)(2,1)S(1)}, u32[]{:S(2)}, u32[]{:S(2)}) %all-to-all-start.1) | async-done | bytes 393248 | tf_op jit(solution)/shard_map/all_to_all | solution.py:410
  19.1 1.5 %grads.4 = (bf16[16,112,128]{2,1,0:T(8,128)(2,1)S(1)}, bf16[1280,256]{1,0:T(8,128)(2,1)S(1)}, bf16[1280,256]{1,0:T(8,128)(2,1)S(1)}) custom-call(bf16[16,48,256]{2,1,0:T(8,128)(2,1)S(1)} %all-to-all-done.1.gathered_ref, f32[2,1,2,1280]{3,2,1,0:T(2,128)S(1)} %copy-done.1, bf16[1280,256]{1,0:T(8,128)(2,1)S(1)} %get-tuple-element.47.key_rows, ...), custom_call_target="tpu_custom_call" | custom-call | flops 1006632960 | bytes 1310720 | tf_op jit(solution)/shard_map/grads/pallas_call | solution.py:193
  20.6 13.3 %all_to_all.50.refs_0_ = bf16[16,112,128]{2,1,0:T(8,128)(2,1)S(1)} all-to-all(bf16[16,112,128]{2,1,0:T(8,128)(2,1)S(1)} %get-tuple-element.50), channel_id=1, replica_groups=mesh['seg'=16,'tok_0'=4,'tok_1'=4] {'tok_0','tok_1'}, dimensions={0} | all-to-all | bytes 917504 | tf_op jit(solution)/shard_map/all_to_all | solution.py:410
  34.1 12.4 %all_to_all.51.gathered_ref = bf16[16,48,256]{2,1,0:T(8,128)(2,1)S(1)} all-to-all(bf16[16,48,256]{2,1,0:T(8,128)(2,1)S(1)} %get-tuple-element.51), channel_id=1, replica_groups=mesh['seg'=16,'tok_0'=4,'tok_1'=4] {'tok_0','tok_1'}, dimensions={0} | all-to-all | bytes 786432 | tf_op jit(solution)/shard_map/all_to_all | solution.py:410
  46.4 1.6 %grads.5 = (bf16[16,48,256]{2,1,0:T(8,128)(2,1)S(1)}, bf16[1280,256]{1,0:T(8,128)(2,1)S(1)}, bf16[1280,256]{1,0:T(8,128)(2,1)S(1)}) custom-call(bf16[16,48,256]{2,1,0:T(8,128)(2,1)S(1)} %all_to_all.51.gathered_ref, f32[2,1,2,1280]{3,2,1,0:T(2,128)S(1)} %copy-done.1, bf16[1280,256]{1,0:T(8,128)(2,1)S(1)} %get-tuple-element.52.key_rows, ...), custom_call_target="tpu_custom_call" | custom-call | flops 1006632960 | bytes 1310720 | tf_op jit(solution)/shard_map/grads/pallas_call | solution.py:193
  48.1 12.6 %all_to_all.52.refs_0_ = bf16[16,48,256]{2,1,0:T(8,128)(2,1)S(1)} all-to-all(bf16[16,48,256]{2,1,0:T(8,128)(2,1)S(1)} %get-tuple-element.54), channel_id=1, replica_groups=mesh['seg'=16,'tok_0'=4,'tok_1'=4] {'tok_0','tok_1'}, dimensions={0} | all-to-all | bytes 786432 | tf_op jit(solution)/shard_map/all_to_all | solution.py:410
  60.9 1.9 %collective-permute-start = (bf16[96,256]{1,0:T(8,128)(2,1)S(1)}, bf16[96,256]{1,0:T(8,128)(2,1)S(1)}, u32[]{:S(2)}, u32[]{:S(2)}) collective-permute-start(bf16[96,256]{1,0:T(8,128)(2,1)S(1)} %get-tuple-element.58.refs_0_.state_ref), channel_id=1, source_target_pairs={{0,16},{16,32},{32,48},{48,64},{64,80},{80,96},{96,112},{112,128},... | collective-permute-start | bytes 147464 | tf_op jit(solution)/shard_map/ppermute | solution.py:415
  62.9 2.8 %apply.6 = (bf16[2,1,2,1280,256]{4,3,2,1,0:T(8,128)(2,1)}, bf16[96,256]{1,0:T(8,128)(2,1)S(1)}) custom-call(bf16[16,48,256]{2,1,0:T(8,128)(2,1)S(1)} %all_to_all.51.gathered_ref, bf16[2,1,2,1280,256]{4,3,2,1,0:T(8,128)(2,1)} %query_ref.7, bf16[96,256]{1,0:T(8,128)(2,1)S(1)} %get-tuple-element.58.refs_0_.state_ref, ...), custom_call_target="tpu_custom_call", output_to_operand_aliasing={{0}: (4, {})} | custom-call | flops 503316480 | bytes 1310720 | tf_op jit(solution)/shard_map/apply/pallas_call | solution.py:387
  66.4 14.6 %all_to_all.53.gathered_ref.refs_0_ = bf16[16,48,256]{2,1,0:T(8,128)(2,1)S(1)} all-to-all(bf16[16,48,256]{2,1,0:T(8,128)(2,1)S(1)} %get-tuple-element.61), channel_id=1, replica_groups=mesh['seg'=16,'tok_0'=4,'tok_1'=4] {'tok_0','tok_1'}, dimensions={0} | all-to-all | bytes 786432 | tf_op jit(solution)/shard_map/all_to_all | solution.py:410
  80.9 1.5 %grads.6 = (bf16[16,48,256]{2,1,0:T(8,128)(2,1)S(1)}, bf16[1280,256]{1,0:T(8,128)(2,1)S(1)}, bf16[1280,256]{1,0:T(8,128)(2,1)S(1)}) custom-call(bf16[16,48,256]{2,1,0:T(8,128)(2,1)S(1)} %all_to_all.53.gathered_ref.refs_0_, f32[2,1,2,1280]{3,2,1,0:T(2,128)S(1)} %copy-done.1, bf16[1280,256]{1,0:T(8,128)(2,1)S(1)} %get-tuple-element.62.key_rows, ...), custom_call_target="tpu_custom_call" | custom-call | flops 1006632960 | bytes 1310720 | tf_op jit(solution)/shard_map/grads/pallas_call | solution.py:193
  82.4 12.9 %all_to_all.54.refs_0_ = bf16[16,48,256]{2,1,0:T(8,128)(2,1)S(1)} all-to-all(bf16[16,48,256]{2,1,0:T(8,128)(2,1)S(1)} %get-tuple-element.64), channel_id=1, replica_groups=mesh['seg'=16,'tok_0'=4,'tok_1'=4] {'tok_0','tok_1'}, dimensions={0} | all-to-all | bytes 786432 | tf_op jit(solution)/shard_map/all_to_all | solution.py:410
  95.5 12.6 %all_to_all.55.gathered_ref = bf16[16,48,256]{2,1,0:T(8,128)(2,1)S(1)} all-to-all(bf16[16,48,256]{2,1,0:T(8,128)(2,1)S(1)} %get-tuple-element.67), channel_id=1, replica_groups=mesh['seg'=16,'tok_0'=4,'tok_1'=4] {'tok_0','tok_1'}, dimensions={0} | all-to-all | bytes 786432 | tf_op jit(solution)/shard_map/all_to_all | solution.py:410
  108.1 2.3 %grads.7 = (bf16[16,48,256]{2,1,0:T(8,128)(2,1)}, bf16[1280,256]{1,0:T(8,128)(2,1)S(1)}) custom-call(bf16[16,48,256]{2,1,0:T(8,128)(2,1)S(1)} %all_to_all.55.gathered_ref, f32[2,1,2,1280]{3,2,1,0:T(2,128)S(1)} %copy-done.1, bf16[1280,256]{1,0:T(8,128)(2,1)S(1)} %get-tuple-element.68.key_rows, bf16[1280,256]{1,0:T(8,128)(2,1)S(1)} %get-tuple-element.69.value_rows, ...), custom_call_target="tpu_custom_call" | custom-call | flops 1006632960 | bytes 1310720 | tf_op jit(solution)/shard_map/grads/pallas_call | solution.py:193
  110.4 3.7 %all-to-all-start.8 = ((bf16[16,48,256]{2,1,0:T(8,128)(2,1)}), bf16[16,48,256]{2,1,0:T(8,128)(2,1)S(1)}, u32[]{:S(2)}, u32[]{:S(2)}) async-start(bf16[16,48,256]{2,1,0:T(8,128)(2,1)} %get-tuple-element.70), calls=%async_computation.8 | async-start | bytes 786432 | tf_op jit(solution)/shard_map/all_to_all | solution.py:410
  114.2 2.8 %apply.7 = (bf16[2,1,2,1280,256]{4,3,2,1,0:T(8,128)(2,1)}, bf16[16,48,256]{2,1,0:T(8,128)(2,1)S(1)}) custom-call(bf16[16,48,256]{2,1,0:T(8,128)(2,1)S(1)} %all_to_all.55.gathered_ref, bf16[2,1,2,1280,256]{4,3,2,1,0:T(8,128)(2,1)} %query_ref.7, bf16[16,48,256]{2,1,0:T(8,128)(2,1)S(1)} %all_to_all.53.gathered_ref.refs_0_, ...), custom_call_target="tpu_custom_call", output_to_operand_aliasing={{0}: (3, {})} | custom-call | flops 503316480 | bytes 1310720 | tf_op jit(solution)/shard_map/apply/pallas_call | solution.py:387
  117.0 1.9 %collective-permute-start.1 = (bf16[16,48,256]{2,1,0:T(8,128)(2,1)S(1)}, bf16[16,48,256]{2,1,0:T(8,128)(2,1)S(1)}, u32[]{:S(2)}, u32[]{:S(2)}) collective-permute-start(bf16[16,48,256]{2,1,0:T(8,128)(2,1)S(1)} %get-tuple-element.74.refs_4_), channel_id=1, source_target_pairs={{16,0},{32,16},{48,32},{64,48},{80,64},{96,80},{112,96},{128,112},... | collective-permute-start | bytes 1179656 | tf_op jit(solution)/shard_map/ppermute | solution.py:420
  118.9 4.4 %all-to-all-done.8.refs_0_ = bf16[16,48,256]{2,1,0:T(8,128)(2,1)S(1)} async-done(((bf16[16,48,256]{2,1,0:T(8,128)(2,1)}), bf16[16,48,256]{2,1,0:T(8,128)(2,1)S(1)}, u32[]{:S(2)}, u32[]{:S(2)}) %all-to-all-start.8) | async-done | bytes 393248 | tf_op jit(solution)/shard_map/all_to_all | solution.py:410
  124.2 3.7 %all-to-all-start.9 = ((bf16[16,48,256]{2,1,0:T(8,128)(2,1)}), bf16[16,48,256]{2,1,0:T(8,128)(2,1)S(1)}, u32[]{:S(2)}, u32[]{:S(2)}) async-start(bf16[16,48,256]{2,1,0:T(8,128)(2,1)} %get-tuple-element.75), calls=%async_computation.9 | async-start | bytes 786432 | tf_op jit(solution)/shard_map/all_to_all | solution.py:410
  129.2 2.8 %apply.8 = (bf16[2,1,2,1280,256]{4,3,2,1,0:T(8,128)(2,1)}, f32[48,256]{1,0:T(8,128)S(1)}) custom-call(bf16[16,48,256]{2,1,0:T(8,128)(2,1)S(1)} %collective-permute-done.1.gathered_ref, bf16[2,1,2,1280,256]{4,3,2,1,0:T(8,128)(2,1)} %query_ref.7, f32[48,256]{1,0:T(8,128)S(1)} %get-tuple-element.77.refs_0_, ...), custom_call_target="tpu_custom_call", output_to_operand_aliasing={{0}: (5, {})} | custom-call | flops 503316480 | bytes 1310720 | tf_op jit(solution)/shard_map/apply/pallas_call | solution.py:387
  132.0 5.6 %all-to-all-done.9.gathered_ref = bf16[16,48,256]{2,1,0:T(8,128)(2,1)S(1)} async-done(((bf16[16,48,256]{2,1,0:T(8,128)(2,1)}), bf16[16,48,256]{2,1,0:T(8,128)(2,1)S(1)}, u32[]{:S(2)}, u32[]{:S(2)}) %all-to-all-start.9) | async-done | bytes 393248 | tf_op jit(solution)/shard_map/all_to_all | solution.py:410
  137.5 1.5 %apply.9 = bf16[2,1,2,1280,256]{4,3,2,1,0:T(8,128)(2,1)} custom-call(bf16[16,48,256]{2,1,0:T(8,128)(2,1)S(1)} %all-to-all-done.9.gathered_ref, bf16[1280,256]{1,0:T(8,128)(2,1)S(1)} %get-tuple-element.76.query_ref, f32[48,256]{1,0:T(8,128)S(1)} %get-tuple-element.79.refs_0_, ...), custom_call_target="tpu_custom_call", output_to_operand_aliasing={{}: (3, {})} | custom-call | flops 503316480 | bytes 1310720 | tf_op jit(solution)/shard_map/apply/pallas_call | solution.py:387
  (24 shorter events, 4.1 us)
Async XLA Ops:
  2.2 16.9 %all-to-all-start.1 = ((bf16[16,48,256]{2,1,0:T(8,128)(2,1)}), bf16[16,48,256]{2,1,0:T(8,128)(2,1)S(1)}, u32[]{:S(2)}, u32[]{:S(2)}) async-start(bf16[16,48,256]{2,1,0:T(8,128)(2,1)} %get-tuple-element.45), calls=%async_computation.1 | async-start | bytes 786432 | tf_op jit(solution)/shard_map/all_to_all | solution.py:410
  9.3 0.7 copy-start
  10.0 9.1 %copy-start.1 = (f32[2,1,2,1280]{3,2,1,0:T(2,128)S(1)}, f32[2,1,2,1280]{3,2,1,0:T(2,128)}, u32[]{:S(2)}) copy-start(f32[2,1,2,1280]{3,2,1,0:T(2,128)} %rate_ref.7) | copy-start | bytes 61444
  19.1 14.8 %copy-start.2 = (f32[1,3,256,16]{2,3,1,0:T(8,128)S(1)}, f32[1,3,256,16]{2,3,1,0:T(8,128)}, u32[]{:S(2)}) copy-start(f32[1,3,256,16]{2,3,1,0:T(8,128)} %param.14) | copy-start | bytes 147460
  19.1 14.8 %copy-start.3 = (f32[1,3,256,16]{2,3,1,0:T(8,128)S(1)}, f32[1,3,256,16]{2,3,1,0:T(8,128)}, u32[]{:S(2)}) copy-start(f32[1,3,256,16]{2,3,1,0:T(8,128)} %param.15) | copy-start | bytes 147460
  60.9 5.4 %collective-permute-start = (bf16[96,256]{1,0:T(8,128)(2,1)S(1)}, bf16[96,256]{1,0:T(8,128)(2,1)S(1)}, u32[]{:S(2)}, u32[]{:S(2)}) collective-permute-start(bf16[96,256]{1,0:T(8,128)(2,1)S(1)} %get-tuple-element.58.refs_0_.state_ref), channel_id=1, source_target_pairs={{0,16},{16,32},{32,48},{48,64},{64,80},{80,96},{96,112},{112,128},... | collective-permute-start | bytes 147464 | tf_op jit(solution)/shard_map/ppermute | solution.py:415
  62.9 3.4 %copy-start.4 = (f32[3,256,16]{1,2,0:T(8,128)S(1)}, f32[3,256,16]{1,2,0:T(8,128)}, u32[]{:S(2)}) copy-start(f32[3,256,16]{1,2,0:T(8,128)} %param.16) | copy-start | bytes 147460
  62.9 3.4 %copy-start.5 = (f32[3,256,16]{1,2,0:T(8,128)S(1)}, f32[3,256,16]{1,2,0:T(8,128)}, u32[]{:S(2)}) copy-start(f32[3,256,16]{1,2,0:T(8,128)} %param.17) | copy-start | bytes 147460
  110.4 12.9 %all-to-all-start.8 = ((bf16[16,48,256]{2,1,0:T(8,128)(2,1)}), bf16[16,48,256]{2,1,0:T(8,128)(2,1)S(1)}, u32[]{:S(2)}, u32[]{:S(2)}) async-start(bf16[16,48,256]{2,1,0:T(8,128)(2,1)} %get-tuple-element.70), calls=%async_computation.8 | async-start | bytes 786432 | tf_op jit(solution)/shard_map/all_to_all | solution.py:410
  117.0 12.2 %collective-permute-start.1 = (bf16[16,48,256]{2,1,0:T(8,128)(2,1)S(1)}, bf16[16,48,256]{2,1,0:T(8,128)(2,1)S(1)}, u32[]{:S(2)}, u32[]{:S(2)}) collective-permute-start(bf16[16,48,256]{2,1,0:T(8,128)(2,1)S(1)} %get-tuple-element.74.refs_4_), channel_id=1, source_target_pairs={{16,0},{32,16},{48,32},{64,48},{80,64},{96,80},{112,96},{128,112},... | collective-permute-start | bytes 1179656 | tf_op jit(solution)/shard_map/ppermute | solution.py:420
  124.2 13.3 %all-to-all-start.9 = ((bf16[16,48,256]{2,1,0:T(8,128)(2,1)}), bf16[16,48,256]{2,1,0:T(8,128)(2,1)S(1)}, u32[]{:S(2)}, u32[]{:S(2)}) async-start(bf16[16,48,256]{2,1,0:T(8,128)(2,1)} %get-tuple-element.75), calls=%async_computation.9 | async-start | bytes 786432 | tf_op jit(solution)/shard_map/all_to_all | solution.py:410
